TPU v7x, 512 devices: a whole 4x4x16 slice. The times are simulated.
512 devices in a mesh: slab: 32 (over y, z_lo), tile: 8 (over x, core), tilt: 2 (over z_hi).
Axes of the slice: x: 4, y: 4, z: 16 (z_hi: 2, z_lo: 8; z = z_hi * 8 + z_lo), core: 2. Of those that a mesh axis runs over, the one named last changes fastest.
Arguments:
- source: float32 [4, 512, 64, 256], P('tilt', 'slab', 'tile'), parts along dimension 0, may hold values from -1.2 to 1.2
- labels: int32 [512, 64, 512], P('slab', 'tile', 'tilt'), parts along dimension 2, may hold values from 0 to 7
- permittivity: float32 [16], P('tilt'), parts along dimension 0, may hold values from 1 to 2
Outputs:
- sweep_field: float32 [4, 512, 64, 256], P('tilt', 'slab', 'tile'), parts along dimension 0
There are 2 independent parts, one for each index of `tilt`. A program takes and returns all parts, laid end to end along the dimension named above; each array names one. Nothing has to cross between parts.
All inputs are finite; a program needn't handle non-finite values.
Results may differ from a plain program's by a relative error of at most 0.0003.
Values sent between devices are 32-bit elements; how exact they have to be, the bound alone decides.
No kernel may reach another device: no remote copies, remote signals or barrier semaphores. Data moves between devices by JAX's collectives and lax.ppermute only.
A program may use at most 64 MiB of HBM per device.

v0:
```python
from functools import reduce

import jax
import jax.numpy as jnp
from jax import lax
from jax.sharding import PartitionSpec as P

ITERS = 3
PML = 8


COUPLE = 0.02
WAVE_SHIFT = 0.15
DAMPING = 0.15
ABSORB = 0.5


def prefix(value, axis, combine, identity, reverse):
    peers, mine = (lax.axis_size(axis), lax.axis_index(axis))
    everything = jax.tree.map(lambda part: lax.all_gather(part, axis), value)
    start = jax.tree.map(
        lambda part, zero: jnp.broadcast_to(jnp.asarray(zero, part.dtype), part.shape),
        value,
        identity,
    )

    def step(k, before):
        at = peers - 1 - k if reverse else k
        reached = at > mine if reverse else at < mine
        new = combine(before, jax.tree.map(lambda part: part[at], everything))
        return jax.tree.map(lambda a, b: jnp.where(reached, a, b), new, before)

    return lax.fori_loop(0, peers, step, start)


def padded_2(block, sides, width):
    for axis, dim in sides:
        count = lax.axis_size(axis)
        forward = [(i, i + 1) for i in range(count - 1)]
        backward = [(target, source) for source, target in forward]
        low = lax.ppermute(
            lax.slice_in_dim(block, block.shape[dim] - width, None, axis=dim), axis, forward
        )
        high = lax.ppermute(lax.slice_in_dim(block, 0, width, axis=dim), axis, backward)
        block = jnp.concatenate([low, block, high], axis=dim)
    return block


def complex_multiply(former, latter):
    former_re = former[..., 0, :, :]
    former_im = former[..., 1, :, :]
    latter_re = latter[..., 0, :, :]
    latter_im = latter[..., 1, :, :]
    return jnp.stack(
        [
            former_re * latter_re - former_im * latter_im,
            former_re * latter_im + former_im * latter_re,
        ],
        axis=-3,
    )


def complex_recip(number):
    number_re = number[..., 0, :, :]
    number_im = number[..., 1, :, :]
    modulus = number_re * number_re + number_im * number_im
    return jnp.stack([number_re / modulus, -number_im / modulus], axis=-3)


def cell_offset_ratio(labels, permittivity):
    materials = jnp.arange(permittivity.shape[0], dtype=jnp.int32)
    chosen = labels[None, :, :, :] == materials[:, None, None, None]
    return jnp.sum(jnp.where(chosen, permittivity[:, None, None, None], jnp.float32(0.0)), axis=0)


def diagonal_from(relative, layer_ids, layer_count):
    inward = jnp.maximum(jnp.maximum(PML - layer_ids, layer_ids - (layer_count - 1 - PML)), 0)
    fraction = inward.astype(jnp.float32) / PML
    absorption_profile = ABSORB * fraction * fraction
    diag_re = 2.0 + 4.0 * COUPLE - WAVE_SHIFT * relative
    diag_im = DAMPING * WAVE_SHIFT * relative + absorption_profile[:, None, None]
    return jnp.stack([diag_re, diag_im], axis=1)


def mobius_grow(matrix, diag_layer):
    upper_left, upper_right, lower_left, lower_right = matrix
    grown_matrix = (
        lower_left,
        lower_right,
        complex_multiply(diag_layer, lower_left) - upper_left,
        complex_multiply(diag_layer, lower_right) - upper_right,
    )
    return (grown_matrix, None)


def normalized(matrix):
    largest = reduce(jnp.maximum, [jnp.max(jnp.abs(element), axis=0) for element in matrix])
    return tuple((element / largest for element in matrix))


def chain_mobius(earlier, latter):
    product = (
        complex_multiply(latter[0], earlier[0]) + complex_multiply(latter[1], earlier[2]),
        complex_multiply(latter[0], earlier[1]) + complex_multiply(latter[1], earlier[3]),
        complex_multiply(latter[2], earlier[0]) + complex_multiply(latter[3], earlier[2]),
        complex_multiply(latter[2], earlier[1]) + complex_multiply(latter[3], earlier[3]),
    )
    return normalized(product)


def chain_affine(earlier, latter):
    return (
        latter[0] + complex_multiply(latter[1], earlier[0]),
        complex_multiply(latter[1], earlier[1]),
    )


def pivot_pass(diagonal, initial):

    def pivot_advance(previous, diag_layer):
        current_layer_value = complex_recip(diag_layer - previous)
        return (current_layer_value, (current_layer_value, previous))

    _, (pivots, neighbours) = lax.scan(pivot_advance, initial, diagonal, reverse=False)
    return (pivots, neighbours)


def running_product(factors, complex_unit, reverse):

    def running_advance(carried_through, factor):
        current_layer_value = complex_multiply(carried_through, factor)
        return (current_layer_value, current_layer_value)

    _, products = lax.scan(running_advance, complex_unit, factors, reverse=reverse)
    return products


def affine_pass(rhs_now, factors, complex_zero, reverse):

    def affine_advance(carried_through, input_arrays):
        rhs_layer, factor = input_arrays
        current_layer_value = rhs_layer + complex_multiply(factor, carried_through)
        return (current_layer_value, current_layer_value)

    _, results = lax.scan(affine_advance, complex_zero, (rhs_now, factors), reverse=reverse)
    return results


def forward_inflow(upward, coef_up, complex_zero, complex_unit):
    inflow, _ = prefix(
        (upward[-1], coef_up[-1]), "slab", chain_affine, (complex_zero, complex_unit), False
    )
    return inflow


def transverse_sum(estimate):
    padded = padded_2(estimate, (("tile", 2),), 1)
    along_x = padded[:, :, 2:, :] + padded[:, :, :-2, :]
    edge_zeros = jnp.zeros(estimate.shape[:-1] + (1,), jnp.float32)
    along_y = jnp.concatenate([estimate[..., 1:], edge_zeros], axis=-1) + jnp.concatenate(
        [edge_zeros, estimate[..., :-1]], axis=-1
    )
    return along_x + along_y


def local(source, labels, permittivity):
    depth_local = labels.shape[0]
    plane_shape = labels.shape[1:]
    slab_count = lax.axis_size("slab")
    relative = cell_offset_ratio(labels, permittivity)
    layer_ids = lax.axis_index("slab") * depth_local + jnp.arange(depth_local, dtype=jnp.int32)
    diagonal = diagonal_from(relative, layer_ids, depth_local * slab_count)
    complex_zero = jnp.zeros((2,) + plane_shape, jnp.float32)
    complex_unit = jnp.stack(
        [jnp.ones(plane_shape, jnp.float32), jnp.zeros(plane_shape, jnp.float32)], axis=0
    )
    identity = (complex_unit, complex_zero, complex_zero, complex_unit)
    rhs_field = jnp.swapaxes(source, 0, 1)
    local_up = normalized(lax.scan(mobius_grow, identity, diagonal)[0])
    prefix_up = prefix(local_up, "slab", chain_mobius, identity, False)
    inflow_pivot = complex_multiply(prefix_up[1], complex_recip(prefix_up[3]))
    pivots, below_pivots = pivot_pass(diagonal, inflow_pivot)
    coef_up = running_product(below_pivots, complex_unit, False)
    coef_back = running_product(pivots, complex_unit, True)

    def solve_line(rhs_now):
        upward = affine_pass(rhs_now, below_pivots, complex_zero, False)
        inflow = forward_inflow(upward, coef_up, complex_zero, complex_unit)
        eliminated = upward + complex_multiply(coef_up, inflow)
        backward = affine_pass(complex_multiply(pivots, eliminated), pivots, complex_zero, True)
        above_value, _ = prefix(
            (backward[0], coef_back[0]), "slab", chain_affine, (complex_zero, complex_unit), True
        )
        return backward + complex_multiply(coef_back, above_value)

    estimate = solve_line(rhs_field)
    for sweep_index in range(ITERS - 1):
        estimate = solve_line(rhs_field + COUPLE * transverse_sum(estimate))
    return jnp.swapaxes(estimate, 0, 1)


def solution(mesh):
    placed = (P("tilt", "slab", "tile", None), P("slab", "tile", "tilt"), P("tilt"))
    return jax.shard_map(
        local,
        mesh=mesh,
        in_specs=placed,
        out_specs=P("tilt", "slab", "tile", None),
        check_vma=False,
    )
```

profile of v0, /device:TPU:1, one launch (start us, length us, event | category | flops | bytes accessed | tf_op | source)
XLA Modules:
  0.0 1443.9 jit_solution(15619790179171903037)
XLA Ops:
  1.8 1.6 while.262
  3.6 116.1 %all-gather = f32[64,8,256]{2,1,0:T(8,128)S(1)} all-gather(f32[2,8,256]{2,1,0:T(8,128)S(1)} %get-tuple-element.2055), channel_id=2, replica_groups=mesh['slab'=32,'tile'=8,'tilt'=2] {'slab'}, dimensions={0}, use_global_device_ids=true | all-gather | bytes 540672 | tf_op jit(solution)/shard_map/all_gather | solution.py:20
  119.7 102.2 %all-gather.1 = f32[64,8,256]{2,1,0:T(8,128)S(1)} all-gather(f32[2,8,256]{2,1,0:T(8,128)S(1)} %get-tuple-element.2053), channel_id=3, replica_groups=mesh['slab'=32,'tile'=8,'tilt'=2] {'slab'}, dimensions={0}, use_global_device_ids=true | all-gather | bytes 540672 | tf_op jit(solution)/shard_map/all_gather | solution.py:20
  221.9 103.5 %all-gather.2 = f32[64,8,256]{2,1,0:T(8,128)S(1)} all-gather(f32[2,8,256]{2,1,0:T(8,128)S(1)} %get-tuple-element.2054), channel_id=4, replica_groups=mesh['slab'=32,'tile'=8,'tilt'=2] {'slab'}, dimensions={0}, use_global_device_ids=true | all-gather | bytes 540672 | tf_op jit(solution)/shard_map/all_gather | solution.py:20
  325.4 102.1 %all-gather.3 = f32[64,8,256]{2,1,0:T(8,128)S(1)} all-gather(f32[2,8,256]{2,1,0:T(8,128)S(1)} %get-tuple-element.2052), channel_id=5, replica_groups=mesh['slab'=32,'tile'=8,'tilt'=2] {'slab'}, dimensions={0}, use_global_device_ids=true | all-gather | bytes 540672 | tf_op jit(solution)/shard_map/all_gather | solution.py:20
  427.5 8.1 while.263
  437.7 103.3 %all_gather.61 = f32[32,2,8,256]{3,2,1,0:T(8,128)S(1)} all-gather(f32[1,2,8,256]{3,2,1,0:T(8,128)S(1)} %slice.759), channel_id=1, replica_groups=mesh['slab'=32,'tile'=8,'tilt'=2] {'slab'}, dimensions={0}, use_global_device_ids=true | all-gather | bytes 540672 | tf_op jit(solution)/shard_map/all_gather | solution.py:20
  543.4 102.3 %all_gather.60 = f32[32,2,8,256]{3,2,1,0:T(8,128)S(1)} all-gather(f32[1,2,8,256]{3,2,1,0:T(8,128)S(1)} %slice.758), channel_id=1, replica_groups=mesh['slab'=32,'tile'=8,'tilt'=2] {'slab'}, dimensions={0}, use_global_device_ids=true | all-gather | bytes 540672 | tf_op jit(solution)/shard_map/all_gather | solution.py:20
  645.7 2.4 while.265
  649.8 103.8 %all_gather.62 = f32[32,2,8,256]{3,2,1,0:T(8,128)S(1)} all-gather(f32[1,2,8,256]{3,2,1,0:T(8,128)S(1)} %slice.767), channel_id=1, replica_groups=mesh['slab'=32,'tile'=8,'tilt'=2] {'slab'}, dimensions={0}, use_global_device_ids=true | all-gather | bytes 540672 | tf_op jit(solution)/shard_map/all_gather | solution.py:20
  754.5 102.7 %all_gather.63 = f32[32,2,8,256]{3,2,1,0:T(8,128)S(1)} all-gather(f32[1,2,8,256]{3,2,1,0:T(8,128)S(1)} %slice.768), channel_id=1, replica_groups=mesh['slab'=32,'tile'=8,'tilt'=2] {'slab'}, dimensions={0}, use_global_device_ids=true | all-gather | bytes 540672 | tf_op jit(solution)/shard_map/all_gather | solution.py:20
  857.2 2.7 while.267
  860.0 115.1 %collective-permute-start = (f32[16,2,1,256]{3,2,0,1:T(1,128)S(1)}, f32[16,2,1,256]{3,2,0,1:T(1,128)S(1)}, u32[]{:S(2)}, u32[]{:S(2)}) collective-permute-start(f32[16,2,1,256]{3,2,0,1:T(1,128)S(1)} %get-tuple-element.2036), channel_id=1, source_target_pairs={{2,0},{4,2},{6,4},{8,6},{10,8},{12,10},{14,12},{3,1},{5,3},{7,5},{... | collective-permute-start | bytes 98312 | tf_op jit(solution)/shard_map/ppermute | solution.py:44
  975.1 2.7 collective-permute-start.1
  981.2 104.3 %all_gather.64 = f32[32,2,8,256]{3,2,1,0:T(8,128)S(1)} all-gather(f32[1,2,8,256]{3,2,1,0:T(8,128)S(1)} %slice.778), channel_id=1, replica_groups=mesh['slab'=32,'tile'=8,'tilt'=2] {'slab'}, dimensions={0}, use_global_device_ids=true | all-gather | bytes 540672 | tf_op jit(solution)/shard_map/all_gather | solution.py:20
  1085.5 2.4 while.269
  1089.6 102.0 %all_gather.65 = f32[32,2,8,256]{3,2,1,0:T(8,128)S(1)} all-gather(f32[1,2,8,256]{3,2,1,0:T(8,128)S(1)} %slice.783), channel_id=1, replica_groups=mesh['slab'=32,'tile'=8,'tilt'=2] {'slab'}, dimensions={0}, use_global_device_ids=true | all-gather | bytes 540672 | tf_op jit(solution)/shard_map/all_gather | solution.py:20
  1191.6 2.7 while.271
  1194.4 29.1 %collective-permute-start.2 = (f32[16,2,1,256]{3,2,0,1:T(1,128)S(1)}, f32[16,2,1,256]{3,2,0,1:T(1,128)S(1)}, u32[]{:S(2)}, u32[]{:S(2)}) collective-permute-start(f32[16,2,1,256]{3,2,0,1:T(1,128)S(1)} %get-tuple-element.2032), channel_id=1, source_target_pairs={{2,0},{4,2},{6,4},{8,6},{10,8},{12,10},{14,12},{3,1},{5,3},{7,5},{... | collective-permute-start | bytes 98312 | tf_op jit(solution)/shard_map/ppermute | solution.py:44
  1223.6 4.4 collective-permute-start.3
  1230.6 103.8 %all_gather.66 = f32[32,2,8,256]{3,2,1,0:T(8,128)S(1)} all-gather(f32[1,2,8,256]{3,2,1,0:T(8,128)S(1)} %slice.792), channel_id=1, replica_groups=mesh['slab'=32,'tile'=8,'tilt'=2] {'slab'}, dimensions={0}, use_global_device_ids=true | all-gather | bytes 540672 | tf_op jit(solution)/shard_map/all_gather | solution.py:20
  1334.4 2.4 while.273
  1338.5 101.9 %all_gather.67 = f32[32,2,8,256]{3,2,1,0:T(8,128)S(1)} all-gather(f32[1,2,8,256]{3,2,1,0:T(8,128)S(1)} %slice.797), channel_id=1, replica_groups=mesh['slab'=32,'tile'=8,'tilt'=2] {'slab'}, dimensions={0}, use_global_device_ids=true | all-gather | bytes 540672 | tf_op jit(solution)/shard_map/all_gather | solution.py:20
  1440.4 2.7 while.275
  (1657 shorter events, 35.9 us)
Async XLA Ops:
  0.0 0.7 copy-start.3
  0.0 0.9 copy-start.1
  0.8 0.7 copy-start.4
  541.0 1.0 copy-start
  860.0 118.0 %collective-permute-start = (f32[16,2,1,256]{3,2,0,1:T(1,128)S(1)}, f32[16,2,1,256]{3,2,0,1:T(1,128)S(1)}, u32[]{:S(2)}, u32[]{:S(2)}) collective-permute-start(f32[16,2,1,256]{3,2,0,1:T(1,128)S(1)} %get-tuple-element.2036), channel_id=1, source_target_pairs={{2,0},{4,2},{6,4},{8,6},{10,8},{12,10},{14,12},{3,1},{5,3},{7,5},{... | collective-permute-start | bytes 98312 | tf_op jit(solution)/shard_map/ppermute | solution.py:44
  975.1 3.7 collective-permute-start.1
  978.0 0.8 copy-start.2
  1194.4 33.7 %collective-permute-start.2 = (f32[16,2,1,256]{3,2,0,1:T(1,128)S(1)}, f32[16,2,1,256]{3,2,0,1:T(1,128)S(1)}, u32[]{:S(2)}, u32[]{:S(2)}) collective-permute-start(f32[16,2,1,256]{3,2,0,1:T(1,128)S(1)} %get-tuple-element.2032), channel_id=1, source_target_pairs={{2,0},{4,2},{6,4},{8,6},{10,8},{12,10},{14,12},{3,1},{5,3},{7,5},{... | collective-permute-start | bytes 98312 | tf_op jit(solution)/shard_map/ppermute | solution.py:44
  1223.6 5.4 collective-permute-start.3
where the time goes:
time: 1470 us; the launch traced here: 1440 us
  blocking collectives  1250 us (85%)
  starting transfers between devices  151 us (10%)
  other arithmetic  19.6 us (1%)
  loops' own time  19.5 us (1%)
    all_gather x12, blocking collectives, prefix(): everything = jax.tree.map(lambda part: lax.all_gather(part, axis), value)  1250 us
    ppermute x2, starting transfers between devices, padded_2(): lax.ppermute(lax.slice_in_dim(block, 0, width, axis=dim), axis, backward)  144 us
  transfers between devices with their start and end apart: 4, of which 2 were waited for; matrix products, arithmetic and copies ran while one was open for 0% of the time, Pallas kernels for 0%

commit v1 on v0

v1 whole, which is shorter than its diff:
```python
import jax
import jax.numpy as jnp
from jax import lax
from jax.experimental import pallas as pl
from jax.experimental.pallas import tpu as pltpu
from jax.sharding import PartitionSpec as P

PML = 8
COUPLE = 0.02
WAVE_SHIFT = 0.15
DAMPING = 0.15
ABSORB = 0.5
NZ = 512
SLABS = 32
TILES = 8
LANES = 128
DEPTH = 8
STEPS = 6
F32 = jnp.float32
VMEM = pl.BlockSpec(memory_space=pltpu.VMEM)
SMEM = pl.BlockSpec(memory_space=pltpu.SMEM)


def chunk_of(device):
    y, z = divmod(device, 8)
    return 8 * y + (z if y % 2 == 0 else 7 - z)


CHUNK = [chunk_of(d) for d in range(SLABS)]
OWNER = [CHUNK.index(c) for c in range(SLABS)]


def roll(x, shift, axis):
    shift %= x.shape[axis]
    return x if shift == 0 else pltpu.roll(x, shift, axis)


def cmul(a, b):
    return a[0] * b[0] - a[1] * b[1], a[0] * b[1] + a[1] * b[0]


def cadd(a, b):
    return a[0] + b[0], a[1] + b[1]


def csub(a, b):
    return a[0] - b[0], a[1] - b[1]


def crecip(a):
    scale = 1.0 / (a[0] * a[0] + a[1] * a[1])
    return a[0] * scale, -a[1] * scale


def block_transpose(parts):
    lane = lax.broadcasted_iota(jnp.int32, (8, LANES), 1)
    parts = list(parts)
    for bit in (1, 2, 4, 8):
        low = (lane & (8 * bit)) == 0
        for i in range(16):
            if i & bit == 0:
                a, b = parts[i], parts[i | bit]
                parts[i] = jnp.where(low, a, roll(b, 8 * bit, 1))
                parts[i | bit] = jnp.where(low, roll(a, -8 * bit, 1), b)
    return parts


def pack_kernel(table, source, labels, out, sides):
    for side in range(2):
        lanes = pl.ds(side * LANES, LANES)
        sides[side, pl.ds(0, 2 * LANES), :] = source[:, lanes]
        lab = labels[:, lanes]
        rel = jnp.full(lab.shape, table[0], F32)
        for m in range(1, 8):
            rel = jnp.where(lab == m, table[m], rel)
        sides[side, pl.ds(2 * LANES, LANES), :] = rel
    for side in range(2):
        for quantity in range(3):
            parts = []
            for half in range(2):
                for x in range(8):
                    first = quantity * LANES + half * 64 + x
                    parts.append(sides[side, pl.ds(first, 8, stride=8), :])
            for block, part in enumerate(block_transpose(parts)):
                dest = OWNER[16 * side + block]
                out[pl.ds(dest * 24 + quantity * 8, 8), :] = part


def unpack_kernel(arrived, out, sides):
    for side in range(2):
        for c in range(2):
            parts = [arrived[pl.ds(OWNER[16 * side + b] * 16 + c * 8, 8), :] for b in range(16)]
            for i, part in enumerate(block_transpose(parts)):
                half, x = divmod(i, 8)
                sides[side, pl.ds(c * LANES + half * 64 + x, 8, stride=8), :] = part
        out[:, pl.ds(side * LANES, LANES)] = sides[side]


def lane_ids():
    lane = lax.broadcasted_iota(jnp.int32, (SLABS, LANES), 1)
    return lane >= 64, (lane // 8) % 8, lane % 8


def up(a, h):
    if h >= 2:
        return roll(a, h // 2, 0)
    upper, _, _ = lane_ids()
    turned = roll(a, 64, 1)
    return jnp.where(upper, turned, roll(turned, 1, 0))


def down(a, h):
    if h >= 2:
        return roll(a, -(h // 2), 0)
    upper, _, _ = lane_ids()
    turned = roll(a, 64, 1)
    return jnp.where(upper, roll(turned, -1, 0), turned)


def both(f, a, h):
    return f(a[0], h), f(a[1], h)


def layer(ref, quantity, r):
    return ref[pl.ds(quantity * 8 + r, SLABS, stride=24), :]


def source_layer(ref, r):
    return layer(ref, 0, r), layer(ref, 1, r)


def put(ref, i, a):
    ref[pl.ds(2 * i * SLABS, SLABS), :] = a[0]
    ref[pl.ds((2 * i + 1) * SLABS, SLABS), :] = a[1]


def get(ref, i):
    return ref[pl.ds(2 * i * SLABS, SLABS), :], ref[pl.ds((2 * i + 1) * SLABS, SLABS), :]


N_FACTORS = 7 + 2 * STEPS + 1


def factorize(arrived, factors):
    upper, _, _ = lane_ids()
    row = lax.broadcasted_iota(jnp.int32, (SLABS, LANES), 0)
    first = row * 16 + jnp.where(upper, 8, 0)
    pivots = []
    diagonal = None
    for r in range(DEPTH):
        z = first + r
        relative = layer(arrived, 2, r)
        inward = jnp.maximum(jnp.maximum(PML - z, z - (NZ - 1 - PML)), 0)
        fraction = inward.astype(F32) / PML
        diagonal = (
            (2.0 + 4.0 * COUPLE) - WAVE_SHIFT * relative,
            (DAMPING * WAVE_SHIFT) * relative + ABSORB * fraction * fraction,
        )
        if r < DEPTH - 1:
            pivots.append(crecip(diagonal if r == 0 else csub(diagonal, pivots[-1])))
            put(factors, r, pivots[-1])
    to_first = pivots[0]
    first_first = pivots[0]
    for r in range(1, DEPTH - 1):
        reached = cmul(to_first, to_first)
        to_first = cmul(to_first, pivots[r])
        first_first = cadd(first_first, cmul(reached, pivots[r]))
    corner = to_first
    last_last = pivots[-1]
    low = (row == 0) & jnp.logical_not(upper)
    left = tuple(jnp.where(low, 0.0, v) for v in corner)
    high = (row == SLABS - 1) & upper
    next_first = tuple(jnp.where(high, 0.0, v) for v in both(down, first_first, 1))
    d = csub(csub(diagonal, last_last), next_first)
    for step in range(STEPS):
        h = 1 << step
        right = both(down, left, h)
        inverse = crecip(d)
        alpha = cmul(left, both(up, inverse, h))
        gamma = cmul(right, both(down, inverse, h))
        put(factors, 7 + 2 * step, alpha)
        put(factors, 8 + 2 * step, gamma)
        d = csub(csub(d, cmul(alpha, left)), cmul(gamma, right))
        left = cmul(alpha, both(up, left, h))
    put(factors, 7 + 2 * STEPS, crecip(d))


def line_solve(rhs, factors):
    pivots = [get(factors, r) for r in range(DEPTH - 1)]
    gone = [rhs[0]]
    for r in range(1, DEPTH - 1):
        gone.append(cadd(rhs[r], cmul(pivots[r - 1], gone[-1])))
    last = cmul(pivots[-1], gone[-1])
    reach = pivots[0]
    reaches = []
    first = cmul(pivots[0], gone[0])
    for r in range(1, DEPTH - 1):
        reaches.append(reach)
        reach = cmul(reach, pivots[r])
        first = cadd(first, cmul(reach, gone[r]))
    upper, _, _ = lane_ids()
    row = lax.broadcasted_iota(jnp.int32, (SLABS, LANES), 0)
    high = (row == SLABS - 1) & upper
    low = (row == 0) & jnp.logical_not(upper)
    after = tuple(jnp.where(high, 0.0, v) for v in both(down, first, 1))
    g = cadd(cadd(rhs[DEPTH - 1], last), after)
    for step in range(STEPS):
        h = 1 << step
        from_low = cmul(get(factors, 7 + 2 * step), both(up, g, h))
        from_high = cmul(get(factors, 8 + 2 * step), both(down, g, h))
        g = cadd(g, cadd(from_low, from_high))
    separator = cmul(get(factors, 7 + 2 * STEPS), g)
    before = tuple(jnp.where(low, 0.0, v) for v in both(up, separator, 1))
    field = [None] * DEPTH
    field[DEPTH - 1] = separator
    for r in range(DEPTH - 2, -1, -1):
        lit = cadd(gone[r], before if r == 0 else cmul(reaches[r - 1], before))
        field[r] = cmul(pivots[r], cadd(lit, field[r + 1]))
    return field


def put_edges(field, edges):
    _, x, y = lane_ids()
    x_low, x_high, y_low, y_high = edges
    for c in range(2):
        sums = [None] * 4
        for r in range(DEPTH):
            f = field[r][c]
            for i, (shift, here) in enumerate(((8 * r, x), (8 * (r - 7), x), (r, y), (r - 7, y))):
                moved = roll(f, shift, 1)
                sums[i] = moved if r == 0 else jnp.where(here == r, moved, sums[i])
        for edge, value in zip(edges, sums):
            edge[pl.ds(c * SLABS, SLABS), :] = value


def transverse(field, halos):
    _, x, y = lane_ids()
    result = []
    for r in range(DEPTH):
        parts = []
        for c in range(2):
            f = field[r][c]
            edge = [h[pl.ds(c * SLABS, SLABS), :] for h in halos]
            total = jnp.where(x == 0, roll(edge[0], -8 * r, 1), roll(f, 8, 1))
            total += jnp.where(x == 7, roll(edge[1], 8 * (7 - r), 1), roll(f, -8, 1))
            total += jnp.where(y == 0, roll(edge[2], -r, 1), roll(f, 1, 1))
            total += jnp.where(y == 7, roll(edge[3], 7 - r, 1), roll(f, -1, 1))
            parts.append(total)
        result.append(tuple(parts))
    return result


def first_kernel(arrived, factors, field_out, *edges):
    factorize(arrived, factors)
    field = line_solve([source_layer(arrived, r) for r in range(DEPTH)], factors)
    for r in range(DEPTH):
        put(field_out, r, field[r])
    put_edges(field, edges)


def relaxed(arrived, factors, field_in, halos):
    spread = transverse([get(field_in, r) for r in range(DEPTH)], halos)
    rhs = []
    for r in range(DEPTH):
        s = source_layer(arrived, r)
        rhs.append((s[0] + COUPLE * spread[r][0], s[1] + COUPLE * spread[r][1]))
    return line_solve(rhs, factors)


def middle_kernel(arrived, factors, field_in, h0, h1, h2, h3, field_out, *edges):
    field = relaxed(arrived, factors, field_in, (h0, h1, h2, h3))
    for r in range(DEPTH):
        put(field_out, r, field[r])
    put_edges(field, edges)


def last_kernel(arrived, factors, field_in, h0, h1, h2, h3, out):
    field = relaxed(arrived, factors, field_in, (h0, h1, h2, h3))
    for r in range(DEPTH):
        for c in range(2):
            out[pl.ds(c * 8 + r, SLABS, stride=16), :] = field[r][c]


def call(kernel, name, outs, *args, scratch=(), smem=False):
    shapes = [jax.ShapeDtypeStruct(s, F32) for s in outs]
    specs = [VMEM] * len(args)
    if smem:
        specs[0] = SMEM
    result = pl.pallas_call(
        kernel,
        out_shape=shapes,
        in_specs=specs,
        out_specs=[VMEM] * len(outs),
        scratch_shapes=list(scratch),
        compiler_params=pltpu.CompilerParams(vmem_limit_bytes=32 << 20),
        name=name,
    )(*args)
    return result


FIELD = (DEPTH * 2 * SLABS, LANES)
FACTORS = (N_FACTORS * 2 * SLABS, LANES)
EDGE = (2 * SLABS, LANES)

TILE_UP = [(i, i + 1) for i in range(TILES - 1)]
TILE_DOWN = [(i + 1, i) for i in range(TILES - 1)]
SLAB_UP = [(OWNER[c], OWNER[c + 1]) for c in range(SLABS - 1)]
SLAB_DOWN = [(OWNER[c + 1], OWNER[c]) for c in range(SLABS - 1)]


def exchange(x_low, x_high, y_low, y_high):
    return (
        lax.ppermute(x_high, "tile", TILE_UP),
        lax.ppermute(x_low, "tile", TILE_DOWN),
        lax.ppermute(y_high, "slab", SLAB_UP),
        lax.ppermute(y_low, "slab", SLAB_DOWN),
    )


def local(source, labels, permittivity):
    rows = source.reshape(2 * 16 * 8, 256)
    marks = labels.reshape(16 * 8, 256)
    (packed,) = call(
        pack_kernel, "pack", [(SLABS * 24, LANES)], permittivity, rows, marks,
        scratch=[pltpu.VMEM((2, 3 * LANES, LANES), F32)], smem=True,
    )
    arrived = lax.all_to_all(packed.reshape(SLABS, 24, LANES), "slab", 0, 0).reshape(SLABS * 24, LANES)
    factors, field, *edges = call(first_kernel, "first", [FACTORS, FIELD] + [EDGE] * 4, arrived)
    halos = exchange(*edges)
    field, *edges = call(middle_kernel, "middle", [FIELD] + [EDGE] * 4, arrived, factors, field, *halos)
    halos = exchange(*edges)
    (packed,) = call(last_kernel, "last", [(SLABS * 16, LANES)], arrived, factors, field, *halos)
    arrived = lax.all_to_all(packed.reshape(SLABS, 16, LANES), "slab", 0, 0).reshape(SLABS * 16, LANES)
    (out,) = call(unpack_kernel, "unpack", [(2 * 16 * 8, 256)], arrived,
                  scratch=[pltpu.VMEM((2, 2 * LANES, LANES), F32)])
    return out.reshape(2, 16, 8, 256)


def solution(mesh):
    placed = (P("tilt", "slab", "tile", None), P("slab", "tile", "tilt"), P("tilt"))
    return jax.shard_map(
        local,
        mesh=mesh,
        in_specs=placed,
        out_specs=P("tilt", "slab", "tile", None),
        check_vma=False,
    )
```

time: 1470 us -> 102 us (0.07); the launches traced: 1440 us -> 101 us
  blocking collectives: 1250 us -> 65.2 us
  starting transfers between devices: 151 us -> 20.6 us
  other arithmetic: 19.6 us -> 0 us
  loops' own time: 19.5 us -> 0 us
    all_gather x12 -> x0, blocking collectives: 1250 us -> none  [prefix(): everything = jax.tree.map(lambda part: lax.all_gather(part, axis), value)]
    ppermute x4 -> x8, starting transfers between devices: 151 us -> 20.6 us  [the longest x2 9.83 us: exchange(): lax.ppermute(x_high, 'tile', TILE_UP)]
    all_to_all x0 -> x2, blocking collectives: none -> 65.2 us  [the longest x1 39.9 us: local(): lax.all_to_all(packed.reshape(SLABS, 24, LANES), 'slab', 0, 0)]
    another operation x17 -> x0, loops' own time: 19.5 us -> none  [the longest x7 12.4 us: prefix(): return lax.fori_loop(0, peers, step, start)]
  transfers between devices with their start and end apart: 4 -> 8, of which waited for: 2 -> 2; matrix products, arithmetic and copies ran while one was open for 0% -> 0% of each run, Pallas kernels for 0% -> 0%
where the time goes in v1:
time: 102 us; the launch traced here: 101 us
  blocking collectives  65.2 us (64%)
  starting transfers between devices  20.6 us (20%)
  waiting for transfers between devices  6.67 us (7%)
  Pallas kernels  5.81 us (6%)
  local copies, waits for them, and re-layouts  2.51 us (2%)
    all_to_all x1, blocking collectives, local(): lax.all_to_all(packed.reshape(SLABS, 24, LANES), 'slab', 0, 0)  39.9 us
    all_to_all x1, blocking collectives, local(): lax.all_to_all(packed.reshape(SLABS, 16, LANES), 'slab', 0, 0)  25.2 us
    ppermute x2, starting transfers between devices, exchange(): lax.ppermute(x_high, 'tile', TILE_UP)  9.83 us
    ppermute x2, waiting for transfers between devices, exchange(): lax.ppermute(y_low, 'slab', SLAB_DOWN)  6.65 us
    pallas_call x5, Pallas kernels, call(): pl.pallas_call(kernel, out_shape=shapes, in_specs=specs, out_specs=[VMEM]...  5.81 us
    ppermute x2, starting transfers between devices, exchange(): lax.ppermute(y_high, 'slab', SLAB_UP)  4.36 us
    ppermute x2, starting transfers between devices, exchange(): lax.ppermute(x_low, 'tile', TILE_DOWN)  3.84 us
    ppermute x2, starting transfers between devices, exchange(): lax.ppermute(y_low, 'slab', SLAB_DOWN)  2.58 us
  transfers between devices with their start and end apart: 8, of which 2 were waited for; matrix products, arithmetic and copies ran while one was open for 0% of the time, Pallas kernels for 0%

profile of v1, /device:TPU:1, one launch (start us, length us, event | category | flops | bytes accessed | tf_op | source)
XLA Modules:
  0.0 100.9 jit_solution(8708390282228392824)
XLA Ops:
  0.0 0.7 copy-done.2
  0.7 0.9 copy-done
  1.6 0.9 copy-done.1
  2.5 1.4 %pack.1 = f32[768,128]{1,0:T(8,128)S(1)} custom-call(f32[8]{0:T(128)S(1)} %copy-done.2, f32[256,256]{1,0:T(8,128)S(1)} %bitcast.13, s32[128,256]{1,0:T(8,128)S(1)} %bitcast.14), custom_call_target="tpu_custom_call" | custom-call | tf_op jit(solution)/shard_map/pack/pallas_call | solution.py:289
  3.9 39.9 %all_to_all.10 = f32[32,24,128]{2,1,0:T(8,128)S(1)} all-to-all(f32[32,24,128]{2,1,0:T(8,128)S(1)} %bitcast.10), channel_id=1, replica_groups=mesh['slab'=32,'tile'=8,'tilt'=2] {'slab'}, dimensions={0} | all-to-all | bytes 786432 | tf_op jit(solution)/shard_map/all_to_all | solution.py:327
  43.9 1.0 first.1
  44.9 4.8 %collective-permute-start = (f32[64,128]{1,0:T(8,128)S(1)}, f32[64,128]{1,0:T(8,128)S(1)}, u32[]{:S(2)}, u32[]{:S(2)}) collective-permute-start(f32[64,128]{1,0:T(8,128)S(1)} %get-tuple-element.18), channel_id=1, source_target_pairs={{0,2},{2,4},{4,6},{6,8},{8,10},{10,12},{12,14},{1,3},{3,5},{5,7},{... | collective-permute-start | bytes 98312 | tf_op jit(solution)/shard_map/ppermute | solution.py:313
  49.7 1.9 %collective-permute-start.1 = (f32[64,128]{1,0:T(8,128)S(1)}, f32[64,128]{1,0:T(8,128)S(1)}, u32[]{:S(2)}, u32[]{:S(2)}) collective-permute-start(f32[64,128]{1,0:T(8,128)S(1)} %get-tuple-element.19), channel_id=1, source_target_pairs={{2,0},{4,2},{6,4},{8,6},{10,8},{12,10},{14,12},{3,1},{5,3},{7,5},{... | collective-permute-start | bytes 98312 | tf_op jit(solution)/shard_map/ppermute | solution.py:314
  51.6 2.0 %collective-permute-start.2 = (f32[64,128]{1,0:T(8,128)S(1)}, f32[64,128]{1,0:T(8,128)S(1)}, u32[]{:S(2)}, u32[]{:S(2)}) collective-permute-start(f32[64,128]{1,0:T(8,128)S(1)} %get-tuple-element.20), channel_id=1, source_target_pairs={{0,16},{16,32},{32,48},{48,64},{64,80},{80,96},{96,112},{112,240},... | collective-permute-start | bytes 98312 | tf_op jit(solution)/shard_map/ppermute | solution.py:315
  53.6 1.3 %collective-permute-start.3 = (f32[64,128]{1,0:T(8,128)S(1)}, f32[64,128]{1,0:T(8,128)S(1)}, u32[]{:S(2)}, u32[]{:S(2)}) collective-permute-start(f32[64,128]{1,0:T(8,128)S(1)} %get-tuple-element.21), channel_id=1, source_target_pairs={{16,0},{32,16},{48,32},{64,48},{80,64},{96,80},{112,96},{240,112},... | collective-permute-start | bytes 98312 | tf_op jit(solution)/shard_map/ppermute | solution.py:316
  54.9 0.0 collective-permute-done.h0
  54.9 0.0 collective-permute-done.2.h2
  54.9 3.3 %collective-permute-done.3.h3 = f32[64,128]{1,0:T(8,128)S(1)} collective-permute-done((f32[64,128]{1,0:T(8,128)S(1)}, f32[64,128]{1,0:T(8,128)S(1)}, u32[]{:S(2)}, u32[]{:S(2)}) %collective-permute-start.3) | collective-permute-done | bytes 32800 | tf_op jit(solution)/shard_map/ppermute | solution.py:316
  58.3 1.2 %middle.1 = (f32[512,128]{1,0:T(8,128)S(1)}, f32[64,128]{1,0:T(8,128)S(1)}, f32[64,128]{1,0:T(8,128)S(1)}, f32[64,128]{1,0:T(8,128)S(1)}, f32[64,128]{1,0:T(8,128)S(1)}) custom-call(f32[768,128]{1,0:T(8,128)S(1)} %bitcast.8, f32[1280,128]{1,0:T(8,128)S(1)} %get-tuple-element.16.factors, f32[512,128]{1,0:T(8,128)S(1)} %get-tuple-element.17.field_in, ...), custom_call_target="tpu_custom_call" | custom-call | tf_op jit(solution)/shard_map/middle/pallas_call | solution.py:289
  59.5 5.1 %collective-permute-start.4 = (f32[64,128]{1,0:T(8,128)S(1)}, f32[64,128]{1,0:T(8,128)S(1)}, u32[]{:S(2)}, u32[]{:S(2)}) collective-permute-start(f32[64,128]{1,0:T(8,128)S(1)} %get-tuple-element.23), channel_id=1, source_target_pairs={{0,2},{2,4},{4,6},{6,8},{8,10},{10,12},{12,14},{1,3},{3,5},{5,7},{... | collective-permute-start | bytes 98312 | tf_op jit(solution)/shard_map/ppermute | solution.py:313
  64.6 1.9 %collective-permute-start.5 = (f32[64,128]{1,0:T(8,128)S(1)}, f32[64,128]{1,0:T(8,128)S(1)}, u32[]{:S(2)}, u32[]{:S(2)}) collective-permute-start(f32[64,128]{1,0:T(8,128)S(1)} %get-tuple-element.24), channel_id=1, source_target_pairs={{2,0},{4,2},{6,4},{8,6},{10,8},{12,10},{14,12},{3,1},{5,3},{7,5},{... | collective-permute-start | bytes 98312 | tf_op jit(solution)/shard_map/ppermute | solution.py:314
  66.5 2.4 %collective-permute-start.6 = (f32[64,128]{1,0:T(8,128)S(1)}, f32[64,128]{1,0:T(8,128)S(1)}, u32[]{:S(2)}, u32[]{:S(2)}) collective-permute-start(f32[64,128]{1,0:T(8,128)S(1)} %get-tuple-element.25), channel_id=1, source_target_pairs={{0,16},{16,32},{32,48},{48,64},{64,80},{80,96},{96,112},{112,240},... | collective-permute-start | bytes 98312 | tf_op jit(solution)/shard_map/ppermute | solution.py:315
  68.9 1.3 %collective-permute-start.7 = (f32[64,128]{1,0:T(8,128)S(1)}, f32[64,128]{1,0:T(8,128)S(1)}, u32[]{:S(2)}, u32[]{:S(2)}) collective-permute-start(f32[64,128]{1,0:T(8,128)S(1)} %get-tuple-element.26), channel_id=1, source_target_pairs={{16,0},{32,16},{48,32},{64,48},{80,64},{96,80},{112,96},{240,112},... | collective-permute-start | bytes 98312 | tf_op jit(solution)/shard_map/ppermute | solution.py:316
  70.2 0.0 collective-permute-done.4.h0
  70.2 0.0 collective-permute-done.6.h2
  70.2 3.3 %collective-permute-done.7.h3 = f32[64,128]{1,0:T(8,128)S(1)} collective-permute-done((f32[64,128]{1,0:T(8,128)S(1)}, f32[64,128]{1,0:T(8,128)S(1)}, u32[]{:S(2)}, u32[]{:S(2)}) %collective-permute-start.7) | collective-permute-done | bytes 32800 | tf_op jit(solution)/shard_map/ppermute | solution.py:316
  73.5 1.0 last.1
  74.5 25.2 %all_to_all.11 = f32[32,16,128]{2,1,0:T(8,128)S(1)} all-to-all(f32[32,16,128]{2,1,0:T(8,128)S(1)} %bitcast.12), channel_id=1, replica_groups=mesh['slab'=32,'tile'=8,'tilt'=2] {'slab'}, dimensions={0} | all-to-all | bytes 524288 | tf_op jit(solution)/shard_map/all_to_all | solution.py:333
  99.7 1.2 %unpack.1 = f32[256,256]{1,0:T(8,128)} custom-call(f32[512,128]{1,0:T(8,128)S(1)} %bitcast.11), custom_call_target="tpu_custom_call" | custom-call | tf_op jit(solution)/shard_map/unpack/pallas_call | solution.py:289
  (5 shorter events, 0.0 us)
Async XLA Ops:
  0.0 0.7 copy-start.2
  0.7 0.9 copy-start
  1.6 0.9 copy-start.1
  44.9 10.0 %collective-permute-start = (f32[64,128]{1,0:T(8,128)S(1)}, f32[64,128]{1,0:T(8,128)S(1)}, u32[]{:S(2)}, u32[]{:S(2)}) collective-permute-start(f32[64,128]{1,0:T(8,128)S(1)} %get-tuple-element.18), channel_id=1, source_target_pairs={{0,2},{2,4},{4,6},{6,8},{8,10},{10,12},{12,14},{1,3},{3,5},{5,7},{... | collective-permute-start | bytes 98312 | tf_op jit(solution)/shard_map/ppermute | solution.py:313
  49.7 5.2 %collective-permute-start.1 = (f32[64,128]{1,0:T(8,128)S(1)}, f32[64,128]{1,0:T(8,128)S(1)}, u32[]{:S(2)}, u32[]{:S(2)}) collective-permute-start(f32[64,128]{1,0:T(8,128)S(1)} %get-tuple-element.19), channel_id=1, source_target_pairs={{2,0},{4,2},{6,4},{8,6},{10,8},{12,10},{14,12},{3,1},{5,3},{7,5},{... | collective-permute-start | bytes 98312 | tf_op jit(solution)/shard_map/ppermute | solution.py:314
  51.6 3.3 %collective-permute-start.2 = (f32[64,128]{1,0:T(8,128)S(1)}, f32[64,128]{1,0:T(8,128)S(1)}, u32[]{:S(2)}, u32[]{:S(2)}) collective-permute-start(f32[64,128]{1,0:T(8,128)S(1)} %get-tuple-element.20), channel_id=1, source_target_pairs={{0,16},{16,32},{32,48},{48,64},{64,80},{80,96},{96,112},{112,240},... | collective-permute-start | bytes 98312 | tf_op jit(solution)/shard_map/ppermute | solution.py:315
  53.6 4.7 %collective-permute-start.3 = (f32[64,128]{1,0:T(8,128)S(1)}, f32[64,128]{1,0:T(8,128)S(1)}, u32[]{:S(2)}, u32[]{:S(2)}) collective-permute-start(f32[64,128]{1,0:T(8,128)S(1)} %get-tuple-element.21), channel_id=1, source_target_pairs={{16,0},{32,16},{48,32},{64,48},{80,64},{96,80},{112,96},{240,112},... | collective-permute-start | bytes 98312 | tf_op jit(solution)/shard_map/ppermute | solution.py:316
  59.5 10.7 %collective-permute-start.4 = (f32[64,128]{1,0:T(8,128)S(1)}, f32[64,128]{1,0:T(8,128)S(1)}, u32[]{:S(2)}, u32[]{:S(2)}) collective-permute-start(f32[64,128]{1,0:T(8,128)S(1)} %get-tuple-element.23), channel_id=1, source_target_pairs={{0,2},{2,4},{4,6},{6,8},{8,10},{10,12},{12,14},{1,3},{3,5},{5,7},{... | collective-permute-start | bytes 98312 | tf_op jit(solution)/shard_map/ppermute | solution.py:313
  64.6 5.6 %collective-permute-start.5 = (f32[64,128]{1,0:T(8,128)S(1)}, f32[64,128]{1,0:T(8,128)S(1)}, u32[]{:S(2)}, u32[]{:S(2)}) collective-permute-start(f32[64,128]{1,0:T(8,128)S(1)} %get-tuple-element.24), channel_id=1, source_target_pairs={{2,0},{4,2},{6,4},{8,6},{10,8},{12,10},{14,12},{3,1},{5,3},{7,5},{... | collective-permute-start | bytes 98312 | tf_op jit(solution)/shard_map/ppermute | solution.py:314
  66.5 3.7 %collective-permute-start.6 = (f32[64,128]{1,0:T(8,128)S(1)}, f32[64,128]{1,0:T(8,128)S(1)}, u32[]{:S(2)}, u32[]{:S(2)}) collective-permute-start(f32[64,128]{1,0:T(8,128)S(1)} %get-tuple-element.25), channel_id=1, source_target_pairs={{0,16},{16,32},{32,48},{48,64},{64,80},{80,96},{96,112},{112,240},... | collective-permute-start | bytes 98312 | tf_op jit(solution)/shard_map/ppermute | solution.py:315
  68.9 4.7 %collective-permute-start.7 = (f32[64,128]{1,0:T(8,128)S(1)}, f32[64,128]{1,0:T(8,128)S(1)}, u32[]{:S(2)}, u32[]{:S(2)}) collective-permute-start(f32[64,128]{1,0:T(8,128)S(1)} %get-tuple-element.26), channel_id=1, source_target_pairs={{16,0},{32,16},{48,32},{64,48},{80,64},{96,80},{112,96},{240,112},... | collective-permute-start | bytes 98312 | tf_op jit(solution)/shard_map/ppermute | solution.py:316

commit v2 on v1

v2 whole, which is shorter than its diff:
```python
import jax
import jax.numpy as jnp
from jax import lax
from jax.experimental import pallas as pl
from jax.experimental.pallas import tpu as pltpu
from jax.sharding import PartitionSpec as P

PML = 8
COUPLE = 0.02
WAVE_SHIFT = 0.15
DAMPING = 0.15
ABSORB = 0.5
NZ = 512
SLABS = 32
TILES = 8
LANES = 128
DEPTH = 8
STEPS = 6
F32 = jnp.float32
VMEM = pl.BlockSpec(memory_space=pltpu.VMEM)
SMEM = pl.BlockSpec(memory_space=pltpu.SMEM)


ROWS = 32


def owner(x_half, y_chunk):
    y, z = divmod(y_chunk, 4)
    return 8 * y + 2 * z + x_half


def roll(x, shift, axis):
    shift %= x.shape[axis]
    return x if shift == 0 else pltpu.roll(x, shift, axis)


def cmul(a, b):
    return a[0] * b[0] - a[1] * b[1], a[0] * b[1] + a[1] * b[0]


def cadd(a, b):
    return a[0] + b[0], a[1] + b[1]


def csub(a, b):
    return a[0] - b[0], a[1] - b[1]


def crecip(a):
    scale = 1.0 / (a[0] * a[0] + a[1] * a[1])
    return a[0] * scale, -a[1] * scale


def lanes8():
    return lax.broadcasted_iota(jnp.int32, (8, LANES), 1)


def block_transpose(parts):
    lane = lanes8()
    parts = list(parts)
    for bit in (1, 2, 4):
        low = (lane & (16 * bit)) == 0
        for i in range(8):
            if i & bit == 0:
                a, b = parts[i], parts[i | bit]
                parts[i] = jnp.where(low, a, roll(b, 16 * bit, 1))
                parts[i | bit] = jnp.where(low, roll(a, -16 * bit, 1), b)
    return parts


def overlap_parts(arrays):
    lane = lanes8()
    slot = lane % 16
    parts = [None, None]
    for q in range(3):
        below = [roll(arrays[side][q], 4 * q + 2, 1) for side in range(2)]
        above = [roll(arrays[side][q], 4 * q - 14, 1) for side in range(2)]
        for side in range(2):
            lower = jnp.where(lane < 16, below[1 - side], below[side])
            upper = jnp.where(lane >= 112, above[1 - side], above[side])
            merged = jnp.where(slot < 4 * q + 2, lower, upper)
            parts[side] = merged if q == 0 else jnp.where(slot < 4 * q, parts[side], merged)
    return parts


def pack_kernel(table, source, labels, out, sides):
    for side in range(2):
        lanes = pl.ds(side * LANES, LANES)
        sides[side, pl.ds(0, 2 * LANES), :] = source[:, lanes]
        lab = labels[:, lanes]
        rel = jnp.full(lab.shape, table[0], F32)
        for m in range(1, 8):
            rel = jnp.where(lab == m, table[m], rel)
        sides[side, pl.ds(2 * LANES, LANES), :] = rel

    def load(side, quantity, half, x):
        return sides[side, pl.ds(quantity * LANES + half * 64 + x, 8, stride=8), :]

    for x_half in range(2):
        overlaps = [[], []]
        for half in range(2):
            for x in range(4 * x_half, 4 * x_half + 4):
                arrays = [[load(side, q, half, x) for q in range(3)] for side in range(2)]
                for side, part in enumerate(overlap_parts(arrays)):
                    overlaps[side].append(part)
        for side in range(2):
            for quantity in range(4):
                if quantity == 3:
                    parts = overlaps[side]
                else:
                    parts = [load(side, quantity, i // 4, 4 * x_half + i % 4) for i in range(8)]
                for block, part in enumerate(block_transpose(parts)):
                    dest = owner(x_half, 8 * side + block)
                    out[pl.ds(dest * ROWS + quantity * 8, 8), :] = part


def unpack_kernel(arrived, out, sides):
    for side in range(2):
        for c in range(2):
            for x_half in range(2):
                parts = [arrived[pl.ds(owner(x_half, 8 * side + b) * 16 + c * 8, 8), :] for b in range(8)]
                for i, part in enumerate(block_transpose(parts)):
                    half, x = divmod(i, 4)
                    sides[side, pl.ds(c * LANES + half * 64 + 4 * x_half + x, 8, stride=8), :] = part
        out[:, pl.ds(side * LANES, LANES)] = sides[side]


def lane_ids():
    lane = lax.broadcasted_iota(jnp.int32, (SLABS, LANES), 1)
    return lane >= 64, (lane // 16) % 4, lane % 16


def upper_half(overlap):
    lane = lax.broadcasted_iota(jnp.int32, (SLABS, LANES), 1)
    if overlap:
        lane = (lane + jnp.where(lane % 16 >= 8, 16, LANES - 16)) % LANES
    return lane >= 64


def up(a, h, upper):
    if h >= 2:
        return roll(a, h // 2, 0)
    turned = roll(a, 64, 1)
    return jnp.where(upper, turned, roll(turned, 1, 0))


def down(a, h, upper):
    if h >= 2:
        return roll(a, -(h // 2), 0)
    turned = roll(a, 64, 1)
    return jnp.where(upper, roll(turned, -1, 0), turned)


def both(f, a, h, upper):
    return f(a[0], h, upper), f(a[1], h, upper)


def layer(ref, quantity, r):
    return ref[pl.ds(quantity * 8 + r, SLABS, stride=ROWS), :]


def source_layer(ref, r):
    return layer(ref, 0, r), layer(ref, 1, r)


def overlap_layer(ref, r):
    _, _, y = lane_ids()
    packed = layer(ref, 3, r)
    quantities = []
    for q in range(3):
        quantities.append(jnp.where(y >= 8, roll(packed, -2 - 4 * q, 1), roll(packed, 14 - 4 * q, 1)))
    used = (y <= 1) | (y >= 14)
    return quantities[0], quantities[1], jnp.where(used, quantities[2], 1.0)


def inside():
    chunk = lax.axis_index("slab") // 2
    _, _, y = lane_ids()
    below = (y >= 14) & jnp.broadcast_to(chunk > 0, y.shape)
    above = (y <= 1) & jnp.broadcast_to(chunk < 15, y.shape)
    return below | above


def put(ref, i, a):
    ref[pl.ds(2 * i * SLABS, SLABS), :] = a[0]
    ref[pl.ds((2 * i + 1) * SLABS, SLABS), :] = a[1]


def get(ref, i):
    return ref[pl.ds(2 * i * SLABS, SLABS), :], ref[pl.ds((2 * i + 1) * SLABS, SLABS), :]


N_FACTORS = 7 + 2 * STEPS + 1


def factorize(relatives, factors, overlap=False):
    upper = upper_half(overlap)
    row = lax.broadcasted_iota(jnp.int32, (SLABS, LANES), 0)
    first = row * 16 + jnp.where(upper, 8, 0)
    pivots = []
    diagonal = None
    for r in range(DEPTH):
        z = first + r
        relative = relatives[r]
        inward = jnp.maximum(jnp.maximum(PML - z, z - (NZ - 1 - PML)), 0)
        fraction = inward.astype(F32) / PML
        diagonal = (
            (2.0 + 4.0 * COUPLE) - WAVE_SHIFT * relative,
            (DAMPING * WAVE_SHIFT) * relative + ABSORB * fraction * fraction,
        )
        if r < DEPTH - 1:
            pivots.append(crecip(diagonal if r == 0 else csub(diagonal, pivots[-1])))
            put(factors, r, pivots[-1])
    to_first = pivots[0]
    first_first = pivots[0]
    for r in range(1, DEPTH - 1):
        reached = cmul(to_first, to_first)
        to_first = cmul(to_first, pivots[r])
        first_first = cadd(first_first, cmul(reached, pivots[r]))
    corner = to_first
    last_last = pivots[-1]
    low = (row == 0) & jnp.logical_not(upper)
    left = tuple(jnp.where(low, 0.0, v) for v in corner)
    high = (row == SLABS - 1) & upper
    next_first = tuple(jnp.where(high, 0.0, v) for v in both(down, first_first, 1, upper))
    d = csub(csub(diagonal, last_last), next_first)
    for step in range(STEPS):
        h = 1 << step
        right = both(down, left, h, upper)
        inverse = crecip(d)
        alpha = cmul(left, both(up, inverse, h, upper))
        gamma = cmul(right, both(down, inverse, h, upper))
        put(factors, 7 + 2 * step, alpha)
        put(factors, 8 + 2 * step, gamma)
        d = csub(csub(d, cmul(alpha, left)), cmul(gamma, right))
        left = cmul(alpha, both(up, left, h, upper))
    put(factors, 7 + 2 * STEPS, crecip(d))


def line_solve(rhs, factors, overlap=False):
    pivots = [get(factors, r) for r in range(DEPTH - 1)]
    gone = [rhs[0]]
    for r in range(1, DEPTH - 1):
        gone.append(cadd(rhs[r], cmul(pivots[r - 1], gone[-1])))
    last = cmul(pivots[-1], gone[-1])
    reach = pivots[0]
    reaches = []
    first = cmul(pivots[0], gone[0])
    for r in range(1, DEPTH - 1):
        reaches.append(reach)
        reach = cmul(reach, pivots[r])
        first = cadd(first, cmul(reach, gone[r]))
    upper = upper_half(overlap)
    row = lax.broadcasted_iota(jnp.int32, (SLABS, LANES), 0)
    high = (row == SLABS - 1) & upper
    low = (row == 0) & jnp.logical_not(upper)
    after = tuple(jnp.where(high, 0.0, v) for v in both(down, first, 1, upper))
    g = cadd(cadd(rhs[DEPTH - 1], last), after)
    for step in range(STEPS):
        h = 1 << step
        from_low = cmul(get(factors, 7 + 2 * step), both(up, g, h, upper))
        from_high = cmul(get(factors, 8 + 2 * step), both(down, g, h, upper))
        g = cadd(g, cadd(from_low, from_high))
    separator = cmul(get(factors, 7 + 2 * STEPS), g)
    before = tuple(jnp.where(low, 0.0, v) for v in both(up, separator, 1, upper))
    field = [None] * DEPTH
    field[DEPTH - 1] = separator
    for r in range(DEPTH - 2, -1, -1):
        lit = cadd(gone[r], before if r == 0 else cmul(reaches[r - 1], before))
        field[r] = cmul(pivots[r], cadd(lit, field[r + 1]))
    return field


def put_edges(main, over, edges):
    _, x, y = lane_ids()
    for edge, is_high in zip(edges, (False, True)):
        for c in range(2):
            for group in range(2):
                total = None
                for i in range(4):
                    moved = roll(main[4 * group + i][c], 16 * (i - 3) if is_high else 16 * i, 1)
                    total = moved if i == 0 else jnp.where(x == i, moved, total)
                edge[pl.ds((2 * c + group) * SLABS, SLABS), :] = total
        if over is None:
            continue
        below_at, above_at = (2, 0) if is_high else (3, 1)
        total = jnp.zeros((SLABS, LANES), F32)
        for c in range(2):
            for r in range(DEPTH):
                f = over[r][c]
                below = (x == (below_at + c) % 4) & (y == 15 - r)
                above = (x == (above_at + c) % 4) & (y == r)
                total = jnp.where(below, roll(f, 16 * c - r, 1), total)
                total = jnp.where(above, roll(f, 16 * c + r, 1), total)
        edge[pl.ds(4 * SLABS, SLABS), :] = total


def transverse(main, over, halos, with_overlap):
    _, x, y = lane_ids()
    results, over_results = [], []
    for r in range(DEPTH):
        parts, over_parts = [], []
        for c in range(2):
            m, e = main[r][c], over[r][c]
            low, high = (h[pl.ds((2 * c + r // 4) * SLABS, SLABS), :] for h in halos)
            m_up, m_down = roll(m, 1, 1), roll(m, -1, 1)
            e_up, e_down = roll(e, 1, 1), roll(e, -1, 1)
            along_x = jnp.where(x == 0, roll(low, -16 * (r % 4), 1), roll(m, 16, 1)) + jnp.where(
                x == 3, roll(high, 16 * (3 - r % 4), 1), roll(m, -16, 1)
            )
            along_y = jnp.where(y == 0, e_up, m_up) + jnp.where(y == 15, e_down, m_down)
            parts.append(along_x + along_y)
            if with_overlap:
                low, high = (h[pl.ds(4 * SLABS, SLABS), :] for h in halos)
                below = y >= 8
                from_low = jnp.where(below, roll(low, -48 - 16 * c + r, 1), roll(low, -48 - 16 * c - r, 1))
                from_high = jnp.where(below, roll(high, 48 - 16 * c + r, 1), roll(high, 48 - 16 * c - r, 1))
                at_low = x == jnp.where(below, 3, 1)
                at_high = x == jnp.where(below, 2, 0)
                along_x = jnp.where(at_low, from_low, roll(e, 16, 1)) + jnp.where(at_high, from_high, roll(e, -16, 1))
                along_y = jnp.where(below, e_up + m_down, m_up + e_down)
                over_parts.append(along_x + along_y)
        results.append(parts)
        over_results.append(over_parts)
    return results, over_results


def relax(source, spread):
    return tuple(s + COUPLE * t for s, t in zip(source, spread))


def masked(field):
    keep = inside()
    return [tuple(jnp.where(keep, v, 0.0) for v in f) for f in field]


def put_all(ref, field):
    for r in range(DEPTH):
        put(ref, r, field[r])


def get_all(ref):
    return [get(ref, r) for r in range(DEPTH)]


def first_kernel(arrived, factors, over_factors, over_source, main_out, over_out, *edges):
    factorize([layer(arrived, 2, r) for r in range(DEPTH)], factors)
    main = line_solve([source_layer(arrived, r) for r in range(DEPTH)], factors)
    put_all(main_out, main)
    overlap = [overlap_layer(arrived, r) for r in range(DEPTH)]
    factorize([o[2] for o in overlap], over_factors, True)
    put_all(over_source, [o[:2] for o in overlap])
    over = masked(line_solve([o[:2] for o in overlap], over_factors, True))
    put_all(over_out, over)
    put_edges(main, over, edges)


def middle_kernel(arrived, factors, over_factors, over_source, main_in, over_in, low, high, main_out, over_out, *edges):
    spread, over_spread = transverse(get_all(main_in), get_all(over_in), (low, high), True)
    main = line_solve([relax(source_layer(arrived, r), spread[r]) for r in range(DEPTH)], factors)
    put_all(main_out, main)
    put_edges(main, None, edges)
    over = line_solve([relax(get(over_source, r), over_spread[r]) for r in range(DEPTH)], over_factors, True)
    put_all(over_out, masked(over))


def last_kernel(arrived, factors, main_in, over_in, low, high, out):
    spread, _ = transverse(get_all(main_in), get_all(over_in), (low, high), False)
    field = line_solve([relax(source_layer(arrived, r), spread[r]) for r in range(DEPTH)], factors)
    for r in range(DEPTH):
        for c in range(2):
            out[pl.ds(c * 8 + r, SLABS, stride=16), :] = field[r][c]


def call(kernel, name, outs, *args, scratch=(), smem=False):
    shapes = [jax.ShapeDtypeStruct(s, F32) for s in outs]
    specs = [VMEM] * len(args)
    if smem:
        specs[0] = SMEM
    result = pl.pallas_call(
        kernel,
        out_shape=shapes,
        in_specs=specs,
        out_specs=[VMEM] * len(outs),
        scratch_shapes=list(scratch),
        compiler_params=pltpu.CompilerParams(vmem_limit_bytes=32 << 20),
        name=name,
    )(*args)
    return result


FIELD = (DEPTH * 2 * SLABS, LANES)
FACTORS = (N_FACTORS * 2 * SLABS, LANES)
EDGE = (5 * SLABS, LANES)
SHORT_EDGE = (4 * SLABS, LANES)


def x_neighbours():
    pairs = []
    for y_chunk in range(16):
        for tile in range(TILES):
            pairs.append((owner(0, y_chunk) * TILES + tile, owner(1, y_chunk) * TILES + tile))
            if tile + 1 < TILES:
                pairs.append((owner(1, y_chunk) * TILES + tile, owner(0, y_chunk) * TILES + tile + 1))
    return pairs


X_UP = x_neighbours()
X_DOWN = [(b, a) for a, b in X_UP]


def exchange(low, high):
    axes = ("slab", "tile")
    return lax.ppermute(high, axes, X_UP), lax.ppermute(low, axes, X_DOWN)


def local(source, labels, permittivity):
    rows = source.reshape(2 * 16 * 8, 256)
    marks = labels.reshape(16 * 8, 256)
    (packed,) = call(
        pack_kernel, "pack", [(SLABS * ROWS, LANES)], permittivity, rows, marks,
        scratch=[pltpu.VMEM((2, 3 * LANES, LANES), F32)], smem=True,
    )
    arrived = lax.all_to_all(packed.reshape(SLABS, ROWS, LANES), "slab", 0, 0).reshape(SLABS * ROWS, LANES)
    factors, over_factors, over_source, main, over, *edges = call(
        first_kernel, "first", [FACTORS, FACTORS, FIELD, FIELD, FIELD, EDGE, EDGE], arrived
    )
    halos = exchange(*edges)
    main, over, *edges = call(
        middle_kernel, "middle", [FIELD, FIELD, SHORT_EDGE, SHORT_EDGE],
        arrived, factors, over_factors, over_source, main, over, *halos,
    )
    halos = exchange(*edges)
    (packed,) = call(last_kernel, "last", [(SLABS * 16, LANES)], arrived, factors, main, over, *halos)
    arrived = lax.all_to_all(packed.reshape(SLABS, 16, LANES), "slab", 0, 0).reshape(SLABS * 16, LANES)
    (out,) = call(
        unpack_kernel, "unpack", [(2 * 16 * 8, 256)], arrived, scratch=[pltpu.VMEM((2, 2 * LANES, LANES), F32)]
    )
    return out.reshape(2, 16, 8, 256)


def solution(mesh):
    placed = (P("tilt", "slab", "tile", None), P("slab", "tile", "tilt"), P("tilt"))
    return jax.shard_map(
        local,
        mesh=mesh,
        in_specs=placed,
        out_specs=P("tilt", "slab", "tile", None),
        check_vma=False,
    )
```

time: 102 us -> 101 us (level)
  starting transfers between devices: 20.6 us -> 12.5 us
  blocking collectives: 65.2 us -> 70.3 us
  Pallas kernels: 5.81 us -> 7.93 us
    ppermute x8 -> x4, starting transfers between devices: 20.6 us -> 12.5 us  [exchange(): return (lax.ppermute(high, axes, X_UP), lax.ppermute(low, axes, X_DOWN))]
    all_to_all x1, blocking collectives: 39.9 us -> 45.2 us  [local(): lax.all_to_all(packed.reshape(SLABS, ROWS, LANES), 'slab', 0, 0)]
    pallas_call x5, Pallas kernels: 5.81 us -> 7.93 us  [call(): pl.pallas_call(kernel, out_shape=shapes, in_specs=specs, out_specs=[VMEM]...]
    ppermute x8 -> x4, waiting for transfers between devices: 6.67 us -> 7.09 us  [exchange(): return (lax.ppermute(high, axes, X_UP), lax.ppermute(low, axes, X_DOWN))]
  transfers between devices with their start and end apart: 8 -> 4, of which waited for: 2 -> 3; matrix products, arithmetic and copies ran while one was open for 0% -> 0% of each run, Pallas kernels for 0% -> 0%
where the time goes in v2:
time: 101 us; the launch traced here: 100 us
  blocking collectives  70.3 us (70%)
  starting transfers between devices  12.5 us (12%)
  Pallas kernels  7.93 us (8%)
  waiting for transfers between devices  7.09 us (7%)
  local copies, waits for them, and re-layouts  2.51 us (2%)
    all_to_all x1, blocking collectives, local(): lax.all_to_all(packed.reshape(SLABS, ROWS, LANES), 'slab', 0, 0)  45.2 us
    all_to_all x1, blocking collectives, local(): lax.all_to_all(packed.reshape(SLABS, 16, LANES), 'slab', 0, 0)  25.1 us
    ppermute x4, starting transfers between devices, exchange(): return (lax.ppermute(high, axes, X_UP), lax.ppermute(low, axes, X_DOWN))  12.5 us
    pallas_call x5, Pallas kernels, call(): pl.pallas_call(kernel, out_shape=shapes, in_specs=specs, out_specs=[VMEM]...  7.93 us
    ppermute x4, waiting for transfers between devices, exchange(): return (lax.ppermute(high, axes, X_UP), lax.ppermute(low, axes, X_DOWN))  7.09 us
    unnamed x6, local copies, waits for them, and re-layouts  2.51 us
  transfers between devices with their start and end apart: 4, of which 3 were waited for; matrix products, arithmetic and copies ran while one was open for 0% of the time, Pallas kernels for 0%

profile of v2, /device:TPU:1, one launch (start us, length us, event | category | flops | bytes accessed | tf_op | source)
XLA Modules:
  0.0 100.4 jit_solution(3368677921870744341)
XLA Ops:
  0.0 0.0 copy-start.2
  0.0 0.7 copy-done.2
  0.7 0.0 copy-start
  0.7 0.9 copy-done
  1.6 0.0 copy-start.1
  1.6 0.9 copy-done.1
  2.5 2.7 %pack.1 = f32[1024,128]{1,0:T(8,128)S(1)} custom-call(f32[8]{0:T(128)S(1)} %copy-done.2, f32[256,256]{1,0:T(8,128)S(1)} %bitcast.13, s32[128,256]{1,0:T(8,128)S(1)} %bitcast.14), custom_call_target="tpu_custom_call" | custom-call | tf_op jit(solution)/shard_map/pack/pallas_call | solution.py:380
  5.2 45.2 %all_to_all.10 = f32[32,32,128]{2,1,0:T(8,128)S(1)} all-to-all(f32[32,32,128]{2,1,0:T(8,128)S(1)} %bitcast.10), channel_id=1, replica_groups=mesh['slab'=32,'tile'=8,'tilt'=2] {'slab'}, dimensions={0} | all-to-all | bytes 1048576 | tf_op jit(solution)/shard_map/all_to_all | solution.py:424
  50.4 1.6 %first.1 = (f32[1280,128]{1,0:T(8,128)S(1)}, f32[1280,128]{1,0:T(8,128)S(1)}, f32[512,128]{1,0:T(8,128)S(1)}, f32[512,128]{1,0:T(8,128)S(1)}, f32[512,128]{1,0:T...) custom-call(f32[1024,128]{1,0:T(8,128)S(1)} %bitcast.7), custom_call_target="tpu_custom_call" | custom-call | tf_op jit(solution)/shard_map/first/pallas_call | solution.py:380
  52.0 1.9 %collective-permute-start = (f32[160,128]{1,0:T(8,128)S(1)}, f32[160,128]{1,0:T(8,128)S(1)}, u32[]{:S(2)}, u32[]{:S(2)}) collective-permute-start(f32[160,128]{1,0:T(8,128)S(1)} %get-tuple-element.21), channel_id=1, source_target_pairs={{0,16},{16,2},{2,18},{18,4},{4,20},{20,6},{6,22},{22,8},{8,24},{24... | collective-permute-start | bytes 245768 | tf_op jit(solution)/shard_map/ppermute | solution.py:414
  53.9 4.3 %collective-permute-start.1 = (f32[160,128]{1,0:T(8,128)S(1)}, f32[160,128]{1,0:T(8,128)S(1)}, u32[]{:S(2)}, u32[]{:S(2)}) collective-permute-start(f32[160,128]{1,0:T(8,128)S(1)} %get-tuple-element.22), channel_id=1, source_target_pairs={{16,0},{2,16},{18,2},{4,18},{20,4},{6,20},{22,6},{8,22},{24,8},{10... | collective-permute-start | bytes 245768 | tf_op jit(solution)/shard_map/ppermute | solution.py:414
  58.3 0.2 collective-permute-done.low
  58.5 3.8 %collective-permute-done.1.high = f32[160,128]{1,0:T(8,128)S(1)} collective-permute-done((f32[160,128]{1,0:T(8,128)S(1)}, f32[160,128]{1,0:T(8,128)S(1)}, u32[]{:S(2)}, u32[]{:S(2)}) %collective-permute-start.1) | collective-permute-done | bytes 81952 | tf_op jit(solution)/shard_map/ppermute | solution.py:414
  62.3 1.6 %middle.1 = (f32[512,128]{1,0:T(8,128)S(1)}, f32[512,128]{1,0:T(8,128)S(1)}, f32[128,128]{1,0:T(8,128)S(1)}, f32[128,128]{1,0:T(8,128)S(1)}) custom-call(f32[1024,128]{1,0:T(8,128)S(1)} %bitcast.8, f32[1280,128]{1,0:T(8,128)S(1)} %get-tuple-element.16.factors, f32[1280,128]{1,0:T(8,128)S(1)} %get-tuple-element.17.over_factors, ...), custom_call_target="tpu_custom_call" | custom-call | tf_op jit(solution)/shard_map/middle/pallas_call | solution.py:380
  63.9 4.3 %collective-permute-start.2 = (f32[128,128]{1,0:T(8,128)S(1)}, f32[128,128]{1,0:T(8,128)S(1)}, u32[]{:S(2)}, u32[]{:S(2)}) collective-permute-start(f32[128,128]{1,0:T(8,128)S(1)} %get-tuple-element.25), channel_id=1, source_target_pairs={{0,16},{16,2},{2,18},{18,4},{4,20},{20,6},{6,22},{22,8},{8,24},{24... | collective-permute-start | bytes 196616 | tf_op jit(solution)/shard_map/ppermute | solution.py:414
  68.2 1.9 %collective-permute-start.3 = (f32[128,128]{1,0:T(8,128)S(1)}, f32[128,128]{1,0:T(8,128)S(1)}, u32[]{:S(2)}, u32[]{:S(2)}) collective-permute-start(f32[128,128]{1,0:T(8,128)S(1)} %get-tuple-element.26), channel_id=1, source_target_pairs={{16,0},{2,16},{18,2},{4,18},{20,4},{6,20},{22,6},{8,22},{24,8},{10... | collective-permute-start | bytes 196616 | tf_op jit(solution)/shard_map/ppermute | solution.py:414
  70.1 0.0 collective-permute-done.2.low
  70.1 3.1 %collective-permute-done.3.high = f32[128,128]{1,0:T(8,128)S(1)} collective-permute-done((f32[128,128]{1,0:T(8,128)S(1)}, f32[128,128]{1,0:T(8,128)S(1)}, u32[]{:S(2)}, u32[]{:S(2)}) %collective-permute-start.3) | collective-permute-done | bytes 65568 | tf_op jit(solution)/shard_map/ppermute | solution.py:414
  73.2 1.0 last.1
  74.2 25.1 %all_to_all.11 = f32[32,16,128]{2,1,0:T(8,128)S(1)} all-to-all(f32[32,16,128]{2,1,0:T(8,128)S(1)} %bitcast.12), channel_id=1, replica_groups=mesh['slab'=32,'tile'=8,'tilt'=2] {'slab'}, dimensions={0} | all-to-all | bytes 524288 | tf_op jit(solution)/shard_map/all_to_all | solution.py:435
  99.3 1.1 %unpack.1 = f32[256,256]{1,0:T(8,128)} custom-call(f32[512,128]{1,0:T(8,128)S(1)} %bitcast.11), custom_call_target="tpu_custom_call" | custom-call | tf_op jit(solution)/shard_map/unpack/pallas_call | solution.py:380
Async XLA Ops:
  0.0 0.7 copy-start.2
  0.7 0.9 copy-start
  1.6 0.9 copy-start.1
  52.0 6.5 %collective-permute-start = (f32[160,128]{1,0:T(8,128)S(1)}, f32[160,128]{1,0:T(8,128)S(1)}, u32[]{:S(2)}, u32[]{:S(2)}) collective-permute-start(f32[160,128]{1,0:T(8,128)S(1)} %get-tuple-element.21), channel_id=1, source_target_pairs={{0,16},{16,2},{2,18},{18,4},{4,20},{20,6},{6,22},{22,8},{8,24},{24... | collective-permute-start | bytes 245768 | tf_op jit(solution)/shard_map/ppermute | solution.py:414
  53.9 8.4 %collective-permute-start.1 = (f32[160,128]{1,0:T(8,128)S(1)}, f32[160,128]{1,0:T(8,128)S(1)}, u32[]{:S(2)}, u32[]{:S(2)}) collective-permute-start(f32[160,128]{1,0:T(8,128)S(1)} %get-tuple-element.22), channel_id=1, source_target_pairs={{16,0},{2,16},{18,2},{4,18},{20,4},{6,20},{22,6},{8,22},{24,8},{10... | collective-permute-start | bytes 245768 | tf_op jit(solution)/shard_map/ppermute | solution.py:414
  63.9 6.2 %collective-permute-start.2 = (f32[128,128]{1,0:T(8,128)S(1)}, f32[128,128]{1,0:T(8,128)S(1)}, u32[]{:S(2)}, u32[]{:S(2)}) collective-permute-start(f32[128,128]{1,0:T(8,128)S(1)} %get-tuple-element.25), channel_id=1, source_target_pairs={{0,16},{16,2},{2,18},{18,4},{4,20},{20,6},{6,22},{22,8},{8,24},{24... | collective-permute-start | bytes 196616 | tf_op jit(solution)/shard_map/ppermute | solution.py:414
  68.2 5.0 %collective-permute-start.3 = (f32[128,128]{1,0:T(8,128)S(1)}, f32[128,128]{1,0:T(8,128)S(1)}, u32[]{:S(2)}, u32[]{:S(2)}) collective-permute-start(f32[128,128]{1,0:T(8,128)S(1)} %get-tuple-element.26), channel_id=1, source_target_pairs={{16,0},{2,16},{18,2},{4,18},{20,4},{6,20},{22,6},{8,22},{24,8},{10... | collective-permute-start | bytes 196616 | tf_op jit(solution)/shard_map/ppermute | solution.py:414

commit v3 on v2

v3 whole, which is shorter than its diff:
```python
import jax
import jax.numpy as jnp
from jax import lax
from jax.experimental import pallas as pl
from jax.experimental.pallas import tpu as pltpu
from jax.sharding import PartitionSpec as P

PML = 8
COUPLE = 0.02
WAVE_SHIFT = 0.15
DAMPING = 0.15
ABSORB = 0.5
NZ = 512
SLABS = 32
TILES = 8
LANES = 128
DEPTH = 8
STEPS = 6
F32 = jnp.float32
VMEM = pl.BlockSpec(memory_space=pltpu.VMEM)
HBM = pl.BlockSpec(memory_space=pltpu.HBM)


ROWS = 36


def roll(x, shift, axis):
    shift %= x.shape[axis]
    return x if shift == 0 else pltpu.roll(x, shift, axis)


def cmul(a, b):
    return a[0] * b[0] - a[1] * b[1], a[0] * b[1] + a[1] * b[0]


def cadd(a, b):
    return a[0] + b[0], a[1] + b[1]


def csub(a, b):
    return a[0] - b[0], a[1] - b[1]


def crecip(a):
    scale = 1.0 / (a[0] * a[0] + a[1] * a[1])
    return a[0] * scale, -a[1] * scale


def lanes8():
    return lax.broadcasted_iota(jnp.int32, (8, LANES), 1)


def lanes8():
    return lax.broadcasted_iota(jnp.int32, (8, LANES), 1)


def block_transpose(parts):
    lane = lanes8()
    parts = list(parts)
    for bit in (1, 2, 4, 8):
        low = (lane & (8 * bit)) == 0
        for i in range(16):
            if i & bit == 0:
                a, b = parts[i], parts[i | bit]
                parts[i] = jnp.where(low, a, roll(b, 8 * bit, 1))
                parts[i | bit] = jnp.where(low, roll(a, -8 * bit, 1), b)
    return parts


def overlap_parts(arrays, base):
    lane = lanes8()
    below = [roll(array, base + 2, 1) for array in arrays]
    above = [roll(array, base - 6, 1) for array in arrays]
    parts = []
    for side in range(2):
        lower = jnp.where(lane < 8, below[1 - side], below[side])
        upper = jnp.where(lane >= 120, above[1 - side], above[side])
        parts.append(jnp.where(lane % 8 < base + 2, lower, upper))
    return parts


def pack_kernel(table_hbm, source, labels, out, sides, marks, table, sems):
    copies = [pltpu.make_async_copy(table_hbm, table, sems.at[0])]
    for side in range(2):
        lanes = pl.ds(side * LANES, LANES)
        copies.append(pltpu.make_async_copy(labels.at[:, lanes], marks.at[side], sems.at[1 + side]))
        into = sides.at[side, pl.ds(0, 2 * LANES)]
        copies.append(pltpu.make_async_copy(source.at[:, lanes], into, sems.at[3 + side]))
    for copy in copies:
        copy.start()
    for copy in copies:
        copy.wait()
    for side in range(2):
        lab = marks[side]
        rel = jnp.full(lab.shape, table[0], F32)
        for m in range(1, 8):
            rel = jnp.where(lab == m, table[m], rel)
        sides[side, pl.ds(2 * LANES, LANES), :] = rel

    def load(side, quantity, half, x):
        return sides[side, pl.ds(quantity * LANES + half * 64 + x, 8, stride=8), :]

    slot = lanes8() % 8
    places = [(half, x) for half in range(2) for x in range(8)]
    pairs, singles = [[], []], [[], []]
    for quantity in range(3):
        arrays = [[load(side, quantity, half, x) for half, x in places] for side in range(2)]
        for side in range(2):
            for block, part in enumerate(block_transpose(arrays[side])):
                out[pl.ds((16 * side + block) * ROWS + quantity * 8, 8), :] = part
        for i in range(16):
            parts = overlap_parts([arrays[0][i], arrays[1][i]], 4 if quantity == 1 else 0)
            for side in range(2):
                if quantity == 0:
                    pairs[side].append(parts[side])
                elif quantity == 1:
                    pairs[side][i] = jnp.where(slot < 4, pairs[side][i], parts[side])
                else:
                    upper = roll(roll(parts[side], 4, 0), 4, 1)
                    singles[side].append(jnp.where(slot < 4, parts[side], upper))
    for side in range(2):
        for block, part in enumerate(block_transpose(pairs[side])):
            out[pl.ds((16 * side + block) * ROWS + 24, 8), :] = part
        for block, part in enumerate(block_transpose(singles[side])):
            out[pl.ds((16 * side + block) * ROWS + 32, 4), :] = part[:4]


def unpack_kernel(arrived, out, sides):
    for side in range(2):
        for c in range(2):
            parts = [arrived[pl.ds((16 * side + b) * 16 + c * 8, 8), :] for b in range(16)]
            for i, part in enumerate(block_transpose(parts)):
                half, x = divmod(i, 8)
                sides[side, pl.ds(c * LANES + half * 64 + x, 8, stride=8), :] = part
        out[:, pl.ds(side * LANES, LANES)] = sides[side]


def lane_ids():
    lane = lax.broadcasted_iota(jnp.int32, (SLABS, LANES), 1)
    return lane >= 64, (lane // 8) % 8, lane % 8


def upper_half(overlap):
    lane = lax.broadcasted_iota(jnp.int32, (SLABS, LANES), 1)
    if overlap:
        lane = (lane + jnp.where(lane % 8 >= 4, 8, LANES - 8)) % LANES
    return lane >= 64


def up(a, h, upper):
    if h >= 2:
        return roll(a, h // 2, 0)
    turned = roll(a, 64, 1)
    return jnp.where(upper, turned, roll(turned, 1, 0))


def down(a, h, upper):
    if h >= 2:
        return roll(a, -(h // 2), 0)
    turned = roll(a, 64, 1)
    return jnp.where(upper, roll(turned, -1, 0), turned)


def both(f, a, h, upper):
    return f(a[0], h, upper), f(a[1], h, upper)


def layer(ref, quantity, r):
    return ref[pl.ds(quantity * 8 + r, SLABS, stride=ROWS), :]


def source_layer(ref, r):
    return layer(ref, 0, r), layer(ref, 1, r)


def overlap_layer(ref, r):
    _, _, y = lane_ids()
    pair = ref[pl.ds(24 + r, SLABS, stride=ROWS), :]
    single = ref[pl.ds(32 + r % 4, SLABS, stride=ROWS), :]
    quantities = []
    for packed, base in ((pair, 0), (pair, 4), (single, 4 * (r // 4))):
        quantities.append(jnp.where(y >= 4, roll(packed, -2 - base, 1), roll(packed, 6 - base, 1)))
    used = (y <= 1) | (y >= 6)
    return quantities[0], quantities[1], jnp.where(used, quantities[2], 1.0)


def inside():
    chunk = lax.axis_index("slab")
    _, _, y = lane_ids()
    below = (y >= 6) & jnp.broadcast_to(chunk > 0, y.shape)
    above = (y <= 1) & jnp.broadcast_to(chunk < SLABS - 1, y.shape)
    return below | above


def put(ref, i, a):
    ref[pl.ds(2 * i * SLABS, SLABS), :] = a[0]
    ref[pl.ds((2 * i + 1) * SLABS, SLABS), :] = a[1]


def get(ref, i):
    return ref[pl.ds(2 * i * SLABS, SLABS), :], ref[pl.ds((2 * i + 1) * SLABS, SLABS), :]


N_FACTORS = 7 + 2 * STEPS + 1


def factorize(relatives, factors, overlap=False):
    upper = upper_half(overlap)
    row = lax.broadcasted_iota(jnp.int32, (SLABS, LANES), 0)
    first = row * 16 + jnp.where(upper, 8, 0)
    pivots = []
    diagonal = None
    for r in range(DEPTH):
        z = first + r
        relative = relatives[r]
        inward = jnp.maximum(jnp.maximum(PML - z, z - (NZ - 1 - PML)), 0)
        fraction = inward.astype(F32) / PML
        diagonal = (
            (2.0 + 4.0 * COUPLE) - WAVE_SHIFT * relative,
            (DAMPING * WAVE_SHIFT) * relative + ABSORB * fraction * fraction,
        )
        if r < DEPTH - 1:
            pivots.append(crecip(diagonal if r == 0 else csub(diagonal, pivots[-1])))
            put(factors, r, pivots[-1])
    to_first = pivots[0]
    first_first = pivots[0]
    for r in range(1, DEPTH - 1):
        reached = cmul(to_first, to_first)
        to_first = cmul(to_first, pivots[r])
        first_first = cadd(first_first, cmul(reached, pivots[r]))
    corner = to_first
    last_last = pivots[-1]
    low = (row == 0) & jnp.logical_not(upper)
    left = tuple(jnp.where(low, 0.0, v) for v in corner)
    high = (row == SLABS - 1) & upper
    next_first = tuple(jnp.where(high, 0.0, v) for v in both(down, first_first, 1, upper))
    d = csub(csub(diagonal, last_last), next_first)
    for step in range(STEPS):
        h = 1 << step
        right = both(down, left, h, upper)
        inverse = crecip(d)
        alpha = cmul(left, both(up, inverse, h, upper))
        gamma = cmul(right, both(down, inverse, h, upper))
        put(factors, 7 + 2 * step, alpha)
        put(factors, 8 + 2 * step, gamma)
        d = csub(csub(d, cmul(alpha, left)), cmul(gamma, right))
        left = cmul(alpha, both(up, left, h, upper))
    put(factors, 7 + 2 * STEPS, crecip(d))


def line_solve(rhs, factors, overlap=False):
    pivots = [get(factors, r) for r in range(DEPTH - 1)]
    gone = [rhs[0]]
    for r in range(1, DEPTH - 1):
        gone.append(cadd(rhs[r], cmul(pivots[r - 1], gone[-1])))
    last = cmul(pivots[-1], gone[-1])
    reach = pivots[0]
    reaches = []
    first = cmul(pivots[0], gone[0])
    for r in range(1, DEPTH - 1):
        reaches.append(reach)
        reach = cmul(reach, pivots[r])
        first = cadd(first, cmul(reach, gone[r]))
    upper = upper_half(overlap)
    row = lax.broadcasted_iota(jnp.int32, (SLABS, LANES), 0)
    high = (row == SLABS - 1) & upper
    low = (row == 0) & jnp.logical_not(upper)
    after = tuple(jnp.where(high, 0.0, v) for v in both(down, first, 1, upper))
    g = cadd(cadd(rhs[DEPTH - 1], last), after)
    for step in range(STEPS):
        h = 1 << step
        from_low = cmul(get(factors, 7 + 2 * step), both(up, g, h, upper))
        from_high = cmul(get(factors, 8 + 2 * step), both(down, g, h, upper))
        g = cadd(g, cadd(from_low, from_high))
    separator = cmul(get(factors, 7 + 2 * STEPS), g)
    before = tuple(jnp.where(low, 0.0, v) for v in both(up, separator, 1, upper))
    field = [None] * DEPTH
    field[DEPTH - 1] = separator
    for r in range(DEPTH - 2, -1, -1):
        lit = cadd(gone[r], before if r == 0 else cmul(reaches[r - 1], before))
        field[r] = cmul(pivots[r], cadd(lit, field[r + 1]))
    return field


def put_edges(main, over, edges):
    _, x, y = lane_ids()
    for edge, is_high in zip(edges, (False, True)):
        for c in range(2):
            total = None
            for r in range(DEPTH):
                moved = roll(main[r][c], 8 * (r - 7) if is_high else 8 * r, 1)
                total = moved if r == 0 else jnp.where(x == r, moved, total)
            edge[pl.ds(c * SLABS, SLABS), :] = total
        if over is None:
            continue
        below_at, above_at = (6, 0) if is_high else (7, 1)
        total = jnp.zeros((SLABS, LANES), F32)
        for c in range(2):
            for r in range(DEPTH):
                i, k = 2 * c + r // 4, r % 4
                below = (x == (below_at + i) % 8) & (y == 7 - k)
                above = (x == (above_at + i) % 8) & (y == k)
                total = jnp.where(below, roll(over[r][c], 8 * i - k, 1), total)
                total = jnp.where(above, roll(over[r][c], 8 * i + k, 1), total)
        edge[pl.ds(2 * SLABS, SLABS), :] = total


def halo(refs, place):
    tile = lax.axis_index("tile")
    rows = pl.ds(place * SLABS, SLABS)
    keep = (tile > 0, tile < TILES - 1)
    return [jnp.where(jnp.broadcast_to(k, (SLABS, LANES)), ref[rows, :], 0.0) for ref, k in zip(refs, keep)]


def transverse(main, over, halos):
    _, x, y = lane_ids()
    packed = [halo(halos, c) for c in range(2)]
    results = []
    for r in range(DEPTH):
        parts = []
        for c in range(2):
            m, e = main[r][c], over[r][c]
            low, high = packed[c]
            along_x = jnp.where(x == 0, roll(low, -8 * r, 1), roll(m, 8, 1))
            along_x += jnp.where(x == 7, roll(high, 8 * (7 - r), 1), roll(m, -8, 1))
            along_y = jnp.where(y == 0, roll(e, 1, 1), roll(m, 1, 1))
            along_y += jnp.where(y == 7, roll(e, -1, 1), roll(m, -1, 1))
            parts.append(along_x + along_y)
        results.append(parts)
    return results


def over_transverse(main, over, halos):
    _, x, y = lane_ids()
    low, high = halo(halos, 2)
    below = y >= 4
    at_low = x == jnp.where(below, 7, 1)
    at_high = x == jnp.where(below, 6, 0)
    results = []
    for r in range(DEPTH):
        parts = []
        for c in range(2):
            m, e = main[r][c], over[r][c]
            i, k = 2 * c + r // 4, r % 4
            from_low = jnp.where(below, roll(low, -56 - 8 * i + k, 1), roll(low, -56 - 8 * i - k, 1))
            from_high = jnp.where(below, roll(high, 56 - 8 * i + k, 1), roll(high, 56 - 8 * i - k, 1))
            along_x = jnp.where(at_low, from_low, roll(e, 8, 1)) + jnp.where(at_high, from_high, roll(e, -8, 1))
            along_y = jnp.where(below, roll(e, 1, 1) + roll(m, -1, 1), roll(m, 1, 1) + roll(e, -1, 1))
            parts.append(along_x + along_y)
        results.append(parts)
    return results


def relax(source, spread):
    return tuple(s + COUPLE * t for s, t in zip(source, spread))


def masked(field):
    keep = inside()
    return [tuple(jnp.where(keep, v, 0.0) for v in f) for f in field]


def put_all(ref, field):
    for r in range(DEPTH):
        put(ref, r, field[r])


def get_all(ref):
    return [get(ref, r) for r in range(DEPTH)]


def first_kernel(arrived, factors, over_factors, over_source, main_out, over_out, *edges):
    factorize([layer(arrived, 2, r) for r in range(DEPTH)], factors)
    main = line_solve([source_layer(arrived, r) for r in range(DEPTH)], factors)
    put_all(main_out, main)
    overlap = [overlap_layer(arrived, r) for r in range(DEPTH)]
    factorize([o[2] for o in overlap], over_factors, True)
    put_all(over_source, [o[:2] for o in overlap])
    over = masked(line_solve([o[:2] for o in overlap], over_factors, True))
    put_all(over_out, over)
    put_edges(main, over, edges)


def middle_kernel(arrived, factors, main_in, over_in, low, high, main_out, *edges):
    spread = transverse(get_all(main_in), get_all(over_in), (low, high))
    main = line_solve([relax(source_layer(arrived, r), spread[r]) for r in range(DEPTH)], factors)
    put_all(main_out, main)
    put_edges(main, None, edges)


def middle_over_kernel(over_factors, over_source, main_in, over_in, low, high, over_out):
    spread = over_transverse(get_all(main_in), get_all(over_in), (low, high))
    over = line_solve([relax(get(over_source, r), spread[r]) for r in range(DEPTH)], over_factors, True)
    put_all(over_out, masked(over))


def last_kernel(arrived, factors, main_in, over_in, low, high, out):
    spread = transverse(get_all(main_in), get_all(over_in), (low, high))
    field = line_solve([relax(source_layer(arrived, r), spread[r]) for r in range(DEPTH)], factors)
    for r in range(DEPTH):
        for c in range(2):
            out[pl.ds(c * 8 + r, SLABS, stride=16), :] = field[r][c]


def call(kernel, name, outs, *args, scratch=(), spec=VMEM):
    return pl.pallas_call(
        kernel,
        out_shape=[jax.ShapeDtypeStruct(s, F32) for s in outs],
        in_specs=[spec] * len(args),
        out_specs=[VMEM] * len(outs),
        scratch_shapes=list(scratch),
        compiler_params=pltpu.CompilerParams(vmem_limit_bytes=(32 if spec is VMEM else 60) << 20),
        cost_estimate=pl.CostEstimate(flops=2_000_000, bytes_accessed=1_000_000, transcendentals=0),
        name=name,
    )(*args)


FIELD = (DEPTH * 2 * SLABS, LANES)
FACTORS = (N_FACTORS * 2 * SLABS, LANES)
EDGE = (3 * SLABS, LANES)
SHORT_EDGE = (2 * SLABS, LANES)

RING_UP = [(i, (i + 1) % TILES) for i in range(TILES)]
RING_DOWN = [(b, a) for a, b in RING_UP]


def exchange(low, high):
    return lax.ppermute(high, "tile", RING_UP), lax.ppermute(low, "tile", RING_DOWN)


def local(source, labels, permittivity):
    rows = source.reshape(2 * 16 * 8, 256)
    marks = labels.reshape(16 * 8, 256)
    (packed,) = call(
        pack_kernel, "pack", [(SLABS * ROWS, LANES)], permittivity, rows, marks, spec=HBM,
        scratch=[
            pltpu.VMEM((2, 3 * LANES, LANES), F32),
            pltpu.VMEM((2, LANES, LANES), jnp.int32),
            pltpu.SMEM((8,), F32),
            pltpu.SemaphoreType.DMA((5,)),
        ],
    )
    arrived = lax.all_to_all(packed.reshape(SLABS, ROWS // 4, 4, LANES), "slab", 0, 0).reshape(SLABS * ROWS, LANES)
    factors, over_factors, over_source, main, over, *edges = call(
        first_kernel, "first", [FACTORS, FACTORS, FIELD, FIELD, FIELD, EDGE, EDGE], arrived
    )
    halos = exchange(*edges)
    next_main, *edges = call(
        middle_kernel, "middle", [FIELD, SHORT_EDGE, SHORT_EDGE], arrived, factors, main, over, *halos
    )
    next_halos = exchange(*edges)
    (over,) = call(middle_over_kernel, "middle_over", [FIELD], over_factors, over_source, main, over, *halos)
    (packed,) = call(
        last_kernel, "last", [(SLABS * 16, LANES)], arrived, factors, next_main, over, *next_halos
    )
    arrived = lax.all_to_all(packed.reshape(SLABS, 16, LANES), "slab", 0, 0).reshape(SLABS * 16, LANES)
    (out,) = call(
        unpack_kernel, "unpack", [(2 * 16 * 8, 256)], arrived, scratch=[pltpu.VMEM((2, 2 * LANES, LANES), F32)]
    )
    return out.reshape(2, 16, 8, 256)


def solution(mesh):
    placed = (P("tilt", "slab", "tile", None), P("slab", "tile", "tilt"), P("tilt"))
    return jax.shard_map(
        local,
        mesh=mesh,
        in_specs=placed,
        out_specs=P("tilt", "slab", "tile", None),
        check_vma=False,
    )
```

time: 101 us -> 91.7 us (0.908)
  starting transfers between devices: 12.5 us -> 3.38 us
  Pallas kernels: 7.93 us -> 10.8 us
  local copies, waits for them, and re-layouts: 2.51 us -> 0 us
  waiting for transfers between devices: 7.09 us -> 5.31 us
  blocking collectives: 70.3 us -> 71.8 us
    ppermute x4, starting transfers between devices: 12.5 us -> 3.38 us  [the longest x2 2.88 us: exchange(): lax.ppermute(high, 'tile', RING_UP)]
    pallas_call x5 -> x6, Pallas kernels: 7.93 us -> 10.8 us  [call(): pl.pallas_call(kernel, out_shape=[jax.ShapeDtypeStruct(s, F32) for s in o...]
    all_to_all x1, blocking collectives: 45.2 us -> 48.1 us  [local(): lax.all_to_all(packed.reshape(SLABS, ROWS // 4, 4, LANES), 'slab', 0, 0)]
    unnamed x6 -> x0, local copies, waits for them, and re-layouts: 2.51 us -> none
    ppermute x4, waiting for transfers between devices: 7.09 us -> 5.31 us  [the longest x2 4.14 us: exchange(): lax.ppermute(low, 'tile', RING_DOWN)]
    all_to_all x1, blocking collectives: 25.1 us -> 23.7 us  [local(): lax.all_to_all(packed.reshape(SLABS, 16, LANES), 'slab', 0, 0)]
  transfers between devices with their start and end apart: 4 -> 4, of which waited for: 3 -> 3; matrix products, arithmetic and copies ran while one was open for 0% -> 0% of each run, Pallas kernels for 0% -> 1%
where the time goes in v3:
time: 91.7 us; the launch traced here: 91.3 us
  blocking collectives  71.8 us (78%)
  Pallas kernels  10.8 us (12%)
  waiting for transfers between devices  5.31 us (6%)
  starting transfers between devices  3.38 us (4%)
    all_to_all x1, blocking collectives, local(): lax.all_to_all(packed.reshape(SLABS, ROWS // 4, 4, LANES), 'slab', 0, 0)  48.1 us
    all_to_all x1, blocking collectives, local(): lax.all_to_all(packed.reshape(SLABS, 16, LANES), 'slab', 0, 0)  23.7 us
    pallas_call x6, Pallas kernels, call(): pl.pallas_call(kernel, out_shape=[jax.ShapeDtypeStruct(s, F32) for s in o...  10.8 us
    ppermute x2, waiting for transfers between devices, exchange(): lax.ppermute(low, 'tile', RING_DOWN)  4.14 us
    ppermute x2, starting transfers between devices, exchange(): lax.ppermute(high, 'tile', RING_UP)  2.88 us
  transfers between devices with their start and end apart: 4, of which 3 were waited for; matrix products, arithmetic and copies ran while one was open for 0% of the time, Pallas kernels for 1%

profile of v3, /device:TPU:1, one launch (start us, length us, event | category | flops | bytes accessed | tf_op | source)
XLA Modules:
  0.0 91.3 jit_solution(6579681398657902556)
XLA Ops:
  0.0 5.1 %pack.1 = f32[1152,128]{1,0:T(8,128)} custom-call(f32[8]{0:T(128)} %table_hbm.1, f32[256,256]{1,0:T(8,128)} %bitcast.13, s32[128,256]{1,0:T(8,128)} %bitcast.14), custom_call_target="tpu_custom_call" | custom-call | flops 2000000 | bytes 1000000 | tf_op jit(solution)/shard_map/pack/pallas_call | solution.py:406
  5.1 48.1 %all_to_all.10 = f32[32,9,4,128]{3,2,1,0:T(4,128)S(1)} all-to-all(f32[32,9,4,128]{3,2,1,0:T(4,128)} %bitcast.12), channel_id=1, replica_groups=mesh['slab'=32,'tile'=8,'tilt'=2] {'slab'}, dimensions={0} | all-to-all | bytes 1179648 | tf_op jit(solution)/shard_map/all_to_all | solution.py:443
  53.2 1.4 %first.1 = (f32[1280,128]{1,0:T(8,128)S(1)}, f32[1280,128]{1,0:T(8,128)S(1)}, f32[512,128]{1,0:T(8,128)S(1)}, f32[512,128]{1,0:T(8,128)S(1)}, f32[512,128]{1,0:T...) custom-call(f32[1152,128]{1,0:T(8,128)S(1)} %bitcast.7), custom_call_target="tpu_custom_call" | custom-call | flops 2000000 | bytes 1000000 | tf_op jit(solution)/shard_map/first/pallas_call | solution.py:406
  54.6 2.9 %collective-permute-start = (f32[96,128]{1,0:T(8,128)S(1)}, f32[96,128]{1,0:T(8,128)S(1)}, u32[]{:S(2)}, u32[]{:S(2)}) collective-permute-start(f32[96,128]{1,0:T(8,128)S(1)} %get-tuple-element.18), channel_id=1, source_target_pairs={{0,2},{2,4},{4,6},{6,8},{8,10},{10,12},{12,14},{14,0},{1,3},{3,5},... | collective-permute-start | bytes 147464 | tf_op jit(solution)/shard_map/ppermute | solution.py:428
  57.5 0.0 collective-permute-start.1
  57.5 1.2 %collective-permute-done.low = f32[96,128]{1,0:T(8,128)S(1)} collective-permute-done((f32[96,128]{1,0:T(8,128)S(1)}, f32[96,128]{1,0:T(8,128)S(1)}, u32[]{:S(2)}, u32[]{:S(2)}) %collective-permute-start) | collective-permute-done | bytes 49184 | tf_op jit(solution)/shard_map/ppermute | solution.py:428
  58.7 2.3 %collective-permute-done.1.high = f32[96,128]{1,0:T(8,128)S(1)} collective-permute-done((f32[96,128]{1,0:T(8,128)S(1)}, f32[96,128]{1,0:T(8,128)S(1)}, u32[]{:S(2)}, u32[]{:S(2)}) %collective-permute-start.1) | collective-permute-done | bytes 49184 | tf_op jit(solution)/shard_map/ppermute | solution.py:428
  61.0 1.1 %middle.1 = (f32[512,128]{1,0:T(8,128)S(1)}, f32[64,128]{1,0:T(8,128)S(1)}, f32[64,128]{1,0:T(8,128)S(1)}) custom-call(f32[1152,128]{1,0:T(8,128)S(1)} %bitcast.8, f32[1280,128]{1,0:T(8,128)S(1)} %get-tuple-element.15.factors, f32[512,128]{1,0:T(8,128)S(1)} %get-tuple-element.16.main_in, f32[512,128]{1,0:T(8,128)S(1)} %get-tuple-element.17.over_in, ...), custom_call_target="tpu_custom_call" | custom-call | flops 2000000 | bytes 1000000 | tf_op jit(solution)/shard_map/middle/pallas_call | solution.py:406
  62.1 0.0 collective-permute-start.2
  62.1 0.5 collective-permute-start.3
  62.6 1.0 %middle_over.1.over_in = f32[512,128]{1,0:T(8,128)S(1)} custom-call(f32[1280,128]{1,0:T(8,128)S(1)} %get-tuple-element.21.over_factors, f32[512,128]{1,0:T(8,128)S(1)} %get-tuple-element.22.over_source, f32[512,128]{1,0:T(8,128)S(1)} %get-tuple-element.16.main_in, f32[512,128]{1,0:T(8,128)S(1)} %get-tuple-element.17.over_in, ...), custom_call_target="tpu_custom_call" | custom-call | flops 2000000 | bytes 1000000 | tf_op jit(solution)/shard_map/middle_over/pallas_call | solution.py:406
  63.7 0.0 collective-permute-done.2.low
  63.7 1.8 %collective-permute-done.3.high = f32[64,128]{1,0:T(8,128)S(1)} collective-permute-done((f32[64,128]{1,0:T(8,128)S(1)}, f32[64,128]{1,0:T(8,128)S(1)}, u32[]{:S(2)}, u32[]{:S(2)}) %collective-permute-start.3) | collective-permute-done | bytes 32800 | tf_op jit(solution)/shard_map/ppermute | solution.py:428
  65.5 0.9 %last.1 = f32[512,128]{1,0:T(8,128)S(1)} custom-call(f32[1152,128]{1,0:T(8,128)S(1)} %bitcast.9, f32[1280,128]{1,0:T(8,128)S(1)} %get-tuple-element.15.factors, f32[512,128]{1,0:T(8,128)S(1)} %get-tuple-element.20.main_in, f32[512,128]{1,0:T(8,128)S(1)} %middle_over.1.over_in, f32[64,128]{1,0:T(8,128)S(1)} %collective-permute-done.2.low, ...), custom_call_target="tpu_custom_call" | custom-call | flops 2000000 | bytes 1000000 | tf_op jit(solution)/shard_map/last/pallas_call | solution.py:406
  66.4 23.7 %all_to_all.11 = f32[32,16,128]{2,1,0:T(8,128)S(1)} all-to-all(f32[32,16,128]{2,1,0:T(8,128)S(1)} %bitcast.11), channel_id=1, replica_groups=mesh['slab'=32,'tile'=8,'tilt'=2] {'slab'}, dimensions={0} | all-to-all | bytes 524288 | tf_op jit(solution)/shard_map/all_to_all | solution.py:456
  90.1 1.2 %unpack.1 = f32[256,256]{1,0:T(8,128)} custom-call(f32[512,128]{1,0:T(8,128)S(1)} %bitcast.10), custom_call_target="tpu_custom_call" | custom-call | flops 2000000 | bytes 1000000 | tf_op jit(solution)/shard_map/unpack/pallas_call | solution.py:406
Async XLA Ops:
  54.6 4.0 %collective-permute-start = (f32[96,128]{1,0:T(8,128)S(1)}, f32[96,128]{1,0:T(8,128)S(1)}, u32[]{:S(2)}, u32[]{:S(2)}) collective-permute-start(f32[96,128]{1,0:T(8,128)S(1)} %get-tuple-element.18), channel_id=1, source_target_pairs={{0,2},{2,4},{4,6},{6,8},{8,10},{10,12},{12,14},{14,0},{1,3},{3,5},... | collective-permute-start | bytes 147464 | tf_op jit(solution)/shard_map/ppermute | solution.py:428
  57.5 3.5 %collective-permute-start.1 = (f32[96,128]{1,0:T(8,128)S(1)}, f32[96,128]{1,0:T(8,128)S(1)}, u32[]{:S(2)}, u32[]{:S(2)}) collective-permute-start(f32[96,128]{1,0:T(8,128)S(1)} %get-tuple-element.19), channel_id=1, source_target_pairs={{2,0},{4,2},{6,4},{8,6},{10,8},{12,10},{14,12},{0,14},{3,1},{5,3},... | collective-permute-start | bytes 147464 | tf_op jit(solution)/shard_map/ppermute | solution.py:428
  62.1 1.6 %collective-permute-start.2 = (f32[64,128]{1,0:T(8,128)S(1)}, f32[64,128]{1,0:T(8,128)S(1)}, u32[]{:S(2)}, u32[]{:S(2)}) collective-permute-start(f32[64,128]{1,0:T(8,128)S(1)} %get-tuple-element.23), channel_id=1, source_target_pairs={{0,2},{2,4},{4,6},{6,8},{8,10},{10,12},{12,14},{14,0},{1,3},{3,5},... | collective-permute-start | bytes 98312 | tf_op jit(solution)/shard_map/ppermute | solution.py:428
  62.1 3.4 %collective-permute-start.3 = (f32[64,128]{1,0:T(8,128)S(1)}, f32[64,128]{1,0:T(8,128)S(1)}, u32[]{:S(2)}, u32[]{:S(2)}) collective-permute-start(f32[64,128]{1,0:T(8,128)S(1)} %get-tuple-element.24), channel_id=1, source_target_pairs={{2,0},{4,2},{6,4},{8,6},{10,8},{12,10},{14,12},{0,14},{3,1},{5,3},... | collective-permute-start | bytes 98312 | tf_op jit(solution)/shard_map/ppermute | solution.py:428

commit v4 on v3

--- a/solution.py
+++ b/solution.py
@@ -54,29 +54,16 @@
     return lax.broadcasted_iota(jnp.int32, (8, LANES), 1)
 
 
-def block_transpose(parts):
-    lane = lanes8()
-    parts = list(parts)
+def block_transpose(turned):
+    block = lanes8() // 8
     for bit in (1, 2, 4, 8):
-        low = (lane & (8 * bit)) == 0
-        for i in range(16):
-            if i & bit == 0:
-                a, b = parts[i], parts[i | bit]
-                parts[i] = jnp.where(low, a, roll(b, 8 * bit, 1))
-                parts[i | bit] = jnp.where(low, roll(a, -8 * bit, 1), b)
-    return parts
-
-
-def overlap_parts(arrays, base):
-    lane = lanes8()
-    below = [roll(array, base + 2, 1) for array in arrays]
-    above = [roll(array, base - 6, 1) for array in arrays]
-    parts = []
-    for side in range(2):
-        lower = jnp.where(lane < 8, below[1 - side], below[side])
-        upper = jnp.where(lane >= 120, above[1 - side], above[side])
-        parts.append(jnp.where(lane % 8 < base + 2, lower, upper))
-    return parts
+        odd = (block & bit) != 0
+        turned = [jnp.where(odd, turned[(j + bit) % 16], turned[j]) for j in range(16)]
+    return [roll(turned[-c % 16], -8 * c, 1) for c in range(16)]
+
+
+def turn(arrays, shift=0):
+    return [roll(array, shift + 8 * i, 1) for i, array in enumerate(arrays)]
 
 
 def pack_kernel(table_hbm, source, labels, out, sides, marks, table, sems):
@@ -97,39 +84,35 @@
             rel = jnp.where(lab == m, table[m], rel)
         sides[side, pl.ds(2 * LANES, LANES), :] = rel
 
-    def load(side, quantity, half, x):
-        return sides[side, pl.ds(quantity * LANES + half * 64 + x, 8, stride=8), :]
+    def load(side, quantity):
+        places = [quantity * LANES + half * 64 + x for half in range(2) for x in range(8)]
+        return [sides[side, pl.ds(place, 8, stride=8), :] for place in places]
 
     slot = lanes8() % 8
-    places = [(half, x) for half in range(2) for x in range(8)]
-    pairs, singles = [[], []], [[], []]
-    for quantity in range(3):
-        arrays = [[load(side, quantity, half, x) for half, x in places] for side in range(2)]
-        for side in range(2):
-            for block, part in enumerate(block_transpose(arrays[side])):
+    first = slot < 4
+    pairs, singles = [], []
+    for side in range(2):
+        arrays = [load(side, quantity) for quantity in range(3)]
+        for quantity in range(3):
+            for block, part in enumerate(block_transpose(turn(arrays[quantity]))):
                 out[pl.ds((16 * side + block) * ROWS + quantity * 8, 8), :] = part
-        for i in range(16):
-            parts = overlap_parts([arrays[0][i], arrays[1][i]], 4 if quantity == 1 else 0)
-            for side in range(2):
-                if quantity == 0:
-                    pairs[side].append(parts[side])
-                elif quantity == 1:
-                    pairs[side][i] = jnp.where(slot < 4, pairs[side][i], parts[side])
-                else:
-                    upper = roll(roll(parts[side], 4, 0), 4, 1)
-                    singles[side].append(jnp.where(slot < 4, parts[side], upper))
-    for side in range(2):
-        for block, part in enumerate(block_transpose(pairs[side])):
-            out[pl.ds((16 * side + block) * ROWS + 24, 8), :] = part
-        for block, part in enumerate(block_transpose(singles[side])):
-            out[pl.ds((16 * side + block) * ROWS + 32, 4), :] = part[:4]
+        pair = [jnp.where(first, v, w) for v, w in zip(turn(arrays[0], 2), turn(arrays[1], 6))]
+        pairs += block_transpose(pair)
+        late = [roll(v, 4, 0) for v in turn(arrays[2], 6)]
+        singles += block_transpose([jnp.where(first, v, w) for v, w in zip(turn(arrays[2], 2), late)])
+    from_above = (slot & 2) != 0
+    for chunk in range(SLABS):
+        lower = (chunk + 16) % SLABS if chunk % 16 == 0 else chunk
+        upper = (chunk + 1) % SLABS
+        out[pl.ds(chunk * ROWS + 24, 8), :] = jnp.where(from_above, pairs[upper], pairs[lower])
+        out[pl.ds(chunk * ROWS + 32, 4), :] = jnp.where(from_above, singles[upper], singles[lower])[:4]
 
 
 def unpack_kernel(arrived, out, sides):
     for side in range(2):
         for c in range(2):
             parts = [arrived[pl.ds((16 * side + b) * 16 + c * 8, 8), :] for b in range(16)]
-            for i, part in enumerate(block_transpose(parts)):
+            for i, part in enumerate(block_transpose(turn(parts))):
                 half, x = divmod(i, 8)
                 sides[side, pl.ds(c * LANES + half * 64 + x, 8, stride=8), :] = part
         out[:, pl.ds(side * LANES, LANES)] = sides[side]
@@ -409,7 +392,7 @@
         in_specs=[spec] * len(args),
         out_specs=[VMEM] * len(outs),
         scratch_shapes=list(scratch),
-        compiler_params=pltpu.CompilerParams(vmem_limit_bytes=(32 if spec is VMEM else 60) << 20),
+        compiler_params=pltpu.CompilerParams(vmem_limit_bytes=32 << 20),
         cost_estimate=pl.CostEstimate(flops=2_000_000, bytes_accessed=1_000_000, transcendentals=0),
         name=name,
     )(*args)
@@ -431,8 +414,9 @@
 def local(source, labels, permittivity):
     rows = source.reshape(2 * 16 * 8, 256)
     marks = labels.reshape(16 * 8, 256)
+    inputs = [pltpu.with_memory_space_constraint(v, pltpu.HBM) for v in (permittivity, rows, marks)]
     (packed,) = call(
-        pack_kernel, "pack", [(SLABS * ROWS, LANES)], permittivity, rows, marks, spec=HBM,
+        pack_kernel, "pack", [(SLABS * ROWS, LANES)], *inputs, spec=HBM,
         scratch=[
             pltpu.VMEM((2, 3 * LANES, LANES), F32),
             pltpu.VMEM((2, LANES, LANES), jnp.int32),

time: 91.7 us -> 88.1 us (0.961)
  Pallas kernels: 10.8 us -> 7.53 us
    pallas_call x6, Pallas kernels: 10.8 us -> 7.53 us  [call(): pl.pallas_call(kernel, out_shape=[jax.ShapeDtypeStruct(s, F32) for s in o...]
where the time goes in v4:
time: 88.1 us; the launch traced here: 87.8 us
  blocking collectives  71.5 us (81%)
  Pallas kernels  7.53 us (9%)
  waiting for transfers between devices  5.31 us (6%)
  starting transfers between devices  3.38 us (4%)
    all_to_all x1, blocking collectives, local(): lax.all_to_all(packed.reshape(SLABS, ROWS // 4, 4, LANES), 'slab', 0, 0)  47.8 us
    all_to_all x1, blocking collectives, local(): lax.all_to_all(packed.reshape(SLABS, 16, LANES), 'slab', 0, 0)  23.7 us
    pallas_call x6, Pallas kernels, call(): pl.pallas_call(kernel, out_shape=[jax.ShapeDtypeStruct(s, F32) for s in o...  7.53 us
    ppermute x2, waiting for transfers between devices, exchange(): lax.ppermute(low, 'tile', RING_DOWN)  4.14 us
    ppermute x2, starting transfers between devices, exchange(): lax.ppermute(high, 'tile', RING_UP)  2.88 us
  transfers between devices with their start and end apart: 4, of which 3 were waited for; matrix products, arithmetic and copies ran while one was open for 0% of the time, Pallas kernels for 1%

profile of v4, /device:TPU:1, one launch (start us, length us, event | category | flops | bytes accessed | tf_op | source)
XLA Modules:
  0.0 87.8 jit_solution(9484733412489699765)
XLA Ops:
  0.0 2.0 %pack.1 = f32[1152,128]{1,0:T(8,128)S(1)} custom-call(f32[8]{0:T(128)} %table_hbm.1, f32[256,256]{1,0:T(8,128)} %bitcast.13, s32[128,256]{1,0:T(8,128)} %bitcast.14), custom_call_target="tpu_custom_call" | custom-call | flops 2000000 | bytes 1000000 | tf_op jit(solution)/shard_map/pack/pallas_call | solution.py:389
  2.1 47.8 %all_to_all.10 = f32[32,9,4,128]{3,2,1,0:T(4,128)S(1)} all-to-all(f32[32,9,4,128]{3,2,1,0:T(4,128)S(1)} %bitcast.10), channel_id=1, replica_groups=mesh['slab'=32,'tile'=8,'tilt'=2] {'slab'}, dimensions={0} | all-to-all | bytes 1179648 | tf_op jit(solution)/shard_map/all_to_all | solution.py:427
  49.9 1.4 %first.1 = (f32[1280,128]{1,0:T(8,128)S(1)}, f32[1280,128]{1,0:T(8,128)S(1)}, f32[512,128]{1,0:T(8,128)S(1)}, f32[512,128]{1,0:T(8,128)S(1)}, f32[512,128]{1,0:T...) custom-call(f32[1152,128]{1,0:T(8,128)S(1)} %bitcast.7), custom_call_target="tpu_custom_call" | custom-call | flops 2000000 | bytes 1000000 | tf_op jit(solution)/shard_map/first/pallas_call | solution.py:389
  51.3 2.9 %collective-permute-start = (f32[96,128]{1,0:T(8,128)S(1)}, f32[96,128]{1,0:T(8,128)S(1)}, u32[]{:S(2)}, u32[]{:S(2)}) collective-permute-start(f32[96,128]{1,0:T(8,128)S(1)} %get-tuple-element.18), channel_id=1, source_target_pairs={{0,2},{2,4},{4,6},{6,8},{8,10},{10,12},{12,14},{14,0},{1,3},{3,5},... | collective-permute-start | bytes 147464 | tf_op jit(solution)/shard_map/ppermute | solution.py:411
  54.2 0.0 collective-permute-start.1
  54.2 1.2 %collective-permute-done.low = f32[96,128]{1,0:T(8,128)S(1)} collective-permute-done((f32[96,128]{1,0:T(8,128)S(1)}, f32[96,128]{1,0:T(8,128)S(1)}, u32[]{:S(2)}, u32[]{:S(2)}) %collective-permute-start) | collective-permute-done | bytes 49184 | tf_op jit(solution)/shard_map/ppermute | solution.py:411
  55.4 2.3 %collective-permute-done.1.high = f32[96,128]{1,0:T(8,128)S(1)} collective-permute-done((f32[96,128]{1,0:T(8,128)S(1)}, f32[96,128]{1,0:T(8,128)S(1)}, u32[]{:S(2)}, u32[]{:S(2)}) %collective-permute-start.1) | collective-permute-done | bytes 49184 | tf_op jit(solution)/shard_map/ppermute | solution.py:411
  57.7 1.1 %middle.1 = (f32[512,128]{1,0:T(8,128)S(1)}, f32[64,128]{1,0:T(8,128)S(1)}, f32[64,128]{1,0:T(8,128)S(1)}) custom-call(f32[1152,128]{1,0:T(8,128)S(1)} %bitcast.8, f32[1280,128]{1,0:T(8,128)S(1)} %get-tuple-element.15.factors, f32[512,128]{1,0:T(8,128)S(1)} %get-tuple-element.16.main_in, f32[512,128]{1,0:T(8,128)S(1)} %get-tuple-element.17.over_in, ...), custom_call_target="tpu_custom_call" | custom-call | flops 2000000 | bytes 1000000 | tf_op jit(solution)/shard_map/middle/pallas_call | solution.py:389
  58.8 0.0 collective-permute-start.2
  58.8 0.5 collective-permute-start.3
  59.3 1.0 %middle_over.1.over_in = f32[512,128]{1,0:T(8,128)S(1)} custom-call(f32[1280,128]{1,0:T(8,128)S(1)} %get-tuple-element.21.over_factors, f32[512,128]{1,0:T(8,128)S(1)} %get-tuple-element.22.over_source, f32[512,128]{1,0:T(8,128)S(1)} %get-tuple-element.16.main_in, f32[512,128]{1,0:T(8,128)S(1)} %get-tuple-element.17.over_in, ...), custom_call_target="tpu_custom_call" | custom-call | flops 2000000 | bytes 1000000 | tf_op jit(solution)/shard_map/middle_over/pallas_call | solution.py:389
  60.4 0.0 collective-permute-done.2.low
  60.4 1.8 %collective-permute-done.3.high = f32[64,128]{1,0:T(8,128)S(1)} collective-permute-done((f32[64,128]{1,0:T(8,128)S(1)}, f32[64,128]{1,0:T(8,128)S(1)}, u32[]{:S(2)}, u32[]{:S(2)}) %collective-permute-start.3) | collective-permute-done | bytes 32800 | tf_op jit(solution)/shard_map/ppermute | solution.py:411
  62.2 0.9 %last.1 = f32[512,128]{1,0:T(8,128)S(1)} custom-call(f32[1152,128]{1,0:T(8,128)S(1)} %bitcast.9, f32[1280,128]{1,0:T(8,128)S(1)} %get-tuple-element.15.factors, f32[512,128]{1,0:T(8,128)S(1)} %get-tuple-element.20.main_in, f32[512,128]{1,0:T(8,128)S(1)} %middle_over.1.over_in, f32[64,128]{1,0:T(8,128)S(1)} %collective-permute-done.2.low, ...), custom_call_target="tpu_custom_call" | custom-call | flops 2000000 | bytes 1000000 | tf_op jit(solution)/shard_map/last/pallas_call | solution.py:389
  63.1 23.7 %all_to_all.11 = f32[32,16,128]{2,1,0:T(8,128)S(1)} all-to-all(f32[32,16,128]{2,1,0:T(8,128)S(1)} %bitcast.12), channel_id=1, replica_groups=mesh['slab'=32,'tile'=8,'tilt'=2] {'slab'}, dimensions={0} | all-to-all | bytes 524288 | tf_op jit(solution)/shard_map/all_to_all | solution.py:440
  86.8 1.0 %unpack.1 = f32[256,256]{1,0:T(8,128)} custom-call(f32[512,128]{1,0:T(8,128)S(1)} %bitcast.11), custom_call_target="tpu_custom_call" | custom-call | flops 2000000 | bytes 1000000 | tf_op jit(solution)/shard_map/unpack/pallas_call | solution.py:389
Async XLA Ops:
  51.3 4.0 %collective-permute-start = (f32[96,128]{1,0:T(8,128)S(1)}, f32[96,128]{1,0:T(8,128)S(1)}, u32[]{:S(2)}, u32[]{:S(2)}) collective-permute-start(f32[96,128]{1,0:T(8,128)S(1)} %get-tuple-element.18), channel_id=1, source_target_pairs={{0,2},{2,4},{4,6},{6,8},{8,10},{10,12},{12,14},{14,0},{1,3},{3,5},... | collective-permute-start | bytes 147464 | tf_op jit(solution)/shard_map/ppermute | solution.py:411
  54.2 3.5 %collective-permute-start.1 = (f32[96,128]{1,0:T(8,128)S(1)}, f32[96,128]{1,0:T(8,128)S(1)}, u32[]{:S(2)}, u32[]{:S(2)}) collective-permute-start(f32[96,128]{1,0:T(8,128)S(1)} %get-tuple-element.19), channel_id=1, source_target_pairs={{2,0},{4,2},{6,4},{8,6},{10,8},{12,10},{14,12},{0,14},{3,1},{5,3},... | collective-permute-start | bytes 147464 | tf_op jit(solution)/shard_map/ppermute | solution.py:411
  58.8 1.6 %collective-permute-start.2 = (f32[64,128]{1,0:T(8,128)S(1)}, f32[64,128]{1,0:T(8,128)S(1)}, u32[]{:S(2)}, u32[]{:S(2)}) collective-permute-start(f32[64,128]{1,0:T(8,128)S(1)} %get-tuple-element.23), channel_id=1, source_target_pairs={{0,2},{2,4},{4,6},{6,8},{8,10},{10,12},{12,14},{14,0},{1,3},{3,5},... | collective-permute-start | bytes 98312 | tf_op jit(solution)/shard_map/ppermute | solution.py:411
  58.8 3.4 %collective-permute-start.3 = (f32[64,128]{1,0:T(8,128)S(1)}, f32[64,128]{1,0:T(8,128)S(1)}, u32[]{:S(2)}, u32[]{:S(2)}) collective-permute-start(f32[64,128]{1,0:T(8,128)S(1)} %get-tuple-element.24), channel_id=1, source_target_pairs={{2,0},{4,2},{6,4},{8,6},{10,8},{12,10},{14,12},{0,14},{3,1},{5,3},... | collective-permute-start | bytes 98312 | tf_op jit(solution)/shard_map/ppermute | solution.py:411

commit v5 on v4

--- a/solution.py
+++ b/solution.py
@@ -265,17 +265,18 @@
     return field
 
 
-def put_edges(main, over, edges):
+def put_edges(main, over, source, relatives, edges):
     _, x, y = lane_ids()
     for edge, is_high in zip(edges, (False, True)):
-        for c in range(2):
+        near, far = (7, 6) if is_high else (0, 1)
+        lines = [([f[c] for f in main], line) for line in (near, far) for c in range(2)]
+        lines += [([f[c] for f in source], near) for c in range(2)] + [(relatives, near)]
+        for place, (layers, line) in enumerate(lines):
             total = None
             for r in range(DEPTH):
-                moved = roll(main[r][c], 8 * (r - 7) if is_high else 8 * r, 1)
+                moved = roll(layers[r], 8 * (r - line), 1)
                 total = moved if r == 0 else jnp.where(x == r, moved, total)
-            edge[pl.ds(c * SLABS, SLABS), :] = total
-        if over is None:
-            continue
+            edge[pl.ds(place * SLABS, SLABS), :] = total
         below_at, above_at = (6, 0) if is_high else (7, 1)
         total = jnp.zeros((SLABS, LANES), F32)
         for c in range(2):
@@ -285,61 +286,65 @@
                 above = (x == (above_at + i) % 8) & (y == k)
                 total = jnp.where(below, roll(over[r][c], 8 * i - k, 1), total)
                 total = jnp.where(above, roll(over[r][c], 8 * i + k, 1), total)
-        edge[pl.ds(2 * SLABS, SLABS), :] = total
-
-
-def halo(refs, place):
+        edge[pl.ds(7 * SLABS, SLABS), :] = total
+
+
+def within():
     tile = lax.axis_index("tile")
-    rows = pl.ds(place * SLABS, SLABS)
-    keep = (tile > 0, tile < TILES - 1)
-    return [jnp.where(jnp.broadcast_to(k, (SLABS, LANES)), ref[rows, :], 0.0) for ref, k in zip(refs, keep)]
-
-
-def transverse(main, over, halos):
+    _, x, _ = lane_ids()
+    low = (x < 4) & jnp.broadcast_to(tile > 0, x.shape)
+    high = (x >= 4) & jnp.broadcast_to(tile < TILES - 1, x.shape)
+    return low | high
+
+
+def beside(halos, place, r):
+    _, x, _ = lane_ids()
+    low, high = (ref[pl.ds(place * SLABS, SLABS), :] for ref in halos)
+    return jnp.where(x < 4, roll(low, -8 * r, 1), roll(high, 8 * (7 - r), 1))
+
+
+def over_beside(halos, c, r):
+    tile = lax.axis_index("tile")
     _, x, y = lane_ids()
-    packed = [halo(halos, c) for c in range(2)]
-    results = []
-    for r in range(DEPTH):
-        parts = []
-        for c in range(2):
-            m, e = main[r][c], over[r][c]
-            low, high = packed[c]
-            along_x = jnp.where(x == 0, roll(low, -8 * r, 1), roll(m, 8, 1))
-            along_x += jnp.where(x == 7, roll(high, 8 * (7 - r), 1), roll(m, -8, 1))
-            along_y = jnp.where(y == 0, roll(e, 1, 1), roll(m, 1, 1))
-            along_y += jnp.where(y == 7, roll(e, -1, 1), roll(m, -1, 1))
-            parts.append(along_x + along_y)
-        results.append(parts)
-    return results
-
-
-def over_transverse(main, over, halos):
+    low, high = (ref[pl.ds(7 * SLABS, SLABS), :] for ref in halos)
+    low = jnp.where(jnp.broadcast_to(tile > 0, x.shape), low, 0.0)
+    high = jnp.where(jnp.broadcast_to(tile < TILES - 1, x.shape), high, 0.0)
+    below = y >= 4
+    i, k = 2 * c + r // 4, r % 4
+    from_low = jnp.where(below, roll(low, -56 - 8 * i + k, 1), roll(low, -56 - 8 * i - k, 1))
+    from_high = jnp.where(below, roll(high, 56 - 8 * i + k, 1), roll(high, 56 - 8 * i - k, 1))
+    return jnp.where(x == jnp.where(below, 7, 1), from_low, from_high)
+
+
+def sum_y(field, over):
+    _, _, y = lane_ids()
+    lower = jnp.where(y == 0, roll(over, 1, 1), roll(field, 1, 1))
+    return lower + jnp.where(y == 7, roll(over, -1, 1), roll(field, -1, 1))
+
+
+def sum_main(main, over, near):
+    _, x, _ = lane_ids()
+    along_x = jnp.where(x == 0, near, roll(main, 8, 1)) + jnp.where(x == 7, near, roll(main, -8, 1))
+    return along_x + sum_y(main, over)
+
+
+def sum_over(main, over, over_near):
     _, x, y = lane_ids()
-    low, high = halo(halos, 2)
     below = y >= 4
-    at_low = x == jnp.where(below, 7, 1)
-    at_high = x == jnp.where(below, 6, 0)
-    results = []
-    for r in range(DEPTH):
-        parts = []
-        for c in range(2):
-            m, e = main[r][c], over[r][c]
-            i, k = 2 * c + r // 4, r % 4
-            from_low = jnp.where(below, roll(low, -56 - 8 * i + k, 1), roll(low, -56 - 8 * i - k, 1))
-            from_high = jnp.where(below, roll(high, 56 - 8 * i + k, 1), roll(high, 56 - 8 * i - k, 1))
-            along_x = jnp.where(at_low, from_low, roll(e, 8, 1)) + jnp.where(at_high, from_high, roll(e, -8, 1))
-            along_y = jnp.where(below, roll(e, 1, 1) + roll(m, -1, 1), roll(m, 1, 1) + roll(e, -1, 1))
-            parts.append(along_x + along_y)
-        results.append(parts)
-    return results
+    along_x = jnp.where(x == jnp.where(below, 7, 1), over_near, roll(over, 8, 1))
+    along_x += jnp.where(x == jnp.where(below, 6, 0), over_near, roll(over, -8, 1))
+    return along_x + jnp.where(below, roll(over, 1, 1) + roll(main, -1, 1), roll(main, 1, 1) + roll(over, -1, 1))
+
+
+def sum_near(main, near, far, over_near):
+    return far + main + sum_y(near, over_near)
 
 
 def relax(source, spread):
     return tuple(s + COUPLE * t for s, t in zip(source, spread))
 
 
-def masked(field):
-    keep = inside()
+def masked(field, keep):
     return [tuple(jnp.where(keep, v, 0.0) for v in f) for f in field]
 
 
@@ -353,33 +358,48 @@
 
 
 def first_kernel(arrived, factors, over_factors, over_source, main_out, over_out, *edges):
-    factorize([layer(arrived, 2, r) for r in range(DEPTH)], factors)
-    main = line_solve([source_layer(arrived, r) for r in range(DEPTH)], factors)
+    relatives = [layer(arrived, 2, r) for r in range(DEPTH)]
+    source = [source_layer(arrived, r) for r in range(DEPTH)]
+    factorize(relatives, factors)
+    main = line_solve(source, factors)
     put_all(main_out, main)
     overlap = [overlap_layer(arrived, r) for r in range(DEPTH)]
     factorize([o[2] for o in overlap], over_factors, True)
     put_all(over_source, [o[:2] for o in overlap])
-    over = masked(line_solve([o[:2] for o in overlap], over_factors, True))
+    over = masked(line_solve([o[:2] for o in overlap], over_factors, True), inside())
     put_all(over_out, over)
-    put_edges(main, over, edges)
-
-
-def middle_kernel(arrived, factors, main_in, over_in, low, high, main_out, *edges):
-    spread = transverse(get_all(main_in), get_all(over_in), (low, high))
-    main = line_solve([relax(source_layer(arrived, r), spread[r]) for r in range(DEPTH)], factors)
-    put_all(main_out, main)
-    put_edges(main, None, edges)
-
-
-def middle_over_kernel(over_factors, over_source, main_in, over_in, low, high, over_out):
-    spread = over_transverse(get_all(main_in), get_all(over_in), (low, high))
-    over = line_solve([relax(get(over_source, r), spread[r]) for r in range(DEPTH)], over_factors, True)
-    put_all(over_out, masked(over))
-
-
-def last_kernel(arrived, factors, main_in, over_in, low, high, out):
-    spread = transverse(get_all(main_in), get_all(over_in), (low, high))
-    field = line_solve([relax(source_layer(arrived, r), spread[r]) for r in range(DEPTH)], factors)
+    put_edges(main, over, source, relatives, edges)
+
+
+def last_kernel(
+    arrived, factors, over_factors, over_source, main_in, over_in, low, high, out, near_factors, main_mid, over_mid, near_mid
+):
+    halos = (low, high)
+    keep = within()
+    factorize([beside(halos, 6, r) for r in range(DEPTH)], near_factors)
+    main_rhs, over_rhs, near_rhs = [], [], []
+    for r in range(DEPTH):
+        main_sums, over_sums, near_sums = [], [], []
+        for c in range(2):
+            rows = pl.ds((2 * r + c) * SLABS, SLABS)
+            main, over = main_in[rows, :], over_in[rows, :]
+            near = jnp.where(keep, beside(halos, c, r), 0.0)
+            far = beside(halos, 2 + c, r)
+            over_near = over_beside(halos, c, r)
+            main_sums.append(sum_main(main, over, near))
+            over_sums.append(sum_over(main, over, over_near))
+            near_sums.append(sum_near(main, near, far, over_near))
+        main_rhs.append(relax(source_layer(arrived, r), main_sums))
+        over_rhs.append(relax(get(over_source, r), over_sums))
+        near_rhs.append(relax((beside(halos, 4, r), beside(halos, 5, r)), near_sums))
+    put_all(main_mid, line_solve(main_rhs, factors))
+    put_all(over_mid, masked(line_solve(over_rhs, over_factors, True), inside()))
+    put_all(near_mid, masked(line_solve(near_rhs, near_factors), keep))
+    rhs = []
+    for r in range(DEPTH):
+        parts = zip(get(main_mid, r), get(over_mid, r), get(near_mid, r))
+        rhs.append(relax(source_layer(arrived, r), [sum_main(*part) for part in parts]))
+    field = line_solve(rhs, factors)
     for r in range(DEPTH):
         for c in range(2):
             out[pl.ds(c * 8 + r, SLABS, stride=16), :] = field[r][c]
@@ -400,8 +420,7 @@
 
 FIELD = (DEPTH * 2 * SLABS, LANES)
 FACTORS = (N_FACTORS * 2 * SLABS, LANES)
-EDGE = (3 * SLABS, LANES)
-SHORT_EDGE = (2 * SLABS, LANES)
+EDGE = (8 * SLABS, LANES)
 
 RING_UP = [(i, (i + 1) % TILES) for i in range(TILES)]
 RING_DOWN = [(b, a) for a, b in RING_UP]
@@ -429,13 +448,9 @@
         first_kernel, "first", [FACTORS, FACTORS, FIELD, FIELD, FIELD, EDGE, EDGE], arrived
     )
     halos = exchange(*edges)
-    next_main, *edges = call(
-        middle_kernel, "middle", [FIELD, SHORT_EDGE, SHORT_EDGE], arrived, factors, main, over, *halos
-    )
-    next_halos = exchange(*edges)
-    (over,) = call(middle_over_kernel, "middle_over", [FIELD], over_factors, over_source, main, over, *halos)
     (packed,) = call(
-        last_kernel, "last", [(SLABS * 16, LANES)], arrived, factors, next_main, over, *next_halos
+        last_kernel, "last", [(SLABS * 16, LANES)], arrived, factors, over_factors, over_source, main, over, *halos,
+        scratch=[pltpu.VMEM(FACTORS, F32)] + [pltpu.VMEM(FIELD, F32)] * 3,
     )
     arrived = lax.all_to_all(packed.reshape(SLABS, 16, LANES), "slab", 0, 0).reshape(SLABS * 16, LANES)
     (out,) = call(

time: 88.1 us -> 87.6 us (level)
  waiting for transfers between devices: 5.31 us -> 4.39 us
    ppermute x2 -> x1, waiting for transfers between devices: 4.14 us -> 2.44 us  [exchange(): lax.ppermute(low, 'tile', RING_DOWN)]
    pallas_call x6 -> x4, Pallas kernels: 7.53 us -> 8.39 us  [call(): pl.pallas_call(kernel, out_shape=[jax.ShapeDtypeStruct(s, F32) for s in o...]
    ppermute x2 -> x1, waiting for transfers between devices: 1.18 us -> 1.94 us  [exchange(): lax.ppermute(high, 'tile', RING_UP)]
    ppermute x2 -> x1, starting transfers between devices: 2.88 us -> 2.86 us  [exchange(): lax.ppermute(high, 'tile', RING_UP)]
  transfers between devices with their start and end apart: 4 -> 2, of which waited for: 3 -> 2; matrix products, arithmetic and copies ran while one was open for 0% -> 0% of each run, Pallas kernels for 1% -> 0%
where the time goes in v5:
time: 87.6 us; the launch traced here: 87.4 us
  blocking collectives  71.7 us (82%)
  Pallas kernels  8.39 us (10%)
  waiting for transfers between devices  4.39 us (5%)
  starting transfers between devices  2.86 us (3%)
    all_to_all x1, blocking collectives, local(): lax.all_to_all(packed.reshape(SLABS, ROWS // 4, 4, LANES), 'slab', 0, 0)  47.8 us
    all_to_all x1, blocking collectives, local(): lax.all_to_all(packed.reshape(SLABS, 16, LANES), 'slab', 0, 0)  23.9 us
    pallas_call x4, Pallas kernels, call(): pl.pallas_call(kernel, out_shape=[jax.ShapeDtypeStruct(s, F32) for s in o...  8.39 us
    ppermute x1, starting transfers between devices, exchange(): lax.ppermute(high, 'tile', RING_UP)  2.86 us
    ppermute x1, waiting for transfers between devices, exchange(): lax.ppermute(low, 'tile', RING_DOWN)  2.44 us
    ppermute x1, waiting for transfers between devices, exchange(): lax.ppermute(high, 'tile', RING_UP)  1.94 us
  transfers between devices with their start and end apart: 2, of which 2 were waited for; matrix products, arithmetic and copies ran while one was open for 0% of the time, Pallas kernels for 0%

profile of v5, /device:TPU:1, one launch (start us, length us, event | category | flops | bytes accessed | tf_op | source)
XLA Modules:
  0.0 87.4 jit_solution(11662848970183867079)
XLA Ops:
  0.0 2.0 %pack.1 = f32[1152,128]{1,0:T(8,128)S(1)} custom-call(f32[8]{0:T(128)} %table_hbm.1, f32[256,256]{1,0:T(8,128)} %bitcast.12, s32[128,256]{1,0:T(8,128)} %bitcast.13), custom_call_target="tpu_custom_call" | custom-call | flops 2000000 | bytes 1000000 | tf_op jit(solution)/shard_map/pack/pallas_call | solution.py:409
  2.1 47.8 %all_to_all.10 = f32[32,9,4,128]{3,2,1,0:T(4,128)S(1)} all-to-all(f32[32,9,4,128]{3,2,1,0:T(4,128)S(1)} %bitcast.9), channel_id=1, replica_groups=mesh['slab'=32,'tile'=8,'tilt'=2] {'slab'}, dimensions={0} | all-to-all | bytes 1179648 | tf_op jit(solution)/shard_map/all_to_all | solution.py:446
  49.9 1.7 %first.1 = (f32[1280,128]{1,0:T(8,128)S(1)}, f32[1280,128]{1,0:T(8,128)S(1)}, f32[512,128]{1,0:T(8,128)S(1)}, f32[512,128]{1,0:T(8,128)S(1)}, f32[512,128]{1,0:T...) custom-call(f32[1152,128]{1,0:T(8,128)S(1)} %bitcast.7), custom_call_target="tpu_custom_call" | custom-call | flops 2000000 | bytes 1000000 | tf_op jit(solution)/shard_map/first/pallas_call | solution.py:409
  51.6 2.9 %collective-permute-start = (f32[256,128]{1,0:T(8,128)S(1)}, f32[256,128]{1,0:T(8,128)S(1)}, u32[]{:S(2)}, u32[]{:S(2)}) collective-permute-start(f32[256,128]{1,0:T(8,128)S(1)} %get-tuple-element.17), channel_id=1, source_target_pairs={{0,2},{2,4},{4,6},{6,8},{8,10},{10,12},{12,14},{14,0},{1,3},{3,5},... | collective-permute-start | bytes 393224 | tf_op jit(solution)/shard_map/ppermute | solution.py:430
  54.5 0.0 collective-permute-start.1
  54.5 1.9 %collective-permute-done.low = f32[256,128]{1,0:T(8,128)S(1)} collective-permute-done((f32[256,128]{1,0:T(8,128)S(1)}, f32[256,128]{1,0:T(8,128)S(1)}, u32[]{:S(2)}, u32[]{:S(2)}) %collective-permute-start) | collective-permute-done | bytes 131104 | tf_op jit(solution)/shard_map/ppermute | solution.py:430
  56.5 2.4 %collective-permute-done.1.high = f32[256,128]{1,0:T(8,128)S(1)} collective-permute-done((f32[256,128]{1,0:T(8,128)S(1)}, f32[256,128]{1,0:T(8,128)S(1)}, u32[]{:S(2)}, u32[]{:S(2)}) %collective-permute-start.1) | collective-permute-done | bytes 131104 | tf_op jit(solution)/shard_map/ppermute | solution.py:430
  58.9 3.6 %last.1 = f32[512,128]{1,0:T(8,128)S(1)} custom-call(f32[1152,128]{1,0:T(8,128)S(1)} %bitcast.8, f32[1280,128]{1,0:T(8,128)S(1)} %get-tuple-element.12.factors, f32[1280,128]{1,0:T(8,128)S(1)} %get-tuple-element.13.over_factors, f32[512,128]{1,0:T(8,128)S(1)} %get-tuple-element.14.over_source, f32[512,128]{1,0:T(8,128)S(1)} %get-tuple-element.15.main_in, ...), custom_call_target="tpu_custom_call" | custom-call | flops 2000000 | bytes 1000000 | tf_op jit(solution)/shard_map/last/pallas_call | solution.py:409
  62.5 23.9 %all_to_all.11 = f32[32,16,128]{2,1,0:T(8,128)S(1)} all-to-all(f32[32,16,128]{2,1,0:T(8,128)S(1)} %bitcast.10), channel_id=1, replica_groups=mesh['slab'=32,'tile'=8,'tilt'=2] {'slab'}, dimensions={0} | all-to-all | bytes 524288 | tf_op jit(solution)/shard_map/all_to_all | solution.py:455
  86.4 1.0 %unpack.1 = f32[256,256]{1,0:T(8,128)} custom-call(f32[512,128]{1,0:T(8,128)S(1)} %bitcast.11), custom_call_target="tpu_custom_call" | custom-call | flops 2000000 | bytes 1000000 | tf_op jit(solution)/shard_map/unpack/pallas_call | solution.py:409
Async XLA Ops:
  51.6 4.8 %collective-permute-start = (f32[256,128]{1,0:T(8,128)S(1)}, f32[256,128]{1,0:T(8,128)S(1)}, u32[]{:S(2)}, u32[]{:S(2)}) collective-permute-start(f32[256,128]{1,0:T(8,128)S(1)} %get-tuple-element.17), channel_id=1, source_target_pairs={{0,2},{2,4},{4,6},{6,8},{8,10},{10,12},{12,14},{14,0},{1,3},{3,5},... | collective-permute-start | bytes 393224 | tf_op jit(solution)/shard_map/ppermute | solution.py:430
  54.5 4.4 %collective-permute-start.1 = (f32[256,128]{1,0:T(8,128)S(1)}, f32[256,128]{1,0:T(8,128)S(1)}, u32[]{:S(2)}, u32[]{:S(2)}) collective-permute-start(f32[256,128]{1,0:T(8,128)S(1)} %get-tuple-element.18), channel_id=1, source_target_pairs={{2,0},{4,2},{6,4},{8,6},{10,8},{12,10},{14,12},{0,14},{3,1},{5,3},... | collective-permute-start | bytes 393224 | tf_op jit(solution)/shard_map/ppermute | solution.py:430

commit v6 on v5

--- a/solution.py
+++ b/solution.py
@@ -265,28 +265,41 @@
     return field
 
 
-def put_edges(main, over, source, relatives, edges):
-    _, x, y = lane_ids()
+def put_edges(main, source, relatives, edges):
+    _, x, _ = lane_ids()
     for edge, is_high in zip(edges, (False, True)):
+        place_to = 0 if is_high else 7
         near, far = (7, 6) if is_high else (0, 1)
         lines = [([f[c] for f in main], line) for line in (near, far) for c in range(2)]
         lines += [([f[c] for f in source], near) for c in range(2)] + [(relatives, near)]
         for place, (layers, line) in enumerate(lines):
             total = None
             for r in range(DEPTH):
-                moved = roll(layers[r], 8 * (r - line), 1)
-                total = moved if r == 0 else jnp.where(x == r, moved, total)
+                moved = roll(layers[r], 8 * (place_to - line + r), 1)
+                total = moved if r == 0 else jnp.where(x == (place_to + r) % 8, moved, total)
             edge[pl.ds(place * SLABS, SLABS), :] = total
-        below_at, above_at = (6, 0) if is_high else (7, 1)
+
+
+def over_place(c, r):
+    n = 8 * c + r
+    return n if n < 9 else n + 9
+
+
+def over_lanes(base, c, r):
+    lane = lax.broadcasted_iota(jnp.int32, (SLABS, LANES), 1) % 64
+    first = base + over_place(c, r)
+    return (lane == (first - 1) % 64) | (lane == (first + 8) % 64)
+
+
+def put_over_edges(over, edges):
+    for edge, is_high in zip(edges, (False, True)):
+        turned, base = (-56, 0) if is_high else (56, 56)
         total = jnp.zeros((SLABS, LANES), F32)
         for c in range(2):
             for r in range(DEPTH):
-                i, k = 2 * c + r // 4, r % 4
-                below = (x == (below_at + i) % 8) & (y == 7 - k)
-                above = (x == (above_at + i) % 8) & (y == k)
-                total = jnp.where(below, roll(over[r][c], 8 * i - k, 1), total)
-                total = jnp.where(above, roll(over[r][c], 8 * i + k, 1), total)
-        edge[pl.ds(7 * SLABS, SLABS), :] = total
+                moved = roll(over[r][c], turned + over_place(c, r), 1)
+                total = jnp.where(over_lanes(base, c, r), moved, total)
+        edge[...] = total
 
 
 def within():
@@ -300,26 +313,16 @@
 def beside(halos, place, r):
     _, x, _ = lane_ids()
     low, high = (ref[pl.ds(place * SLABS, SLABS), :] for ref in halos)
-    return jnp.where(x < 4, roll(low, -8 * r, 1), roll(high, 8 * (7 - r), 1))
-
-
-def over_beside(halos, c, r):
-    tile = lax.axis_index("tile")
-    _, x, y = lane_ids()
-    low, high = (ref[pl.ds(7 * SLABS, SLABS), :] for ref in halos)
-    low = jnp.where(jnp.broadcast_to(tile > 0, x.shape), low, 0.0)
-    high = jnp.where(jnp.broadcast_to(tile < TILES - 1, x.shape), high, 0.0)
-    below = y >= 4
-    i, k = 2 * c + r // 4, r % 4
-    from_low = jnp.where(below, roll(low, -56 - 8 * i + k, 1), roll(low, -56 - 8 * i - k, 1))
-    from_high = jnp.where(below, roll(high, 56 - 8 * i + k, 1), roll(high, 56 - 8 * i - k, 1))
-    return jnp.where(x == jnp.where(below, 7, 1), from_low, from_high)
+    return roll(jnp.where(x == r, low, high), -8 * r, 1)
+
+
+def over_beside(low, high, c, r):
+    return roll(jnp.where(over_lanes(0, c, r), low, high), -over_place(c, r), 1)
 
 
 def sum_y(field, over):
     _, _, y = lane_ids()
-    lower = jnp.where(y == 0, roll(over, 1, 1), roll(field, 1, 1))
-    return lower + jnp.where(y == 7, roll(over, -1, 1), roll(field, -1, 1))
+    return roll(jnp.where(y == 7, over, field), 1, 1) + roll(jnp.where(y == 0, over, field), -1, 1)
 
 
 def sum_main(main, over, near):
@@ -328,16 +331,16 @@
     return along_x + sum_y(main, over)
 
 
-def sum_over(main, over, over_near):
+def over_edge():
     _, x, y = lane_ids()
     below = y >= 4
-    along_x = jnp.where(x == jnp.where(below, 7, 1), over_near, roll(over, 8, 1))
-    along_x += jnp.where(x == jnp.where(below, 6, 0), over_near, roll(over, -8, 1))
-    return along_x + jnp.where(below, roll(over, 1, 1) + roll(main, -1, 1), roll(main, 1, 1) + roll(over, -1, 1))
-
-
-def sum_near(main, near, far, over_near):
-    return far + main + sum_y(near, over_near)
+    return x == jnp.where(below, 7, 1), x == jnp.where(below, 6, 0)
+
+
+def sum_over(main, over):
+    at_low, at_high = over_edge()
+    along_x = jnp.where(at_low, 0.0, roll(over, 8, 1)) + jnp.where(at_high, 0.0, roll(over, -8, 1))
+    return along_x + sum_y(over, main)
 
 
 def relax(source, spread):
@@ -357,40 +360,52 @@
     return [get(ref, r) for r in range(DEPTH)]
 
 
-def first_kernel(arrived, factors, over_factors, over_source, main_out, over_out, *edges):
+def first_kernel(arrived, factors, main_out, *edges):
     relatives = [layer(arrived, 2, r) for r in range(DEPTH)]
     source = [source_layer(arrived, r) for r in range(DEPTH)]
     factorize(relatives, factors)
     main = line_solve(source, factors)
     put_all(main_out, main)
+    put_edges(main, source, relatives, edges)
+
+
+def over_kernel(arrived, main_in, over_factors, main_part, over_part, *edges):
     overlap = [overlap_layer(arrived, r) for r in range(DEPTH)]
     factorize([o[2] for o in overlap], over_factors, True)
-    put_all(over_source, [o[:2] for o in overlap])
     over = masked(line_solve([o[:2] for o in overlap], over_factors, True), inside())
-    put_all(over_out, over)
-    put_edges(main, over, source, relatives, edges)
+    put_over_edges(over, edges)
+    for r in range(DEPTH):
+        main = get(main_in, r)
+        put(main_part, r, relax(source_layer(arrived, r), [sum_main(m, e, 0.0) for m, e in zip(main, over[r])]))
+        put(over_part, r, relax(overlap[r][:2], [sum_over(m, e) for m, e in zip(main, over[r])]))
 
 
 def last_kernel(
-    arrived, factors, over_factors, over_source, main_in, over_in, low, high, out, near_factors, main_mid, over_mid, near_mid
+    arrived, factors, over_factors, main_in, main_part, over_part, low, high, over_low, over_high,
+    out, near_factors, main_mid, over_mid, near_mid,
 ):
     halos = (low, high)
     keep = within()
+    _, x, _ = lane_ids()
+    outermost = (x == 0) | (x == 7)
+    at_low, at_high = over_edge()
+    over_outermost = at_low | at_high
+    tile = lax.axis_index("tile")
+    cells_low = jnp.where(jnp.broadcast_to(tile > 0, x.shape), over_low[...], 0.0)
+    cells_high = jnp.where(jnp.broadcast_to(tile < TILES - 1, x.shape), over_high[...], 0.0)
     factorize([beside(halos, 6, r) for r in range(DEPTH)], near_factors)
     main_rhs, over_rhs, near_rhs = [], [], []
     for r in range(DEPTH):
-        main_sums, over_sums, near_sums = [], [], []
+        main_adds, over_adds, near_sums = [], [], []
         for c in range(2):
-            rows = pl.ds((2 * r + c) * SLABS, SLABS)
-            main, over = main_in[rows, :], over_in[rows, :]
             near = jnp.where(keep, beside(halos, c, r), 0.0)
-            far = beside(halos, 2 + c, r)
-            over_near = over_beside(halos, c, r)
-            main_sums.append(sum_main(main, over, near))
-            over_sums.append(sum_over(main, over, over_near))
-            near_sums.append(sum_near(main, near, far, over_near))
-        main_rhs.append(relax(source_layer(arrived, r), main_sums))
-        over_rhs.append(relax(get(over_source, r), over_sums))
+            cells = over_beside(cells_low, cells_high, c, r)
+            main_adds.append(jnp.where(outermost, near, 0.0))
+            over_adds.append(jnp.where(over_outermost, cells, 0.0))
+            main = main_in[pl.ds((2 * r + c) * SLABS, SLABS), :]
+            near_sums.append(beside(halos, 2 + c, r) + main + sum_y(near, cells))
+        main_rhs.append(relax(get(main_part, r), main_adds))
+        over_rhs.append(relax(get(over_part, r), over_adds))
         near_rhs.append(relax((beside(halos, 4, r), beside(halos, 5, r)), near_sums))
     put_all(main_mid, line_solve(main_rhs, factors))
     put_all(over_mid, masked(line_solve(over_rhs, over_factors, True), inside()))
@@ -420,7 +435,8 @@
 
 FIELD = (DEPTH * 2 * SLABS, LANES)
 FACTORS = (N_FACTORS * 2 * SLABS, LANES)
-EDGE = (8 * SLABS, LANES)
+EDGE = (7 * SLABS, LANES)
+OVER_EDGE = (SLABS, LANES)
 
 RING_UP = [(i, (i + 1) % TILES) for i in range(TILES)]
 RING_DOWN = [(b, a) for a, b in RING_UP]
@@ -444,12 +460,15 @@
         ],
     )
     arrived = lax.all_to_all(packed.reshape(SLABS, ROWS // 4, 4, LANES), "slab", 0, 0).reshape(SLABS * ROWS, LANES)
-    factors, over_factors, over_source, main, over, *edges = call(
-        first_kernel, "first", [FACTORS, FACTORS, FIELD, FIELD, FIELD, EDGE, EDGE], arrived
+    factors, main, *edges = call(first_kernel, "first", [FACTORS, FIELD, EDGE, EDGE], arrived)
+    halos = exchange(*edges)
+    over_factors, main_part, over_part, *edges = call(
+        over_kernel, "over", [FACTORS, FIELD, FIELD, OVER_EDGE, OVER_EDGE], arrived, main
     )
-    halos = exchange(*edges)
+    over_halos = exchange(*edges)
     (packed,) = call(
-        last_kernel, "last", [(SLABS * 16, LANES)], arrived, factors, over_factors, over_source, main, over, *halos,
+        last_kernel, "last", [(SLABS * 16, LANES)],
+        arrived, factors, over_factors, main, main_part, over_part, *halos, *over_halos,
         scratch=[pltpu.VMEM(FACTORS, F32)] + [pltpu.VMEM(FIELD, F32)] * 3,
     )
     arrived = lax.all_to_all(packed.reshape(SLABS, 16, LANES), "slab", 0, 0).reshape(SLABS * 16, LANES)

time: 87.6 us -> 87.7 us (level)
  starting transfers between devices: 2.86 us -> 4.75 us
  waiting for transfers between devices: 4.39 us -> 3.03 us
    ppermute x1 -> x2, starting transfers between devices: 2.86 us -> 4.61 us  [exchange(): lax.ppermute(high, 'tile', RING_UP)]
    ppermute x1 -> x2, waiting for transfers between devices: 1.94 us -> 0.73 us  [exchange(): lax.ppermute(high, 'tile', RING_UP)]
    pallas_call x4 -> x5, Pallas kernels: 8.39 us -> 7.98 us  [call(): pl.pallas_call(kernel, out_shape=[jax.ShapeDtypeStruct(s, F32) for s in o...]
    ppermute x1 -> x2, waiting for transfers between devices: 2.44 us -> 2.3 us  [exchange(): lax.ppermute(low, 'tile', RING_DOWN)]
  transfers between devices with their start and end apart: 2 -> 4, of which waited for: 2 -> 2; matrix products, arithmetic and copies ran while one was open for 0% -> 0% of each run, Pallas kernels for 0% -> 2%
where the time goes in v6:
time: 87.7 us; the launch traced here: 87.3 us
  blocking collectives  71.5 us (82%)
  Pallas kernels  7.98 us (9%)
  starting transfers between devices  4.75 us (5%)
  waiting for transfers between devices  3.03 us (3%)
    all_to_all x1, blocking collectives, local(): lax.all_to_all(packed.reshape(SLABS, ROWS // 4, 4, LANES), 'slab', 0, 0)  47.8 us
    all_to_all x1, blocking collectives, local(): lax.all_to_all(packed.reshape(SLABS, 16, LANES), 'slab', 0, 0)  23.7 us
    pallas_call x5, Pallas kernels, call(): pl.pallas_call(kernel, out_shape=[jax.ShapeDtypeStruct(s, F32) for s in o...  7.98 us
    ppermute x2, starting transfers between devices, exchange(): lax.ppermute(high, 'tile', RING_UP)  4.61 us
    ppermute x2, waiting for transfers between devices, exchange(): lax.ppermute(low, 'tile', RING_DOWN)  2.3 us
  transfers between devices with their start and end apart: 4, of which 2 were waited for; matrix products, arithmetic and copies ran while one was open for 0% of the time, Pallas kernels for 2%

profile of v6, /device:TPU:1, one launch (start us, length us, event | category | flops | bytes accessed | tf_op | source)
XLA Modules:
  0.0 87.3 jit_solution(11870815488637176323)
XLA Ops:
  0.0 2.0 %pack.1 = f32[1152,128]{1,0:T(8,128)S(1)} custom-call(f32[8]{0:T(128)} %table_hbm.1, f32[256,256]{1,0:T(8,128)} %bitcast.13, s32[128,256]{1,0:T(8,128)} %bitcast.14), custom_call_target="tpu_custom_call" | custom-call | flops 2000000 | bytes 1000000 | tf_op jit(solution)/shard_map/pack/pallas_call | solution.py:424
  2.1 47.8 %all_to_all.10 = f32[32,9,4,128]{3,2,1,0:T(4,128)S(1)} all-to-all(f32[32,9,4,128]{3,2,1,0:T(4,128)S(1)} %bitcast.10), channel_id=1, replica_groups=mesh['slab'=32,'tile'=8,'tilt'=2] {'slab'}, dimensions={0} | all-to-all | bytes 1179648 | tf_op jit(solution)/shard_map/all_to_all | solution.py:462
  49.9 1.1 %first.1 = (f32[1280,128]{1,0:T(8,128)S(1)}, f32[512,128]{1,0:T(8,128)S(1)}, f32[224,128]{1,0:T(8,128)S(1)}, f32[224,128]{1,0:T(8,128)S(1)}) custom-call(f32[1152,128]{1,0:T(8,128)S(1)} %bitcast.7), custom_call_target="tpu_custom_call" | custom-call | flops 2000000 | bytes 1000000 | tf_op jit(solution)/shard_map/first/pallas_call | solution.py:424
  51.0 2.9 %collective-permute-start = (f32[224,128]{1,0:T(8,128)S(1)}, f32[224,128]{1,0:T(8,128)S(1)}, u32[]{:S(2)}, u32[]{:S(2)}) collective-permute-start(f32[224,128]{1,0:T(8,128)S(1)} %get-tuple-element.19), channel_id=1, source_target_pairs={{0,2},{2,4},{4,6},{6,8},{8,10},{10,12},{12,14},{14,0},{1,3},{3,5},... | collective-permute-start | bytes 344072 | tf_op jit(solution)/shard_map/ppermute | solution.py:446
  53.8 0.0 collective-permute-start.1
  53.8 1.5 %over.1 = (f32[1280,128]{1,0:T(8,128)S(1)}, f32[512,128]{1,0:T(8,128)S(1)}, f32[512,128]{1,0:T(8,128)S(1)}, f32[32,128]{1,0:T(8,128)S(1)}, f32[32,128]{1,0:T(8,128)S(1)}) custom-call(f32[1152,128]{1,0:T(8,128)S(1)} %bitcast.8, f32[512,128]{1,0:T(8,128)S(1)} %get-tuple-element.15.main_in), custom_call_target="tpu_custom_call" | custom-call | flops 2000000 | bytes 1000000 | tf_op jit(solution)/shard_map/over/pallas_call | solution.py:424
  55.3 1.8 %collective-permute-start.2 = (f32[32,128]{1,0:T(8,128)S(1)}, f32[32,128]{1,0:T(8,128)S(1)}, u32[]{:S(2)}, u32[]{:S(2)}) collective-permute-start(f32[32,128]{1,0:T(8,128)S(1)} %get-tuple-element.21), channel_id=1, source_target_pairs={{0,2},{2,4},{4,6},{6,8},{8,10},{10,12},{12,14},{14,0},{1,3},{3,5},... | collective-permute-start | bytes 49160 | tf_op jit(solution)/shard_map/ppermute | solution.py:446
  57.1 0.1 collective-permute-start.3
  57.2 0.7 collective-permute-done.2.over_low
  57.9 2.3 %collective-permute-done.3.over_high = f32[32,128]{1,0:T(8,128)S(1)} collective-permute-done((f32[32,128]{1,0:T(8,128)S(1)}, f32[32,128]{1,0:T(8,128)S(1)}, u32[]{:S(2)}, u32[]{:S(2)}) %collective-permute-start.3) | collective-permute-done | bytes 16416 | tf_op jit(solution)/shard_map/ppermute | solution.py:446
  60.2 0.0 collective-permute-done.low
  60.2 0.0 collective-permute-done.1.high
  60.2 2.4 %last.1 = f32[512,128]{1,0:T(8,128)S(1)} custom-call(f32[1152,128]{1,0:T(8,128)S(1)} %bitcast.9, f32[1280,128]{1,0:T(8,128)S(1)} %get-tuple-element.14.factors, f32[1280,128]{1,0:T(8,128)S(1)} %get-tuple-element.16.over_factors, f32[512,128]{1,0:T(8,128)S(1)} %get-tuple-element.15.main_in, f32[512,128]{1,0:T(8,128)S(1)} %get-tuple-element.17.main_part, ...), custom_call_target="tpu_custom_call" | custom-call | flops 2000000 | bytes 1000000 | tf_op jit(solution)/shard_map/last/pallas_call | solution.py:424
  62.7 23.7 %all_to_all.11 = f32[32,16,128]{2,1,0:T(8,128)S(1)} all-to-all(f32[32,16,128]{2,1,0:T(8,128)S(1)} %bitcast.11), channel_id=1, replica_groups=mesh['slab'=32,'tile'=8,'tilt'=2] {'slab'}, dimensions={0} | all-to-all | bytes 524288 | tf_op jit(solution)/shard_map/all_to_all | solution.py:474
  86.4 1.0 %unpack.1 = f32[256,256]{1,0:T(8,128)} custom-call(f32[512,128]{1,0:T(8,128)S(1)} %bitcast.12), custom_call_target="tpu_custom_call" | custom-call | flops 2000000 | bytes 1000000 | tf_op jit(solution)/shard_map/unpack/pallas_call | solution.py:424
Async XLA Ops:
  51.0 9.3 %collective-permute-start = (f32[224,128]{1,0:T(8,128)S(1)}, f32[224,128]{1,0:T(8,128)S(1)}, u32[]{:S(2)}, u32[]{:S(2)}) collective-permute-start(f32[224,128]{1,0:T(8,128)S(1)} %get-tuple-element.19), channel_id=1, source_target_pairs={{0,2},{2,4},{4,6},{6,8},{8,10},{10,12},{12,14},{14,0},{1,3},{3,5},... | collective-permute-start | bytes 344072 | tf_op jit(solution)/shard_map/ppermute | solution.py:446
  53.8 6.4 %collective-permute-start.1 = (f32[224,128]{1,0:T(8,128)S(1)}, f32[224,128]{1,0:T(8,128)S(1)}, u32[]{:S(2)}, u32[]{:S(2)}) collective-permute-start(f32[224,128]{1,0:T(8,128)S(1)} %get-tuple-element.20), channel_id=1, source_target_pairs={{2,0},{4,2},{6,4},{8,6},{10,8},{12,10},{14,12},{0,14},{3,1},{5,3},... | collective-permute-start | bytes 344072 | tf_op jit(solution)/shard_map/ppermute | solution.py:446
  55.3 2.6 %collective-permute-start.2 = (f32[32,128]{1,0:T(8,128)S(1)}, f32[32,128]{1,0:T(8,128)S(1)}, u32[]{:S(2)}, u32[]{:S(2)}) collective-permute-start(f32[32,128]{1,0:T(8,128)S(1)} %get-tuple-element.21), channel_id=1, source_target_pairs={{0,2},{2,4},{4,6},{6,8},{8,10},{10,12},{12,14},{14,0},{1,3},{3,5},... | collective-permute-start | bytes 49160 | tf_op jit(solution)/shard_map/ppermute | solution.py:446
  57.1 3.2 %collective-permute-start.3 = (f32[32,128]{1,0:T(8,128)S(1)}, f32[32,128]{1,0:T(8,128)S(1)}, u32[]{:S(2)}, u32[]{:S(2)}) collective-permute-start(f32[32,128]{1,0:T(8,128)S(1)} %get-tuple-element.22), channel_id=1, source_target_pairs={{2,0},{4,2},{6,4},{8,6},{10,8},{12,10},{14,12},{0,14},{3,1},{5,3},... | collective-permute-start | bytes 49160 | tf_op jit(solution)/shard_map/ppermute | solution.py:446

commit v7 on v6

--- a/solution.py
+++ b/solution.py
@@ -299,7 +299,7 @@
             for r in range(DEPTH):
                 moved = roll(over[r][c], turned + over_place(c, r), 1)
                 total = jnp.where(over_lanes(base, c, r), moved, total)
-        edge[...] = total
+        edge[pl.ds(7 * SLABS, SLABS), :] = total
 
 
 def within():
@@ -360,28 +360,30 @@
     return [get(ref, r) for r in range(DEPTH)]
 
 
-def first_kernel(arrived, factors, main_out, *edges):
+def first_kernel(arrived, factors, over_factors, over_source, main_out, over_out, *edges):
     relatives = [layer(arrived, 2, r) for r in range(DEPTH)]
     source = [source_layer(arrived, r) for r in range(DEPTH)]
     factorize(relatives, factors)
     main = line_solve(source, factors)
     put_all(main_out, main)
     put_edges(main, source, relatives, edges)
-
-
-def over_kernel(arrived, main_in, over_factors, main_part, over_part, *edges):
     overlap = [overlap_layer(arrived, r) for r in range(DEPTH)]
+    put_all(over_source, [o[:2] for o in overlap])
     factorize([o[2] for o in overlap], over_factors, True)
     over = masked(line_solve([o[:2] for o in overlap], over_factors, True), inside())
+    put_all(over_out, over)
     put_over_edges(over, edges)
-    for r in range(DEPTH):
-        main = get(main_in, r)
-        put(main_part, r, relax(source_layer(arrived, r), [sum_main(m, e, 0.0) for m, e in zip(main, over[r])]))
-        put(over_part, r, relax(overlap[r][:2], [sum_over(m, e) for m, e in zip(main, over[r])]))
+
+
+def own_kernel(arrived, over_source, main_in, over_in, main_part, over_part):
+    for r in range(DEPTH):
+        main, over = get(main_in, r), get(over_in, r)
+        put(main_part, r, relax(source_layer(arrived, r), [sum_main(m, e, 0.0) for m, e in zip(main, over)]))
+        put(over_part, r, relax(get(over_source, r), [sum_over(m, e) for m, e in zip(main, over)]))
 
 
 def last_kernel(
-    arrived, factors, over_factors, main_in, main_part, over_part, low, high, over_low, over_high,
+    arrived, factors, over_factors, main_in, main_part, over_part, low, high,
     out, near_factors, main_mid, over_mid, near_mid,
 ):
     halos = (low, high)
@@ -391,8 +393,8 @@
     at_low, at_high = over_edge()
     over_outermost = at_low | at_high
     tile = lax.axis_index("tile")
-    cells_low = jnp.where(jnp.broadcast_to(tile > 0, x.shape), over_low[...], 0.0)
-    cells_high = jnp.where(jnp.broadcast_to(tile < TILES - 1, x.shape), over_high[...], 0.0)
+    cells_low = jnp.where(jnp.broadcast_to(tile > 0, x.shape), low[pl.ds(7 * SLABS, SLABS), :], 0.0)
+    cells_high = jnp.where(jnp.broadcast_to(tile < TILES - 1, x.shape), high[pl.ds(7 * SLABS, SLABS), :], 0.0)
     factorize([beside(halos, 6, r) for r in range(DEPTH)], near_factors)
     main_rhs, over_rhs, near_rhs = [], [], []
     for r in range(DEPTH):
@@ -435,8 +437,7 @@
 
 FIELD = (DEPTH * 2 * SLABS, LANES)
 FACTORS = (N_FACTORS * 2 * SLABS, LANES)
-EDGE = (7 * SLABS, LANES)
-OVER_EDGE = (SLABS, LANES)
+EDGE = (8 * SLABS, LANES)
 
 RING_UP = [(i, (i + 1) % TILES) for i in range(TILES)]
 RING_DOWN = [(b, a) for a, b in RING_UP]
@@ -460,15 +461,14 @@
         ],
     )
     arrived = lax.all_to_all(packed.reshape(SLABS, ROWS // 4, 4, LANES), "slab", 0, 0).reshape(SLABS * ROWS, LANES)
-    factors, main, *edges = call(first_kernel, "first", [FACTORS, FIELD, EDGE, EDGE], arrived)
+    factors, over_factors, over_source, main, over, *edges = call(
+        first_kernel, "first", [FACTORS, FACTORS, FIELD, FIELD, FIELD, EDGE, EDGE], arrived
+    )
     halos = exchange(*edges)
-    over_factors, main_part, over_part, *edges = call(
-        over_kernel, "over", [FACTORS, FIELD, FIELD, OVER_EDGE, OVER_EDGE], arrived, main
-    )
-    over_halos = exchange(*edges)
+    main_part, over_part = call(own_kernel, "own", [FIELD, FIELD], arrived, over_source, main, over)
     (packed,) = call(
         last_kernel, "last", [(SLABS * 16, LANES)],
-        arrived, factors, over_factors, main, main_part, over_part, *halos, *over_halos,
+        arrived, factors, over_factors, main, main_part, over_part, *halos,
         scratch=[pltpu.VMEM(FACTORS, F32)] + [pltpu.VMEM(FIELD, F32)] * 3,
     )
     arrived = lax.all_to_all(packed.reshape(SLABS, 16, LANES), "slab", 0, 0).reshape(SLABS * 16, LANES)

time: 87.7 us -> 86.6 us (0.987)
  starting transfers between devices: 4.75 us -> 2.86 us
    ppermute x2 -> x1, starting transfers between devices: 4.61 us -> 2.86 us  [exchange(): lax.ppermute(high, 'tile', RING_UP)]
    ppermute x2 -> x1, waiting for transfers between devices: 2.3 us -> 2.44 us  [exchange(): lax.ppermute(low, 'tile', RING_DOWN)]
  transfers between devices with their start and end apart: 4 -> 2, of which waited for: 2 -> 2; matrix products, arithmetic and copies ran while one was open for 0% -> 0% of each run, Pallas kernels for 2% -> 1%
where the time goes in v7:
time: 86.6 us; the launch traced here: 86.4 us
  blocking collectives  71.7 us (83%)
  Pallas kernels  7.99 us (9%)
  waiting for transfers between devices  3.78 us (4%)
  starting transfers between devices  2.86 us (3%)
    all_to_all x1, blocking collectives, local(): lax.all_to_all(packed.reshape(SLABS, ROWS // 4, 4, LANES), 'slab', 0, 0)  47.8 us
    all_to_all x1, blocking collectives, local(): lax.all_to_all(packed.reshape(SLABS, 16, LANES), 'slab', 0, 0)  23.9 us
    pallas_call x5, Pallas kernels, call(): pl.pallas_call(kernel, out_shape=[jax.ShapeDtypeStruct(s, F32) for s in o...  7.99 us
    ppermute x1, starting transfers between devices, exchange(): lax.ppermute(high, 'tile', RING_UP)  2.86 us
    ppermute x1, waiting for transfers between devices, exchange(): lax.ppermute(low, 'tile', RING_DOWN)  2.44 us
  transfers between devices with their start and end apart: 2, of which 2 were waited for; matrix products, arithmetic and copies ran while one was open for 0% of the time, Pallas kernels for 1%

profile of v7, /device:TPU:1, one launch (start us, length us, event | category | flops | bytes accessed | tf_op | source)
XLA Modules:
  0.0 86.4 jit_solution(8412300539062932144)
XLA Ops:
  0.0 2.0 %pack.1 = f32[1152,128]{1,0:T(8,128)S(1)} custom-call(f32[8]{0:T(128)} %table_hbm.1, f32[256,256]{1,0:T(8,128)} %bitcast.13, s32[128,256]{1,0:T(8,128)} %bitcast.14), custom_call_target="tpu_custom_call" | custom-call | flops 2000000 | bytes 1000000 | tf_op jit(solution)/shard_map/pack/pallas_call | solution.py:426
  2.1 47.8 %all_to_all.10 = f32[32,9,4,128]{3,2,1,0:T(4,128)S(1)} all-to-all(f32[32,9,4,128]{3,2,1,0:T(4,128)S(1)} %bitcast.10), channel_id=1, replica_groups=mesh['slab'=32,'tile'=8,'tilt'=2] {'slab'}, dimensions={0} | all-to-all | bytes 1179648 | tf_op jit(solution)/shard_map/all_to_all | solution.py:463
  49.9 1.9 %first.1 = (f32[1280,128]{1,0:T(8,128)S(1)}, f32[1280,128]{1,0:T(8,128)S(1)}, f32[512,128]{1,0:T(8,128)S(1)}, f32[512,128]{1,0:T(8,128)S(1)}, f32[512,128]{1,0:T...) custom-call(f32[1152,128]{1,0:T(8,128)S(1)} %bitcast.7), custom_call_target="tpu_custom_call" | custom-call | flops 2000000 | bytes 1000000 | tf_op jit(solution)/shard_map/first/pallas_call | solution.py:426
  51.9 2.9 %collective-permute-start = (f32[256,128]{1,0:T(8,128)S(1)}, f32[256,128]{1,0:T(8,128)S(1)}, u32[]{:S(2)}, u32[]{:S(2)}) collective-permute-start(f32[256,128]{1,0:T(8,128)S(1)} %get-tuple-element.21), channel_id=1, source_target_pairs={{0,2},{2,4},{4,6},{6,8},{8,10},{10,12},{12,14},{14,0},{1,3},{3,5},... | collective-permute-start | bytes 393224 | tf_op jit(solution)/shard_map/ppermute | solution.py:447
  54.7 0.0 collective-permute-start.1
  54.7 0.6 own.1
  55.3 1.3 %collective-permute-done.low = f32[256,128]{1,0:T(8,128)S(1)} collective-permute-done((f32[256,128]{1,0:T(8,128)S(1)}, f32[256,128]{1,0:T(8,128)S(1)}, u32[]{:S(2)}, u32[]{:S(2)}) %collective-permute-start) | collective-permute-done | bytes 131104 | tf_op jit(solution)/shard_map/ppermute | solution.py:447
  56.7 2.4 %collective-permute-done.1.high = f32[256,128]{1,0:T(8,128)S(1)} collective-permute-done((f32[256,128]{1,0:T(8,128)S(1)}, f32[256,128]{1,0:T(8,128)S(1)}, u32[]{:S(2)}, u32[]{:S(2)}) %collective-permute-start.1) | collective-permute-done | bytes 131104 | tf_op jit(solution)/shard_map/ppermute | solution.py:447
  59.1 2.4 %last.1 = f32[512,128]{1,0:T(8,128)S(1)} custom-call(f32[1152,128]{1,0:T(8,128)S(1)} %bitcast.9, f32[1280,128]{1,0:T(8,128)S(1)} %get-tuple-element.14.factors, f32[1280,128]{1,0:T(8,128)S(1)} %get-tuple-element.15.over_factors, f32[512,128]{1,0:T(8,128)S(1)} %get-tuple-element.16.main_in, f32[512,128]{1,0:T(8,128)S(1)} %get-tuple-element.19.main_part, ...), custom_call_target="tpu_custom_call" | custom-call | flops 2000000 | bytes 1000000 | tf_op jit(solution)/shard_map/last/pallas_call | solution.py:426
  61.5 23.9 %all_to_all.11 = f32[32,16,128]{2,1,0:T(8,128)S(1)} all-to-all(f32[32,16,128]{2,1,0:T(8,128)S(1)} %bitcast.11), channel_id=1, replica_groups=mesh['slab'=32,'tile'=8,'tilt'=2] {'slab'}, dimensions={0} | all-to-all | bytes 524288 | tf_op jit(solution)/shard_map/all_to_all | solution.py:474
  85.4 1.0 %unpack.1 = f32[256,256]{1,0:T(8,128)} custom-call(f32[512,128]{1,0:T(8,128)S(1)} %bitcast.12), custom_call_target="tpu_custom_call" | custom-call | flops 2000000 | bytes 1000000 | tf_op jit(solution)/shard_map/unpack/pallas_call | solution.py:426
Async XLA Ops:
  51.9 4.8 %collective-permute-start = (f32[256,128]{1,0:T(8,128)S(1)}, f32[256,128]{1,0:T(8,128)S(1)}, u32[]{:S(2)}, u32[]{:S(2)}) collective-permute-start(f32[256,128]{1,0:T(8,128)S(1)} %get-tuple-element.21), channel_id=1, source_target_pairs={{0,2},{2,4},{4,6},{6,8},{8,10},{10,12},{12,14},{14,0},{1,3},{3,5},... | collective-permute-start | bytes 393224 | tf_op jit(solution)/shard_map/ppermute | solution.py:447
  54.7 4.4 %collective-permute-start.1 = (f32[256,128]{1,0:T(8,128)S(1)}, f32[256,128]{1,0:T(8,128)S(1)}, u32[]{:S(2)}, u32[]{:S(2)}) collective-permute-start(f32[256,128]{1,0:T(8,128)S(1)} %get-tuple-element.22), channel_id=1, source_target_pairs={{2,0},{4,2},{6,4},{8,6},{10,8},{12,10},{14,12},{0,14},{3,1},{5,3},... | collective-permute-start | bytes 393224 | tf_op jit(solution)/shard_map/ppermute | solution.py:447

commit v8 on v7

--- a/solution.py
+++ b/solution.py
@@ -265,17 +265,15 @@
     return field
 
 
-def put_edges(main, source, relatives, edges):
+def put_edges(main, part, relatives, edges):
     _, x, _ = lane_ids()
     for edge, is_high in zip(edges, (False, True)):
-        place_to = 0 if is_high else 7
-        near, far = (7, 6) if is_high else (0, 1)
-        lines = [([f[c] for f in main], line) for line in (near, far) for c in range(2)]
-        lines += [([f[c] for f in source], near) for c in range(2)] + [(relatives, near)]
-        for place, (layers, line) in enumerate(lines):
+        place_to, turned = (0, -56) if is_high else (7, 56)
+        arrays = [[f[c] for f in main] for c in range(2)] + [[f[c] for f in part] for c in range(2)] + [relatives]
+        for place, layers in enumerate(arrays):
             total = None
             for r in range(DEPTH):
-                moved = roll(layers[r], 8 * (place_to - line + r), 1)
+                moved = roll(layers[r], turned + 8 * r, 1)
                 total = moved if r == 0 else jnp.where(x == (place_to + r) % 8, moved, total)
             edge[pl.ds(place * SLABS, SLABS), :] = total
 
@@ -299,7 +297,7 @@
             for r in range(DEPTH):
                 moved = roll(over[r][c], turned + over_place(c, r), 1)
                 total = jnp.where(over_lanes(base, c, r), moved, total)
-        edge[pl.ds(7 * SLABS, SLABS), :] = total
+        edge[pl.ds(5 * SLABS, SLABS), :] = total
 
 
 def within():
@@ -360,26 +358,26 @@
     return [get(ref, r) for r in range(DEPTH)]
 
 
-def first_kernel(arrived, factors, over_factors, over_source, main_out, over_out, *edges):
-    relatives = [layer(arrived, 2, r) for r in range(DEPTH)]
-    source = [source_layer(arrived, r) for r in range(DEPTH)]
-    factorize(relatives, factors)
-    main = line_solve(source, factors)
-    put_all(main_out, main)
-    put_edges(main, source, relatives, edges)
+def first_kernel(arrived, factors, over_factors, over_source, main_out, over_out, main_part, *edges):
     overlap = [overlap_layer(arrived, r) for r in range(DEPTH)]
     put_all(over_source, [o[:2] for o in overlap])
     factorize([o[2] for o in overlap], over_factors, True)
     over = masked(line_solve([o[:2] for o in overlap], over_factors, True), inside())
     put_all(over_out, over)
     put_over_edges(over, edges)
-
-
-def own_kernel(arrived, over_source, main_in, over_in, main_part, over_part):
-    for r in range(DEPTH):
-        main, over = get(main_in, r), get(over_in, r)
-        put(main_part, r, relax(source_layer(arrived, r), [sum_main(m, e, 0.0) for m, e in zip(main, over)]))
-        put(over_part, r, relax(get(over_source, r), [sum_over(m, e) for m, e in zip(main, over)]))
+    relatives = [layer(arrived, 2, r) for r in range(DEPTH)]
+    source = [source_layer(arrived, r) for r in range(DEPTH)]
+    factorize(relatives, factors)
+    main = line_solve(source, factors)
+    put_all(main_out, main)
+    part = [relax(source[r], [sum_main(m, e, 0.0) for m, e in zip(main[r], get(over_out, r))]) for r in range(DEPTH)]
+    put_all(main_part, part)
+    put_edges(main, part, relatives, edges)
+
+
+def own_kernel(over_source, main_in, over_in, over_part):
+    for r in range(DEPTH):
+        put(over_part, r, relax(get(over_source, r), [sum_over(m, e) for m, e in zip(get(main_in, r), get(over_in, r))]))
 
 
 def last_kernel(
@@ -393,22 +391,19 @@
     at_low, at_high = over_edge()
     over_outermost = at_low | at_high
     tile = lax.axis_index("tile")
-    cells_low = jnp.where(jnp.broadcast_to(tile > 0, x.shape), low[pl.ds(7 * SLABS, SLABS), :], 0.0)
-    cells_high = jnp.where(jnp.broadcast_to(tile < TILES - 1, x.shape), high[pl.ds(7 * SLABS, SLABS), :], 0.0)
-    factorize([beside(halos, 6, r) for r in range(DEPTH)], near_factors)
+    cells_low = jnp.where(jnp.broadcast_to(tile > 0, x.shape), low[pl.ds(5 * SLABS, SLABS), :], 0.0)
+    cells_high = jnp.where(jnp.broadcast_to(tile < TILES - 1, x.shape), high[pl.ds(5 * SLABS, SLABS), :], 0.0)
+    factorize([beside(halos, 4, r) for r in range(DEPTH)], near_factors)
     main_rhs, over_rhs, near_rhs = [], [], []
     for r in range(DEPTH):
-        main_adds, over_adds, near_sums = [], [], []
+        main_adds, over_adds = [], []
         for c in range(2):
             near = jnp.where(keep, beside(halos, c, r), 0.0)
-            cells = over_beside(cells_low, cells_high, c, r)
             main_adds.append(jnp.where(outermost, near, 0.0))
-            over_adds.append(jnp.where(over_outermost, cells, 0.0))
-            main = main_in[pl.ds((2 * r + c) * SLABS, SLABS), :]
-            near_sums.append(beside(halos, 2 + c, r) + main + sum_y(near, cells))
+            over_adds.append(jnp.where(over_outermost, over_beside(cells_low, cells_high, c, r), 0.0))
         main_rhs.append(relax(get(main_part, r), main_adds))
         over_rhs.append(relax(get(over_part, r), over_adds))
-        near_rhs.append(relax((beside(halos, 4, r), beside(halos, 5, r)), near_sums))
+        near_rhs.append(relax((beside(halos, 2, r), beside(halos, 3, r)), get(main_in, r)))
     put_all(main_mid, line_solve(main_rhs, factors))
     put_all(over_mid, masked(line_solve(over_rhs, over_factors, True), inside()))
     put_all(near_mid, masked(line_solve(near_rhs, near_factors), keep))
@@ -437,7 +432,7 @@
 
 FIELD = (DEPTH * 2 * SLABS, LANES)
 FACTORS = (N_FACTORS * 2 * SLABS, LANES)
-EDGE = (8 * SLABS, LANES)
+EDGE = (6 * SLABS, LANES)
 
 RING_UP = [(i, (i + 1) % TILES) for i in range(TILES)]
 RING_DOWN = [(b, a) for a, b in RING_UP]
@@ -461,11 +456,11 @@
         ],
     )
     arrived = lax.all_to_all(packed.reshape(SLABS, ROWS // 4, 4, LANES), "slab", 0, 0).reshape(SLABS * ROWS, LANES)
-    factors, over_factors, over_source, main, over, *edges = call(
-        first_kernel, "first", [FACTORS, FACTORS, FIELD, FIELD, FIELD, EDGE, EDGE], arrived
+    factors, over_factors, over_source, main, over, main_part, *edges = call(
+        first_kernel, "first", [FACTORS, FACTORS, FIELD, FIELD, FIELD, FIELD, EDGE, EDGE], arrived
     )
     halos = exchange(*edges)
-    main_part, over_part = call(own_kernel, "own", [FIELD, FIELD], arrived, over_source, main, over)
+    (over_part,) = call(own_kernel, "own", [FIELD], over_source, main, over)
     (packed,) = call(
         last_kernel, "last", [(SLABS * 16, LANES)],
         arrived, factors, over_factors, main, main_part, over_part, *halos,

time: 86.6 us -> 85.7 us (0.990)
  transfers between devices with their start and end apart: 2 -> 2, of which waited for: 2 -> 2; matrix products, arithmetic and copies ran while one was open for 0% -> 0% of each run, Pallas kernels for 1% -> 0%
where the time goes in v8:
time: 85.7 us; the launch traced here: 85.5 us
  blocking collectives  71.7 us (84%)
  Pallas kernels  7.17 us (8%)
  waiting for transfers between devices  3.7 us (4%)
  starting transfers between devices  2.86 us (3%)
    all_to_all x1, blocking collectives, local(): lax.all_to_all(packed.reshape(SLABS, ROWS // 4, 4, LANES), 'slab', 0, 0)  47.8 us
    all_to_all x1, blocking collectives, local(): lax.all_to_all(packed.reshape(SLABS, 16, LANES), 'slab', 0, 0)  23.9 us
    pallas_call x5, Pallas kernels, call(): pl.pallas_call(kernel, out_shape=[jax.ShapeDtypeStruct(s, F32) for s in o...  7.17 us
    ppermute x1, starting transfers between devices, exchange(): lax.ppermute(high, 'tile', RING_UP)  2.86 us
    ppermute x1, waiting for transfers between devices, exchange(): lax.ppermute(low, 'tile', RING_DOWN)  2.4 us
  transfers between devices with their start and end apart: 2, of which 2 were waited for; matrix products, arithmetic and copies ran while one was open for 0% of the time, Pallas kernels for 0%

profile of v8, /device:TPU:1, one launch (start us, length us, event | category | flops | bytes accessed | tf_op | source)
XLA Modules:
  0.0 85.5 jit_solution(6954152268370998194)
XLA Ops:
  0.0 2.0 %pack.1 = f32[1152,128]{1,0:T(8,128)S(1)} custom-call(f32[8]{0:T(128)} %table_hbm.1, f32[256,256]{1,0:T(8,128)} %bitcast.12, s32[128,256]{1,0:T(8,128)} %bitcast.13), custom_call_target="tpu_custom_call" | custom-call | flops 2000000 | bytes 1000000 | tf_op jit(solution)/shard_map/pack/pallas_call | solution.py:421
  2.1 47.8 %all_to_all.10 = f32[32,9,4,128]{3,2,1,0:T(4,128)S(1)} all-to-all(f32[32,9,4,128]{3,2,1,0:T(4,128)S(1)} %bitcast.9), channel_id=1, replica_groups=mesh['slab'=32,'tile'=8,'tilt'=2] {'slab'}, dimensions={0} | all-to-all | bytes 1179648 | tf_op jit(solution)/shard_map/all_to_all | solution.py:458
  49.9 2.1 %first.1 = (f32[1280,128]{1,0:T(8,128)S(1)}, f32[1280,128]{1,0:T(8,128)S(1)}, f32[512,128]{1,0:T(8,128)S(1)}, f32[512,128]{1,0:T(8,128)S(1)}, f32[512,128]{1,0:T...) custom-call(f32[1152,128]{1,0:T(8,128)S(1)} %bitcast.7), custom_call_target="tpu_custom_call" | custom-call | flops 2000000 | bytes 1000000 | tf_op jit(solution)/shard_map/first/pallas_call | solution.py:421
  52.0 2.9 %collective-permute-start = (f32[192,128]{1,0:T(8,128)S(1)}, f32[192,128]{1,0:T(8,128)S(1)}, u32[]{:S(2)}, u32[]{:S(2)}) collective-permute-start(f32[192,128]{1,0:T(8,128)S(1)} %get-tuple-element.19), channel_id=1, source_target_pairs={{0,2},{2,4},{4,6},{6,8},{8,10},{10,12},{12,14},{14,0},{1,3},{3,5},... | collective-permute-start | bytes 294920 | tf_op jit(solution)/shard_map/ppermute | solution.py:442
  54.8 0.0 collective-permute-start.1
  54.8 0.3 own.1.over_part
  55.2 1.3 %collective-permute-done.low = f32[192,128]{1,0:T(8,128)S(1)} collective-permute-done((f32[192,128]{1,0:T(8,128)S(1)}, f32[192,128]{1,0:T(8,128)S(1)}, u32[]{:S(2)}, u32[]{:S(2)}) %collective-permute-start) | collective-permute-done | bytes 98336 | tf_op jit(solution)/shard_map/ppermute | solution.py:442
  56.5 2.4 %collective-permute-done.1.high = f32[192,128]{1,0:T(8,128)S(1)} collective-permute-done((f32[192,128]{1,0:T(8,128)S(1)}, f32[192,128]{1,0:T(8,128)S(1)}, u32[]{:S(2)}, u32[]{:S(2)}) %collective-permute-start.1) | collective-permute-done | bytes 98336 | tf_op jit(solution)/shard_map/ppermute | solution.py:442
  58.9 1.7 %last.1 = f32[512,128]{1,0:T(8,128)S(1)} custom-call(f32[1152,128]{1,0:T(8,128)S(1)} %bitcast.8, f32[1280,128]{1,0:T(8,128)S(1)} %get-tuple-element.13.factors, f32[1280,128]{1,0:T(8,128)S(1)} %get-tuple-element.14.over_factors, f32[512,128]{1,0:T(8,128)S(1)} %get-tuple-element.15.main_in, f32[512,128]{1,0:T(8,128)S(1)} %get-tuple-element.16.main_part, ...), custom_call_target="tpu_custom_call" | custom-call | flops 2000000 | bytes 1000000 | tf_op jit(solution)/shard_map/last/pallas_call | solution.py:421
  60.6 23.9 %all_to_all.11 = f32[32,16,128]{2,1,0:T(8,128)S(1)} all-to-all(f32[32,16,128]{2,1,0:T(8,128)S(1)} %bitcast.10), channel_id=1, replica_groups=mesh['slab'=32,'tile'=8,'tilt'=2] {'slab'}, dimensions={0} | all-to-all | bytes 524288 | tf_op jit(solution)/shard_map/all_to_all | solution.py:469
  84.5 1.0 %unpack.1 = f32[256,256]{1,0:T(8,128)} custom-call(f32[512,128]{1,0:T(8,128)S(1)} %bitcast.11), custom_call_target="tpu_custom_call" | custom-call | flops 2000000 | bytes 1000000 | tf_op jit(solution)/shard_map/unpack/pallas_call | solution.py:421
Async XLA Ops:
  52.0 4.5 %collective-permute-start = (f32[192,128]{1,0:T(8,128)S(1)}, f32[192,128]{1,0:T(8,128)S(1)}, u32[]{:S(2)}, u32[]{:S(2)}) collective-permute-start(f32[192,128]{1,0:T(8,128)S(1)} %get-tuple-element.19), channel_id=1, source_target_pairs={{0,2},{2,4},{4,6},{6,8},{8,10},{10,12},{12,14},{14,0},{1,3},{3,5},... | collective-permute-start | bytes 294920 | tf_op jit(solution)/shard_map/ppermute | solution.py:442
  54.8 4.0 %collective-permute-start.1 = (f32[192,128]{1,0:T(8,128)S(1)}, f32[192,128]{1,0:T(8,128)S(1)}, u32[]{:S(2)}, u32[]{:S(2)}) collective-permute-start(f32[192,128]{1,0:T(8,128)S(1)} %get-tuple-element.20), channel_id=1, source_target_pairs={{2,0},{4,2},{6,4},{8,6},{10,8},{12,10},{14,12},{0,14},{3,1},{5,3},... | collective-permute-start | bytes 294920 | tf_op jit(solution)/shard_map/ppermute | solution.py:442

commit v9 on v8

--- a/solution.py
+++ b/solution.py
@@ -71,11 +71,13 @@
     for side in range(2):
         lanes = pl.ds(side * LANES, LANES)
         copies.append(pltpu.make_async_copy(labels.at[:, lanes], marks.at[side], sems.at[1 + side]))
+    for side in range(2):
+        lanes = pl.ds(side * LANES, LANES)
         into = sides.at[side, pl.ds(0, 2 * LANES)]
         copies.append(pltpu.make_async_copy(source.at[:, lanes], into, sems.at[3 + side]))
     for copy in copies:
         copy.start()
-    for copy in copies:
+    for copy in copies[:3]:
         copy.wait()
     for side in range(2):
         lab = marks[side]
@@ -83,6 +85,8 @@
         for m in range(1, 8):
             rel = jnp.where(lab == m, table[m], rel)
         sides[side, pl.ds(2 * LANES, LANES), :] = rel
+    for copy in copies[3:]:
+        copy.wait()
 
     def load(side, quantity):
         places = [quantity * LANES + half * 64 + x for half in range(2) for x in range(8)]
@@ -108,14 +112,19 @@
         out[pl.ds(chunk * ROWS + 32, 4), :] = jnp.where(from_above, singles[upper], singles[lower])[:4]
 
 
-def unpack_kernel(arrived, out, sides):
+def unpack_kernel(arrived, out, sides, sems):
+    copies = []
     for side in range(2):
         for c in range(2):
             parts = [arrived[pl.ds((16 * side + b) * 16 + c * 8, 8), :] for b in range(16)]
             for i, part in enumerate(block_transpose(turn(parts))):
                 half, x = divmod(i, 8)
                 sides[side, pl.ds(c * LANES + half * 64 + x, 8, stride=8), :] = part
-        out[:, pl.ds(side * LANES, LANES)] = sides[side]
+        lanes = pl.ds(side * LANES, LANES)
+        copies.append(pltpu.make_async_copy(sides.at[side], out.at[:, lanes], sems.at[side]))
+        copies[-1].start()
+    for copy in copies:
+        copy.wait()
 
 
 def lane_ids():
@@ -265,39 +274,45 @@
     return field
 
 
-def put_edges(main, part, relatives, edges):
+def cell_lanes(r, low_line):
+    _, x, y = lane_ids()
+    at = r if low_line else 7 + r
+    return ((x == (at - 1) % 8) & (y == 7)) | ((x == (at + 1) % 8) & (y == 0))
+
+
+def put_edges(main, over, source, relatives, edges):
     _, x, _ = lane_ids()
-    for edge, is_high in zip(edges, (False, True)):
-        place_to, turned = (0, -56) if is_high else (7, 56)
-        arrays = [[f[c] for f in main] for c in range(2)] + [[f[c] for f in part] for c in range(2)] + [relatives]
-        for place, layers in enumerate(arrays):
-            total = None
-            for r in range(DEPTH):
-                moved = roll(layers[r], turned + 8 * r, 1)
-                total = moved if r == 0 else jnp.where(x == (place_to + r) % 8, moved, total)
-            edge[pl.ds(place * SLABS, SLABS), :] = total
-
-
-def over_place(c, r):
-    n = 8 * c + r
-    return n if n < 9 else n + 9
-
-
-def over_lanes(base, c, r):
-    lane = lax.broadcasted_iota(jnp.int32, (SLABS, LANES), 1) % 64
-    first = base + over_place(c, r)
-    return (lane == (first - 1) % 64) | (lane == (first + 8) % 64)
-
-
-def put_over_edges(over, edges):
-    for edge, is_high in zip(edges, (False, True)):
-        turned, base = (-56, 0) if is_high else (56, 56)
-        total = jnp.zeros((SLABS, LANES), F32)
-        for c in range(2):
-            for r in range(DEPTH):
-                moved = roll(over[r][c], turned + over_place(c, r), 1)
-                total = jnp.where(over_lanes(base, c, r), moved, total)
-        edge[pl.ds(5 * SLABS, SLABS), :] = total
+
+    def pack(layers, low_line, high_line):
+        low = high = layers[0]
+        for r in range(1, DEPTH):
+            moved = roll(layers[r], 8 * r, 1)
+            low = jnp.where(x == (low_line + r) % 8, moved, low)
+            high = jnp.where(x == (high_line + r) % 8, moved, high)
+        return low, high
+
+    def pack_cells(layers):
+        low = high = jnp.zeros((SLABS, LANES), F32)
+        for r in range(DEPTH):
+            moved = roll(layers[r], 8 * r, 1)
+            low = jnp.where(cell_lanes(r, True), moved, low)
+            high = jnp.where(cell_lanes(r, False), moved, high)
+        return low, high
+
+    packed = [None] * 7
+    for c in range(2):
+        near = pack([f[c] for f in main], 0, 7)
+        far = pack([f[c] for f in main], 1, 6)
+        far = roll(far[0], -8, 1), roll(far[1], 8, 1)
+        own = pack([f[c] for f in source], 0, 7)
+        cells = pack_cells([f[c] for f in over])
+        packed[c] = near
+        packed[2 + c] = [own[i] + COUPLE * (far[i] + sum_y(near[i], cells[i])) for i in range(2)]
+        packed[5 + c] = cells
+    packed[4] = pack(relatives, 0, 7)
+    for place, pair in enumerate(packed):
+        for edge, array, turned in zip(edges, pair, (56, -56)):
+            edge[pl.ds(place * SLABS, SLABS), :] = roll(array, turned, 1)
 
 
 def within():
@@ -314,8 +329,8 @@
     return roll(jnp.where(x == r, low, high), -8 * r, 1)
 
 
-def over_beside(low, high, c, r):
-    return roll(jnp.where(over_lanes(0, c, r), low, high), -over_place(c, r), 1)
+def over_beside(low, high, r):
+    return roll(jnp.where(cell_lanes(r, True), low, high), -8 * r, 1)
 
 
 def sum_y(field, over):
@@ -358,26 +373,25 @@
     return [get(ref, r) for r in range(DEPTH)]
 
 
-def first_kernel(arrived, factors, over_factors, over_source, main_out, over_out, main_part, *edges):
+def first_kernel(arrived, factors, over_factors, over_source, main_out, over_out, *edges):
     overlap = [overlap_layer(arrived, r) for r in range(DEPTH)]
     put_all(over_source, [o[:2] for o in overlap])
     factorize([o[2] for o in overlap], over_factors, True)
     over = masked(line_solve([o[:2] for o in overlap], over_factors, True), inside())
     put_all(over_out, over)
-    put_over_edges(over, edges)
     relatives = [layer(arrived, 2, r) for r in range(DEPTH)]
     source = [source_layer(arrived, r) for r in range(DEPTH)]
     factorize(relatives, factors)
     main = line_solve(source, factors)
     put_all(main_out, main)
-    part = [relax(source[r], [sum_main(m, e, 0.0) for m, e in zip(main[r], get(over_out, r))]) for r in range(DEPTH)]
-    put_all(main_part, part)
-    put_edges(main, part, relatives, edges)
-
-
-def own_kernel(over_source, main_in, over_in, over_part):
-    for r in range(DEPTH):
-        put(over_part, r, relax(get(over_source, r), [sum_over(m, e) for m, e in zip(get(main_in, r), get(over_in, r))]))
+    put_edges(main, over, source, relatives, edges)
+
+
+def own_kernel(arrived, over_source, main_in, over_in, main_part, over_part):
+    for r in range(DEPTH):
+        main, over = get(main_in, r), get(over_in, r)
+        put(main_part, r, relax(source_layer(arrived, r), [sum_main(m, e, 0.0) for m, e in zip(main, over)]))
+        put(over_part, r, relax(get(over_source, r), [sum_over(m, e) for m, e in zip(main, over)]))
 
 
 def last_kernel(
@@ -391,8 +405,8 @@
     at_low, at_high = over_edge()
     over_outermost = at_low | at_high
     tile = lax.axis_index("tile")
-    cells_low = jnp.where(jnp.broadcast_to(tile > 0, x.shape), low[pl.ds(5 * SLABS, SLABS), :], 0.0)
-    cells_high = jnp.where(jnp.broadcast_to(tile < TILES - 1, x.shape), high[pl.ds(5 * SLABS, SLABS), :], 0.0)
+    exists = [jnp.broadcast_to(k, x.shape) for k in (tile > 0, tile < TILES - 1)]
+    cells = [[jnp.where(k, h[pl.ds((5 + c) * SLABS, SLABS), :], 0.0) for h, k in zip(halos, exists)] for c in range(2)]
     factorize([beside(halos, 4, r) for r in range(DEPTH)], near_factors)
     main_rhs, over_rhs, near_rhs = [], [], []
     for r in range(DEPTH):
@@ -400,7 +414,7 @@
         for c in range(2):
             near = jnp.where(keep, beside(halos, c, r), 0.0)
             main_adds.append(jnp.where(outermost, near, 0.0))
-            over_adds.append(jnp.where(over_outermost, over_beside(cells_low, cells_high, c, r), 0.0))
+            over_adds.append(jnp.where(over_outermost, over_beside(*cells[c], r), 0.0))
         main_rhs.append(relax(get(main_part, r), main_adds))
         over_rhs.append(relax(get(over_part, r), over_adds))
         near_rhs.append(relax((beside(halos, 2, r), beside(halos, 3, r)), get(main_in, r)))
@@ -417,12 +431,12 @@
             out[pl.ds(c * 8 + r, SLABS, stride=16), :] = field[r][c]
 
 
-def call(kernel, name, outs, *args, scratch=(), spec=VMEM):
+def call(kernel, name, outs, *args, scratch=(), spec=VMEM, out_spec=VMEM):
     return pl.pallas_call(
         kernel,
         out_shape=[jax.ShapeDtypeStruct(s, F32) for s in outs],
         in_specs=[spec] * len(args),
-        out_specs=[VMEM] * len(outs),
+        out_specs=[out_spec] * len(outs),
         scratch_shapes=list(scratch),
         compiler_params=pltpu.CompilerParams(vmem_limit_bytes=32 << 20),
         cost_estimate=pl.CostEstimate(flops=2_000_000, bytes_accessed=1_000_000, transcendentals=0),
@@ -432,7 +446,7 @@
 
 FIELD = (DEPTH * 2 * SLABS, LANES)
 FACTORS = (N_FACTORS * 2 * SLABS, LANES)
-EDGE = (6 * SLABS, LANES)
+EDGE = (7 * SLABS, LANES)
 
 RING_UP = [(i, (i + 1) % TILES) for i in range(TILES)]
 RING_DOWN = [(b, a) for a, b in RING_UP]
@@ -456,11 +470,11 @@
         ],
     )
     arrived = lax.all_to_all(packed.reshape(SLABS, ROWS // 4, 4, LANES), "slab", 0, 0).reshape(SLABS * ROWS, LANES)
-    factors, over_factors, over_source, main, over, main_part, *edges = call(
-        first_kernel, "first", [FACTORS, FACTORS, FIELD, FIELD, FIELD, FIELD, EDGE, EDGE], arrived
+    factors, over_factors, over_source, main, over, *edges = call(
+        first_kernel, "first", [FACTORS, FACTORS, FIELD, FIELD, FIELD, EDGE, EDGE], arrived
     )
     halos = exchange(*edges)
-    (over_part,) = call(own_kernel, "own", [FIELD], over_source, main, over)
+    main_part, over_part = call(own_kernel, "own", [FIELD, FIELD], arrived, over_source, main, over)
     (packed,) = call(
         last_kernel, "last", [(SLABS * 16, LANES)],
         arrived, factors, over_factors, main, main_part, over_part, *halos,
@@ -468,7 +482,8 @@
     )
     arrived = lax.all_to_all(packed.reshape(SLABS, 16, LANES), "slab", 0, 0).reshape(SLABS * 16, LANES)
     (out,) = call(
-        unpack_kernel, "unpack", [(2 * 16 * 8, 256)], arrived, scratch=[pltpu.VMEM((2, 2 * LANES, LANES), F32)]
+        unpack_kernel, "unpack", [(2 * 16 * 8, 256)], arrived, out_spec=HBM,
+        scratch=[pltpu.VMEM((2, 2 * LANES, LANES), F32), pltpu.SemaphoreType.DMA((2,))],
     )
     return out.reshape(2, 16, 8, 256)
 

time: 85.7 us -> 85.4 us (level)
  transfers between devices with their start and end apart: 2 -> 2, of which waited for: 2 -> 2; matrix products, arithmetic and copies ran while one was open for 0% -> 0% of each run, Pallas kernels for 0% -> 1%
where the time goes in v9:
time: 85.4 us; the launch traced here: 85.2 us
  blocking collectives  71.7 us (84%)
  Pallas kernels  6.95 us (8%)
  waiting for transfers between devices  3.6 us (4%)
  starting transfers between devices  2.86 us (3%)
    all_to_all x1, blocking collectives, local(): lax.all_to_all(packed.reshape(SLABS, ROWS // 4, 4, LANES), 'slab', 0, 0)  47.8 us
    all_to_all x1, blocking collectives, local(): lax.all_to_all(packed.reshape(SLABS, 16, LANES), 'slab', 0, 0)  23.9 us
    pallas_call x5, Pallas kernels, call(): pl.pallas_call(kernel, out_shape=[jax.ShapeDtypeStruct(s, F32) for s in o...  6.95 us
    ppermute x1, starting transfers between devices, exchange(): lax.ppermute(high, 'tile', RING_UP)  2.86 us
    ppermute x1, waiting for transfers between devices, exchange(): lax.ppermute(low, 'tile', RING_DOWN)  2.42 us
  transfers between devices with their start and end apart: 2, of which 2 were waited for; matrix products, arithmetic and copies ran while one was open for 0% of the time, Pallas kernels for 1%

profile of v9, /device:TPU:1, one launch (start us, length us, event | category | flops | bytes accessed | tf_op | source)
XLA Modules:
  0.0 85.2 jit_solution(16251454809924905147)
XLA Ops:
  0.0 2.0 %pack.1 = f32[1152,128]{1,0:T(8,128)S(1)} custom-call(f32[8]{0:T(128)} %table_hbm.1, f32[256,256]{1,0:T(8,128)} %bitcast.13, s32[128,256]{1,0:T(8,128)} %bitcast.14), custom_call_target="tpu_custom_call" | custom-call | flops 2000000 | bytes 1000000 | tf_op jit(solution)/shard_map/pack/pallas_call | solution.py:435
  2.0 47.8 %all_to_all.10 = f32[32,9,4,128]{3,2,1,0:T(4,128)S(1)} all-to-all(f32[32,9,4,128]{3,2,1,0:T(4,128)S(1)} %bitcast.10), channel_id=1, replica_groups=mesh['slab'=32,'tile'=8,'tilt'=2] {'slab'}, dimensions={0} | all-to-all | bytes 1179648 | tf_op jit(solution)/shard_map/all_to_all | solution.py:472
  49.9 1.6 %first.1 = (f32[1280,128]{1,0:T(8,128)S(1)}, f32[1280,128]{1,0:T(8,128)S(1)}, f32[512,128]{1,0:T(8,128)S(1)}, f32[512,128]{1,0:T(8,128)S(1)}, f32[512,128]{1,0:T...) custom-call(f32[1152,128]{1,0:T(8,128)S(1)} %bitcast.7), custom_call_target="tpu_custom_call" | custom-call | flops 2000000 | bytes 1000000 | tf_op jit(solution)/shard_map/first/pallas_call | solution.py:435
  51.5 2.9 %collective-permute-start = (f32[224,128]{1,0:T(8,128)S(1)}, f32[224,128]{1,0:T(8,128)S(1)}, u32[]{:S(2)}, u32[]{:S(2)}) collective-permute-start(f32[224,128]{1,0:T(8,128)S(1)} %get-tuple-element.21), channel_id=1, source_target_pairs={{0,2},{2,4},{4,6},{6,8},{8,10},{10,12},{12,14},{14,0},{1,3},{3,5},... | collective-permute-start | bytes 344072 | tf_op jit(solution)/shard_map/ppermute | solution.py:456
  54.4 0.0 collective-permute-start.1
  54.4 0.6 own.1
  55.0 1.2 %collective-permute-done.low = f32[224,128]{1,0:T(8,128)S(1)} collective-permute-done((f32[224,128]{1,0:T(8,128)S(1)}, f32[224,128]{1,0:T(8,128)S(1)}, u32[]{:S(2)}, u32[]{:S(2)}) %collective-permute-start) | collective-permute-done | bytes 114720 | tf_op jit(solution)/shard_map/ppermute | solution.py:456
  56.2 2.4 %collective-permute-done.1.high = f32[224,128]{1,0:T(8,128)S(1)} collective-permute-done((f32[224,128]{1,0:T(8,128)S(1)}, f32[224,128]{1,0:T(8,128)S(1)}, u32[]{:S(2)}, u32[]{:S(2)}) %collective-permute-start.1) | collective-permute-done | bytes 114720 | tf_op jit(solution)/shard_map/ppermute | solution.py:456
  58.6 1.7 %last.1 = f32[512,128]{1,0:T(8,128)S(1)} custom-call(f32[1152,128]{1,0:T(8,128)S(1)} %bitcast.9, f32[1280,128]{1,0:T(8,128)S(1)} %get-tuple-element.14.factors, f32[1280,128]{1,0:T(8,128)S(1)} %get-tuple-element.15.over_factors, f32[512,128]{1,0:T(8,128)S(1)} %get-tuple-element.16.main_in, f32[512,128]{1,0:T(8,128)S(1)} %get-tuple-element.19.main_part, ...), custom_call_target="tpu_custom_call" | custom-call | flops 2000000 | bytes 1000000 | tf_op jit(solution)/shard_map/last/pallas_call | solution.py:435
  60.3 23.9 %all_to_all.11 = f32[32,16,128]{2,1,0:T(8,128)S(1)} all-to-all(f32[32,16,128]{2,1,0:T(8,128)S(1)} %bitcast.11), channel_id=1, replica_groups=mesh['slab'=32,'tile'=8,'tilt'=2] {'slab'}, dimensions={0} | all-to-all | bytes 524288 | tf_op jit(solution)/shard_map/all_to_all | solution.py:483
  84.2 0.9 %unpack.1 = f32[256,256]{1,0:T(8,128)} custom-call(f32[512,128]{1,0:T(8,128)S(1)} %bitcast.12), custom_call_target="tpu_custom_call" | custom-call | flops 2000000 | bytes 1000000 | tf_op jit(solution)/shard_map/unpack/pallas_call | solution.py:435
Async XLA Ops:
  51.5 4.7 %collective-permute-start = (f32[224,128]{1,0:T(8,128)S(1)}, f32[224,128]{1,0:T(8,128)S(1)}, u32[]{:S(2)}, u32[]{:S(2)}) collective-permute-start(f32[224,128]{1,0:T(8,128)S(1)} %get-tuple-element.21), channel_id=1, source_target_pairs={{0,2},{2,4},{4,6},{6,8},{8,10},{10,12},{12,14},{14,0},{1,3},{3,5},... | collective-permute-start | bytes 344072 | tf_op jit(solution)/shard_map/ppermute | solution.py:456
  54.4 4.2 %collective-permute-start.1 = (f32[224,128]{1,0:T(8,128)S(1)}, f32[224,128]{1,0:T(8,128)S(1)}, u32[]{:S(2)}, u32[]{:S(2)}) collective-permute-start(f32[224,128]{1,0:T(8,128)S(1)} %get-tuple-element.22), channel_id=1, source_target_pairs={{2,0},{4,2},{6,4},{8,6},{10,8},{12,10},{14,12},{0,14},{3,1},{5,3},... | collective-permute-start | bytes 344072 | tf_op jit(solution)/shard_map/ppermute | solution.py:456

commit v10 on v9

--- a/solution.py
+++ b/solution.py
@@ -42,7 +42,9 @@
 
 
 def crecip(a):
-    scale = 1.0 / (a[0] * a[0] + a[1] * a[1])
+    square = a[0] * a[0] + a[1] * a[1]
+    scale = pl.reciprocal(square, approx=True)
+    scale = scale * (2.0 - square * scale)
     return a[0] * scale, -a[1] * scale
 
 
@@ -299,7 +301,9 @@
             high = jnp.where(cell_lanes(r, False), moved, high)
         return low, high
 
-    packed = [None] * 7
+    _, _, y = lane_ids()
+    beside_lines = (y == 0) | (y == 7)
+    packed = [None] * 6
     for c in range(2):
         near = pack([f[c] for f in main], 0, 7)
         far = pack([f[c] for f in main], 1, 6)
@@ -308,7 +312,10 @@
         cells = pack_cells([f[c] for f in over])
         packed[c] = near
         packed[2 + c] = [own[i] + COUPLE * (far[i] + sum_y(near[i], cells[i])) for i in range(2)]
-        packed[5 + c] = cells
+        if c == 0:
+            packed[5] = cells
+        else:
+            packed[5] = [jnp.where(beside_lines, re, roll(im, 2, 1)) for re, im in zip(packed[5], cells)]
     packed[4] = pack(relatives, 0, 7)
     for place, pair in enumerate(packed):
         for edge, array, turned in zip(edges, pair, (56, -56)):
@@ -329,8 +336,13 @@
     return roll(jnp.where(x == r, low, high), -8 * r, 1)
 
 
-def over_beside(low, high, r):
-    return roll(jnp.where(cell_lanes(r, True), low, high), -8 * r, 1)
+def over_beside(low, high, c, r):
+    _, x, y = lane_ids()
+    if c == 0:
+        from_low = cell_lanes(r, True)
+    else:
+        from_low = ((x == r) & (y == 1)) | ((x == (r + 1) % 8) & (y == 2))
+    return roll(jnp.where(from_low, low, high), -8 * r - 2 * c, 1)
 
 
 def sum_y(field, over):
@@ -406,7 +418,7 @@
     over_outermost = at_low | at_high
     tile = lax.axis_index("tile")
     exists = [jnp.broadcast_to(k, x.shape) for k in (tile > 0, tile < TILES - 1)]
-    cells = [[jnp.where(k, h[pl.ds((5 + c) * SLABS, SLABS), :], 0.0) for h, k in zip(halos, exists)] for c in range(2)]
+    cells = [jnp.where(k, h[pl.ds(5 * SLABS, SLABS), :], 0.0) for h, k in zip(halos, exists)]
     factorize([beside(halos, 4, r) for r in range(DEPTH)], near_factors)
     main_rhs, over_rhs, near_rhs = [], [], []
     for r in range(DEPTH):
@@ -414,7 +426,7 @@
         for c in range(2):
             near = jnp.where(keep, beside(halos, c, r), 0.0)
             main_adds.append(jnp.where(outermost, near, 0.0))
-            over_adds.append(jnp.where(over_outermost, over_beside(*cells[c], r), 0.0))
+            over_adds.append(jnp.where(over_outermost, over_beside(*cells, c, r), 0.0))
         main_rhs.append(relax(get(main_part, r), main_adds))
         over_rhs.append(relax(get(over_part, r), over_adds))
         near_rhs.append(relax((beside(halos, 2, r), beside(halos, 3, r)), get(main_in, r)))
@@ -446,7 +458,7 @@
 
 FIELD = (DEPTH * 2 * SLABS, LANES)
 FACTORS = (N_FACTORS * 2 * SLABS, LANES)
-EDGE = (7 * SLABS, LANES)
+EDGE = (6 * SLABS, LANES)
 
 RING_UP = [(i, (i + 1) % TILES) for i in range(TILES)]
 RING_DOWN = [(b, a) for a, b in RING_UP]

time: 85.4 us -> 85.2 us (level)
  no operation moved by 1% of the time
where the time goes in v10:
time: 85.2 us; the launch traced here: 85 us
  blocking collectives  71.7 us (84%)
  Pallas kernels  6.92 us (8%)
  waiting for transfers between devices  3.43 us (4%)
  starting transfers between devices  2.86 us (3%)
    all_to_all x1, blocking collectives, local(): lax.all_to_all(packed.reshape(SLABS, ROWS // 4, 4, LANES), 'slab', 0, 0)  47.8 us
    all_to_all x1, blocking collectives, local(): lax.all_to_all(packed.reshape(SLABS, 16, LANES), 'slab', 0, 0)  23.9 us
    pallas_call x5, Pallas kernels, call(): pl.pallas_call(kernel, out_shape=[jax.ShapeDtypeStruct(s, F32) for s in o...  6.92 us
    ppermute x1, starting transfers between devices, exchange(): lax.ppermute(high, 'tile', RING_UP)  2.86 us
    ppermute x1, waiting for transfers between devices, exchange(): lax.ppermute(low, 'tile', RING_DOWN)  2.4 us
  transfers between devices with their start and end apart: 2, of which 2 were waited for; matrix products, arithmetic and copies ran while one was open for 0% of the time, Pallas kernels for 1%

profile of v10, /device:TPU:1, one launch (start us, length us, event | category | flops | bytes accessed | tf_op | source)
XLA Modules:
  0.0 85.0 jit_solution(17042641312562295421)
XLA Ops:
  0.0 2.0 %pack.1 = f32[1152,128]{1,0:T(8,128)S(1)} custom-call(f32[8]{0:T(128)} %table_hbm.1, f32[256,256]{1,0:T(8,128)} %bitcast.13, s32[128,256]{1,0:T(8,128)} %bitcast.14), custom_call_target="tpu_custom_call" | custom-call | flops 2000000 | bytes 1000000 | tf_op jit(solution)/shard_map/pack/pallas_call | solution.py:447
  2.0 47.8 %all_to_all.10 = f32[32,9,4,128]{3,2,1,0:T(4,128)S(1)} all-to-all(f32[32,9,4,128]{3,2,1,0:T(4,128)S(1)} %bitcast.10), channel_id=1, replica_groups=mesh['slab'=32,'tile'=8,'tilt'=2] {'slab'}, dimensions={0} | all-to-all | bytes 1179648 | tf_op jit(solution)/shard_map/all_to_all | solution.py:484
  49.9 1.6 %first.1 = (f32[1280,128]{1,0:T(8,128)S(1)}, f32[1280,128]{1,0:T(8,128)S(1)}, f32[512,128]{1,0:T(8,128)S(1)}, f32[512,128]{1,0:T(8,128)S(1)}, f32[512,128]{1,0:T...) custom-call(f32[1152,128]{1,0:T(8,128)S(1)} %bitcast.7), custom_call_target="tpu_custom_call" | custom-call | flops 2000000 | bytes 1000000 | tf_op jit(solution)/shard_map/first/pallas_call | solution.py:447
  51.5 2.9 %collective-permute-start = (f32[192,128]{1,0:T(8,128)S(1)}, f32[192,128]{1,0:T(8,128)S(1)}, u32[]{:S(2)}, u32[]{:S(2)}) collective-permute-start(f32[192,128]{1,0:T(8,128)S(1)} %get-tuple-element.21), channel_id=1, source_target_pairs={{0,2},{2,4},{4,6},{6,8},{8,10},{10,12},{12,14},{14,0},{1,3},{3,5},... | collective-permute-start | bytes 294920 | tf_op jit(solution)/shard_map/ppermute | solution.py:468
  54.3 0.0 collective-permute-start.1
  54.3 0.6 own.1
  54.9 1.0 %collective-permute-done.low = f32[192,128]{1,0:T(8,128)S(1)} collective-permute-done((f32[192,128]{1,0:T(8,128)S(1)}, f32[192,128]{1,0:T(8,128)S(1)}, u32[]{:S(2)}, u32[]{:S(2)}) %collective-permute-start) | collective-permute-done | bytes 98336 | tf_op jit(solution)/shard_map/ppermute | solution.py:468
  56.0 2.4 %collective-permute-done.1.high = f32[192,128]{1,0:T(8,128)S(1)} collective-permute-done((f32[192,128]{1,0:T(8,128)S(1)}, f32[192,128]{1,0:T(8,128)S(1)}, u32[]{:S(2)}, u32[]{:S(2)}) %collective-permute-start.1) | collective-permute-done | bytes 98336 | tf_op jit(solution)/shard_map/ppermute | solution.py:468
  58.4 1.8 %last.1 = f32[512,128]{1,0:T(8,128)S(1)} custom-call(f32[1152,128]{1,0:T(8,128)S(1)} %bitcast.9, f32[1280,128]{1,0:T(8,128)S(1)} %get-tuple-element.14.factors, f32[1280,128]{1,0:T(8,128)S(1)} %get-tuple-element.15.over_factors, f32[512,128]{1,0:T(8,128)S(1)} %get-tuple-element.16.main_in, f32[512,128]{1,0:T(8,128)S(1)} %get-tuple-element.19.main_part, ...), custom_call_target="tpu_custom_call" | custom-call | flops 2000000 | bytes 1000000 | tf_op jit(solution)/shard_map/last/pallas_call | solution.py:447
  60.1 23.9 %all_to_all.11 = f32[32,16,128]{2,1,0:T(8,128)S(1)} all-to-all(f32[32,16,128]{2,1,0:T(8,128)S(1)} %bitcast.11), channel_id=1, replica_groups=mesh['slab'=32,'tile'=8,'tilt'=2] {'slab'}, dimensions={0} | all-to-all | bytes 524288 | tf_op jit(solution)/shard_map/all_to_all | solution.py:495
  84.0 0.9 %unpack.1 = f32[256,256]{1,0:T(8,128)} custom-call(f32[512,128]{1,0:T(8,128)S(1)} %bitcast.12), custom_call_target="tpu_custom_call" | custom-call | flops 2000000 | bytes 1000000 | tf_op jit(solution)/shard_map/unpack/pallas_call | solution.py:447
Async XLA Ops:
  51.5 4.5 %collective-permute-start = (f32[192,128]{1,0:T(8,128)S(1)}, f32[192,128]{1,0:T(8,128)S(1)}, u32[]{:S(2)}, u32[]{:S(2)}) collective-permute-start(f32[192,128]{1,0:T(8,128)S(1)} %get-tuple-element.21), channel_id=1, source_target_pairs={{0,2},{2,4},{4,6},{6,8},{8,10},{10,12},{12,14},{14,0},{1,3},{3,5},... | collective-permute-start | bytes 294920 | tf_op jit(solution)/shard_map/ppermute | solution.py:468
  54.3 4.0 %collective-permute-start.1 = (f32[192,128]{1,0:T(8,128)S(1)}, f32[192,128]{1,0:T(8,128)S(1)}, u32[]{:S(2)}, u32[]{:S(2)}) collective-permute-start(f32[192,128]{1,0:T(8,128)S(1)} %get-tuple-element.22), channel_id=1, source_target_pairs={{2,0},{4,2},{6,4},{8,6},{10,8},{12,10},{14,12},{0,14},{3,1},{5,3},... | collective-permute-start | bytes 294920 | tf_op jit(solution)/shard_map/ppermute | solution.py:468

commit v11 on v10

--- a/solution.py
+++ b/solution.py
@@ -96,22 +96,18 @@
 
     slot = lanes8() % 8
     first = slot < 4
-    pairs, singles = [], []
-    for side in range(2):
-        arrays = [load(side, quantity) for quantity in range(3)]
-        for quantity in range(3):
-            for block, part in enumerate(block_transpose(turn(arrays[quantity]))):
-                out[pl.ds((16 * side + block) * ROWS + quantity * 8, 8), :] = part
-        pair = [jnp.where(first, v, w) for v, w in zip(turn(arrays[0], 2), turn(arrays[1], 6))]
-        pairs += block_transpose(pair)
-        late = [roll(v, 4, 0) for v in turn(arrays[2], 6)]
-        singles += block_transpose([jnp.where(first, v, w) for v, w in zip(turn(arrays[2], 2), late)])
-    from_above = (slot & 2) != 0
+    chunks = []
+    for quantity in range(3):
+        blocks = block_transpose(turn(load(0, quantity))) + block_transpose(turn(load(1, quantity)))
+        chunks.append(blocks)
+        for chunk, block in enumerate(blocks):
+            out[pl.ds(chunk * ROWS + quantity * 8, 8), :] = block
     for chunk in range(SLABS):
-        lower = (chunk + 16) % SLABS if chunk % 16 == 0 else chunk
-        upper = (chunk + 1) % SLABS
-        out[pl.ds(chunk * ROWS + 24, 8), :] = jnp.where(from_above, pairs[upper], pairs[lower])
-        out[pl.ds(chunk * ROWS + 32, 4), :] = jnp.where(from_above, singles[upper], singles[lower])[:4]
+        picked = [jnp.where(first, blocks[(chunk + 1) % SLABS], blocks[chunk - 1]) for blocks in chunks]
+        pair = jnp.where(first, roll(picked[0], 2, 1), roll(picked[1], 6, 1))
+        single = jnp.where(first, roll(picked[2], 2, 1), roll(roll(picked[2], 6, 1), 4, 0))
+        out[pl.ds(chunk * ROWS + 24, 8), :] = pair
+        out[pl.ds(chunk * ROWS + 32, 4), :] = single[:4]
 
 
 def unpack_kernel(arrived, out, sides, sems):
@@ -173,7 +169,7 @@
     single = ref[pl.ds(32 + r % 4, SLABS, stride=ROWS), :]
     quantities = []
     for packed, base in ((pair, 0), (pair, 4), (single, 4 * (r // 4))):
-        quantities.append(jnp.where(y >= 4, roll(packed, -2 - base, 1), roll(packed, 6 - base, 1)))
+        quantities.append(jnp.where(y >= 4, roll(packed, -10 - base, 1), roll(packed, 6 - base, 1)))
     used = (y <= 1) | (y >= 6)
     return quantities[0], quantities[1], jnp.where(used, quantities[2], 1.0)
 

time: 85.2 us -> 85 us (level)
  no operation moved by 1% of the time
where the time goes in v11:
time: 85 us; the launch traced here: 84.8 us
  blocking collectives  71.7 us (84%)
  Pallas kernels  6.73 us (8%)
  waiting for transfers between devices  3.43 us (4%)
  starting transfers between devices  2.86 us (3%)
    all_to_all x1, blocking collectives, local(): lax.all_to_all(packed.reshape(SLABS, ROWS // 4, 4, LANES), 'slab', 0, 0)  47.8 us
    all_to_all x1, blocking collectives, local(): lax.all_to_all(packed.reshape(SLABS, 16, LANES), 'slab', 0, 0)  23.9 us
    pallas_call x5, Pallas kernels, call(): pl.pallas_call(kernel, out_shape=[jax.ShapeDtypeStruct(s, F32) for s in o...  6.73 us
    ppermute x1, starting transfers between devices, exchange(): lax.ppermute(high, 'tile', RING_UP)  2.86 us
    ppermute x1, waiting for transfers between devices, exchange(): lax.ppermute(low, 'tile', RING_DOWN)  2.4 us
  transfers between devices with their start and end apart: 2, of which 2 were waited for; matrix products, arithmetic and copies ran while one was open for 0% of the time, Pallas kernels for 1%

profile of v11, /device:TPU:1, one launch (start us, length us, event | category | flops | bytes accessed | tf_op | source)
XLA Modules:
  0.0 84.8 jit_solution(5172037026436756515)
XLA Ops:
  0.0 1.9 %pack.1 = f32[1152,128]{1,0:T(8,128)S(1)} custom-call(f32[8]{0:T(128)} %table_hbm.1, f32[256,256]{1,0:T(8,128)} %bitcast.13, s32[128,256]{1,0:T(8,128)} %bitcast.14), custom_call_target="tpu_custom_call" | custom-call | flops 2000000 | bytes 1000000 | tf_op jit(solution)/shard_map/pack/pallas_call | solution.py:443
  1.9 47.8 %all_to_all.10 = f32[32,9,4,128]{3,2,1,0:T(4,128)S(1)} all-to-all(f32[32,9,4,128]{3,2,1,0:T(4,128)S(1)} %bitcast.10), channel_id=1, replica_groups=mesh['slab'=32,'tile'=8,'tilt'=2] {'slab'}, dimensions={0} | all-to-all | bytes 1179648 | tf_op jit(solution)/shard_map/all_to_all | solution.py:480
  49.7 1.6 %first.1 = (f32[1280,128]{1,0:T(8,128)S(1)}, f32[1280,128]{1,0:T(8,128)S(1)}, f32[512,128]{1,0:T(8,128)S(1)}, f32[512,128]{1,0:T(8,128)S(1)}, f32[512,128]{1,0:T...) custom-call(f32[1152,128]{1,0:T(8,128)S(1)} %bitcast.7), custom_call_target="tpu_custom_call" | custom-call | flops 2000000 | bytes 1000000 | tf_op jit(solution)/shard_map/first/pallas_call | solution.py:443
  51.3 2.9 %collective-permute-start = (f32[192,128]{1,0:T(8,128)S(1)}, f32[192,128]{1,0:T(8,128)S(1)}, u32[]{:S(2)}, u32[]{:S(2)}) collective-permute-start(f32[192,128]{1,0:T(8,128)S(1)} %get-tuple-element.21), channel_id=1, source_target_pairs={{0,2},{2,4},{4,6},{6,8},{8,10},{10,12},{12,14},{14,0},{1,3},{3,5},... | collective-permute-start | bytes 294920 | tf_op jit(solution)/shard_map/ppermute | solution.py:464
  54.1 0.0 collective-permute-start.1
  54.1 0.6 own.1
  54.7 1.0 %collective-permute-done.low = f32[192,128]{1,0:T(8,128)S(1)} collective-permute-done((f32[192,128]{1,0:T(8,128)S(1)}, f32[192,128]{1,0:T(8,128)S(1)}, u32[]{:S(2)}, u32[]{:S(2)}) %collective-permute-start) | collective-permute-done | bytes 98336 | tf_op jit(solution)/shard_map/ppermute | solution.py:464
  55.8 2.4 %collective-permute-done.1.high = f32[192,128]{1,0:T(8,128)S(1)} collective-permute-done((f32[192,128]{1,0:T(8,128)S(1)}, f32[192,128]{1,0:T(8,128)S(1)}, u32[]{:S(2)}, u32[]{:S(2)}) %collective-permute-start.1) | collective-permute-done | bytes 98336 | tf_op jit(solution)/shard_map/ppermute | solution.py:464
  58.2 1.8 %last.1 = f32[512,128]{1,0:T(8,128)S(1)} custom-call(f32[1152,128]{1,0:T(8,128)S(1)} %bitcast.9, f32[1280,128]{1,0:T(8,128)S(1)} %get-tuple-element.14.factors, f32[1280,128]{1,0:T(8,128)S(1)} %get-tuple-element.15.over_factors, f32[512,128]{1,0:T(8,128)S(1)} %get-tuple-element.16.main_in, f32[512,128]{1,0:T(8,128)S(1)} %get-tuple-element.19.main_part, ...), custom_call_target="tpu_custom_call" | custom-call | flops 2000000 | bytes 1000000 | tf_op jit(solution)/shard_map/last/pallas_call | solution.py:443
  59.9 23.9 %all_to_all.11 = f32[32,16,128]{2,1,0:T(8,128)S(1)} all-to-all(f32[32,16,128]{2,1,0:T(8,128)S(1)} %bitcast.11), channel_id=1, replica_groups=mesh['slab'=32,'tile'=8,'tilt'=2] {'slab'}, dimensions={0} | all-to-all | bytes 524288 | tf_op jit(solution)/shard_map/all_to_all | solution.py:491
  83.8 0.9 %unpack.1 = f32[256,256]{1,0:T(8,128)} custom-call(f32[512,128]{1,0:T(8,128)S(1)} %bitcast.12), custom_call_target="tpu_custom_call" | custom-call | flops 2000000 | bytes 1000000 | tf_op jit(solution)/shard_map/unpack/pallas_call | solution.py:443
Async XLA Ops:
  51.3 4.5 %collective-permute-start = (f32[192,128]{1,0:T(8,128)S(1)}, f32[192,128]{1,0:T(8,128)S(1)}, u32[]{:S(2)}, u32[]{:S(2)}) collective-permute-start(f32[192,128]{1,0:T(8,128)S(1)} %get-tuple-element.21), channel_id=1, source_target_pairs={{0,2},{2,4},{4,6},{6,8},{8,10},{10,12},{12,14},{14,0},{1,3},{3,5},... | collective-permute-start | bytes 294920 | tf_op jit(solution)/shard_map/ppermute | solution.py:464
  54.1 4.0 %collective-permute-start.1 = (f32[192,128]{1,0:T(8,128)S(1)}, f32[192,128]{1,0:T(8,128)S(1)}, u32[]{:S(2)}, u32[]{:S(2)}) collective-permute-start(f32[192,128]{1,0:T(8,128)S(1)} %get-tuple-element.22), channel_id=1, source_target_pairs={{2,0},{4,2},{6,4},{8,6},{10,8},{12,10},{14,12},{0,14},{3,1},{5,3},... | collective-permute-start | bytes 294920 | tf_op jit(solution)/shard_map/ppermute | solution.py:464

commit v12 on v11

--- a/solution.py
+++ b/solution.py
@@ -381,9 +381,8 @@
     return [get(ref, r) for r in range(DEPTH)]
 
 
-def first_kernel(arrived, factors, over_factors, over_source, main_out, over_out, *edges):
+def first_kernel(arrived, factors, over_factors, main_out, over_out, *edges):
     overlap = [overlap_layer(arrived, r) for r in range(DEPTH)]
-    put_all(over_source, [o[:2] for o in overlap])
     factorize([o[2] for o in overlap], over_factors, True)
     over = masked(line_solve([o[:2] for o in overlap], over_factors, True), inside())
     put_all(over_out, over)
@@ -395,11 +394,11 @@
     put_edges(main, over, source, relatives, edges)
 
 
-def own_kernel(arrived, over_source, main_in, over_in, main_part, over_part):
+def own_kernel(arrived, main_in, over_in, main_part, over_part):
     for r in range(DEPTH):
         main, over = get(main_in, r), get(over_in, r)
         put(main_part, r, relax(source_layer(arrived, r), [sum_main(m, e, 0.0) for m, e in zip(main, over)]))
-        put(over_part, r, relax(get(over_source, r), [sum_over(m, e) for m, e in zip(main, over)]))
+        put(over_part, r, relax(overlap_layer(arrived, r)[:2], [sum_over(m, e) for m, e in zip(main, over)]))
 
 
 def last_kernel(
@@ -478,11 +477,11 @@
         ],
     )
     arrived = lax.all_to_all(packed.reshape(SLABS, ROWS // 4, 4, LANES), "slab", 0, 0).reshape(SLABS * ROWS, LANES)
-    factors, over_factors, over_source, main, over, *edges = call(
-        first_kernel, "first", [FACTORS, FACTORS, FIELD, FIELD, FIELD, EDGE, EDGE], arrived
+    factors, over_factors, main, over, *edges = call(
+        first_kernel, "first", [FACTORS, FACTORS, FIELD, FIELD, EDGE, EDGE], arrived
     )
     halos = exchange(*edges)
-    main_part, over_part = call(own_kernel, "own", [FIELD, FIELD], arrived, over_source, main, over)
+    main_part, over_part = call(own_kernel, "own", [FIELD, FIELD], arrived, main, over)
     (packed,) = call(
         last_kernel, "last", [(SLABS * 16, LANES)],
         arrived, factors, over_factors, main, main_part, over_part, *halos,

time: 85 us -> 85 us (level)
  no operation moved by 1% of the time
where the time goes in v12:
time: 85 us; the launch traced here: 84.8 us
  blocking collectives  71.7 us (84%)
  Pallas kernels  6.85 us (8%)
  waiting for transfers between devices  3.3 us (4%)
  starting transfers between devices  2.86 us (3%)
    all_to_all x1, blocking collectives, local(): lax.all_to_all(packed.reshape(SLABS, ROWS // 4, 4, LANES), 'slab', 0, 0)  47.8 us
    all_to_all x1, blocking collectives, local(): lax.all_to_all(packed.reshape(SLABS, 16, LANES), 'slab', 0, 0)  23.9 us
    pallas_call x5, Pallas kernels, call(): pl.pallas_call(kernel, out_shape=[jax.ShapeDtypeStruct(s, F32) for s in o...  6.85 us
    ppermute x1, starting transfers between devices, exchange(): lax.ppermute(high, 'tile', RING_UP)  2.86 us
    ppermute x1, waiting for transfers between devices, exchange(): lax.ppermute(low, 'tile', RING_DOWN)  2.4 us
  transfers between devices with their start and end apart: 2, of which 2 were waited for; matrix products, arithmetic and copies ran while one was open for 0% of the time, Pallas kernels for 1%

profile of v12, /device:TPU:1, one launch (start us, length us, event | category | flops | bytes accessed | tf_op | source)
XLA Modules:
  0.0 84.8 jit_solution(3785324349140598634)
XLA Ops:
  0.0 1.9 %pack.1 = f32[1152,128]{1,0:T(8,128)S(1)} custom-call(f32[8]{0:T(128)} %table_hbm.1, f32[256,256]{1,0:T(8,128)} %bitcast.13, s32[128,256]{1,0:T(8,128)} %bitcast.14), custom_call_target="tpu_custom_call" | custom-call | flops 2000000 | bytes 1000000 | tf_op jit(solution)/shard_map/pack/pallas_call | solution.py:442
  1.9 47.8 %all_to_all.10 = f32[32,9,4,128]{3,2,1,0:T(4,128)S(1)} all-to-all(f32[32,9,4,128]{3,2,1,0:T(4,128)S(1)} %bitcast.10), channel_id=1, replica_groups=mesh['slab'=32,'tile'=8,'tilt'=2] {'slab'}, dimensions={0} | all-to-all | bytes 1179648 | tf_op jit(solution)/shard_map/all_to_all | solution.py:479
  49.7 1.6 %first.1 = (f32[1280,128]{1,0:T(8,128)S(1)}, f32[1280,128]{1,0:T(8,128)S(1)}, f32[512,128]{1,0:T(8,128)S(1)}, f32[512,128]{1,0:T(8,128)S(1)}, f32[192,128]{1,0:T(8,128)S(1)}, /*index=5*/f32[192,128]{1,0:T(8,128)S(1)}) custom-call(f32[1152,128]{1,0:T(8,128)S(1)} %bitcast.7), custom_call_target="tpu_custom_call" | custom-call | flops 2000000 | bytes 1000000 | tf_op jit(solution)/shard_map/first/pallas_call | solution.py:442
  51.3 2.9 %collective-permute-start = (f32[192,128]{1,0:T(8,128)S(1)}, f32[192,128]{1,0:T(8,128)S(1)}, u32[]{:S(2)}, u32[]{:S(2)}) collective-permute-start(f32[192,128]{1,0:T(8,128)S(1)} %get-tuple-element.19), channel_id=1, source_target_pairs={{0,2},{2,4},{4,6},{6,8},{8,10},{10,12},{12,14},{14,0},{1,3},{3,5},... | collective-permute-start | bytes 294920 | tf_op jit(solution)/shard_map/ppermute | solution.py:463
  54.1 0.0 collective-permute-start.1
  54.1 0.7 own.1
  54.9 0.9 %collective-permute-done.low = f32[192,128]{1,0:T(8,128)S(1)} collective-permute-done((f32[192,128]{1,0:T(8,128)S(1)}, f32[192,128]{1,0:T(8,128)S(1)}, u32[]{:S(2)}, u32[]{:S(2)}) %collective-permute-start) | collective-permute-done | bytes 98336 | tf_op jit(solution)/shard_map/ppermute | solution.py:463
  55.8 2.4 %collective-permute-done.1.high = f32[192,128]{1,0:T(8,128)S(1)} collective-permute-done((f32[192,128]{1,0:T(8,128)S(1)}, f32[192,128]{1,0:T(8,128)S(1)}, u32[]{:S(2)}, u32[]{:S(2)}) %collective-permute-start.1) | collective-permute-done | bytes 98336 | tf_op jit(solution)/shard_map/ppermute | solution.py:463
  58.2 1.8 %last.1 = f32[512,128]{1,0:T(8,128)S(1)} custom-call(f32[1152,128]{1,0:T(8,128)S(1)} %bitcast.9, f32[1280,128]{1,0:T(8,128)S(1)} %get-tuple-element.13.factors, f32[1280,128]{1,0:T(8,128)S(1)} %get-tuple-element.14.over_factors, f32[512,128]{1,0:T(8,128)S(1)} %get-tuple-element.15.main_in, f32[512,128]{1,0:T(8,128)S(1)} %get-tuple-element.17.main_part, ...), custom_call_target="tpu_custom_call" | custom-call | flops 2000000 | bytes 1000000 | tf_op jit(solution)/shard_map/last/pallas_call | solution.py:442
  59.9 23.9 %all_to_all.11 = f32[32,16,128]{2,1,0:T(8,128)S(1)} all-to-all(f32[32,16,128]{2,1,0:T(8,128)S(1)} %bitcast.11), channel_id=1, replica_groups=mesh['slab'=32,'tile'=8,'tilt'=2] {'slab'}, dimensions={0} | all-to-all | bytes 524288 | tf_op jit(solution)/shard_map/all_to_all | solution.py:490
  83.8 0.9 %unpack.1 = f32[256,256]{1,0:T(8,128)} custom-call(f32[512,128]{1,0:T(8,128)S(1)} %bitcast.12), custom_call_target="tpu_custom_call" | custom-call | flops 2000000 | bytes 1000000 | tf_op jit(solution)/shard_map/unpack/pallas_call | solution.py:442
Async XLA Ops:
  51.3 4.5 %collective-permute-start = (f32[192,128]{1,0:T(8,128)S(1)}, f32[192,128]{1,0:T(8,128)S(1)}, u32[]{:S(2)}, u32[]{:S(2)}) collective-permute-start(f32[192,128]{1,0:T(8,128)S(1)} %get-tuple-element.19), channel_id=1, source_target_pairs={{0,2},{2,4},{4,6},{6,8},{8,10},{10,12},{12,14},{14,0},{1,3},{3,5},... | collective-permute-start | bytes 294920 | tf_op jit(solution)/shard_map/ppermute | solution.py:463
  54.1 4.0 %collective-permute-start.1 = (f32[192,128]{1,0:T(8,128)S(1)}, f32[192,128]{1,0:T(8,128)S(1)}, u32[]{:S(2)}, u32[]{:S(2)}) collective-permute-start(f32[192,128]{1,0:T(8,128)S(1)} %get-tuple-element.20), channel_id=1, source_target_pairs={{2,0},{4,2},{6,4},{8,6},{10,8},{12,10},{14,12},{0,14},{3,1},{5,3},... | collective-permute-start | bytes 294920 | tf_op jit(solution)/shard_map/ppermute | solution.py:463

commit v13 on v12

--- a/solution.py
+++ b/solution.py
@@ -73,10 +73,12 @@
     for side in range(2):
         lanes = pl.ds(side * LANES, LANES)
         copies.append(pltpu.make_async_copy(labels.at[:, lanes], marks.at[side], sems.at[1 + side]))
-    for side in range(2):
-        lanes = pl.ds(side * LANES, LANES)
-        into = sides.at[side, pl.ds(0, 2 * LANES)]
-        copies.append(pltpu.make_async_copy(source.at[:, lanes], into, sems.at[3 + side]))
+    for quantity in range(2):
+        rows = pl.ds(quantity * LANES, LANES)
+        for side in range(2):
+            lanes = pl.ds(side * LANES, LANES)
+            sem = sems.at[3 + 2 * quantity + side]
+            copies.append(pltpu.make_async_copy(source.at[rows, lanes], sides.at[side, rows], sem))
     for copy in copies:
         copy.start()
     for copy in copies[:3]:
@@ -87,8 +89,6 @@
         for m in range(1, 8):
             rel = jnp.where(lab == m, table[m], rel)
         sides[side, pl.ds(2 * LANES, LANES), :] = rel
-    for copy in copies[3:]:
-        copy.wait()
 
     def load(side, quantity):
         places = [quantity * LANES + half * 64 + x for half in range(2) for x in range(8)]
@@ -96,10 +96,13 @@
 
     slot = lanes8() % 8
     first = slot < 4
-    chunks = []
-    for quantity in range(3):
+    chunks = [None] * 3
+    for quantity in (2, 0, 1):
+        if quantity < 2:
+            for copy in copies[3 + 2 * quantity : 5 + 2 * quantity]:
+                copy.wait()
         blocks = block_transpose(turn(load(0, quantity))) + block_transpose(turn(load(1, quantity)))
-        chunks.append(blocks)
+        chunks[quantity] = blocks
         for chunk, block in enumerate(blocks):
             out[pl.ds(chunk * ROWS + quantity * 8, 8), :] = block
     for chunk in range(SLABS):
@@ -473,7 +476,7 @@
             pltpu.VMEM((2, 3 * LANES, LANES), F32),
             pltpu.VMEM((2, LANES, LANES), jnp.int32),
             pltpu.SMEM((8,), F32),
-            pltpu.SemaphoreType.DMA((5,)),
+            pltpu.SemaphoreType.DMA((7,)),
         ],
     )
     arrived = lax.all_to_all(packed.reshape(SLABS, ROWS // 4, 4, LANES), "slab", 0, 0).reshape(SLABS * ROWS, LANES)

time: 85 us -> 84.9 us (level)
  no operation moved by 1% of the time
where the time goes in v13:
time: 84.9 us; the launch traced here: 84.6 us
  blocking collectives  71.7 us (84%)
  Pallas kernels  6.72 us (8%)
  waiting for transfers between devices  3.3 us (4%)
  starting transfers between devices  2.86 us (3%)
    all_to_all x1, blocking collectives, local(): lax.all_to_all(packed.reshape(SLABS, ROWS // 4, 4, LANES), 'slab', 0, 0)  47.8 us
    all_to_all x1, blocking collectives, local(): lax.all_to_all(packed.reshape(SLABS, 16, LANES), 'slab', 0, 0)  23.9 us
    pallas_call x5, Pallas kernels, call(): pl.pallas_call(kernel, out_shape=[jax.ShapeDtypeStruct(s, F32) for s in o...  6.72 us
    ppermute x1, starting transfers between devices, exchange(): lax.ppermute(high, 'tile', RING_UP)  2.86 us
    ppermute x1, waiting for transfers between devices, exchange(): lax.ppermute(low, 'tile', RING_DOWN)  2.4 us
  transfers between devices with their start and end apart: 2, of which 2 were waited for; matrix products, arithmetic and copies ran while one was open for 0% of the time, Pallas kernels for 1%

profile of v13, /device:TPU:1, one launch (start us, length us, event | category | flops | bytes accessed | tf_op | source)
XLA Modules:
  0.0 84.6 jit_solution(14843503741181668386)
XLA Ops:
  0.0 1.7 %pack.1 = f32[1152,128]{1,0:T(8,128)S(1)} custom-call(f32[8]{0:T(128)} %table_hbm.1, f32[256,256]{1,0:T(8,128)} %bitcast.13, s32[128,256]{1,0:T(8,128)} %bitcast.14), custom_call_target="tpu_custom_call" | custom-call | flops 2000000 | bytes 1000000 | tf_op jit(solution)/shard_map/pack/pallas_call | solution.py:445
  1.7 47.8 %all_to_all.10 = f32[32,9,4,128]{3,2,1,0:T(4,128)S(1)} all-to-all(f32[32,9,4,128]{3,2,1,0:T(4,128)S(1)} %bitcast.10), channel_id=1, replica_groups=mesh['slab'=32,'tile'=8,'tilt'=2] {'slab'}, dimensions={0} | all-to-all | bytes 1179648 | tf_op jit(solution)/shard_map/all_to_all | solution.py:482
  49.6 1.6 %first.1 = (f32[1280,128]{1,0:T(8,128)S(1)}, f32[1280,128]{1,0:T(8,128)S(1)}, f32[512,128]{1,0:T(8,128)S(1)}, f32[512,128]{1,0:T(8,128)S(1)}, f32[192,128]{1,0:T(8,128)S(1)}, /*index=5*/f32[192,128]{1,0:T(8,128)S(1)}) custom-call(f32[1152,128]{1,0:T(8,128)S(1)} %bitcast.7), custom_call_target="tpu_custom_call" | custom-call | flops 2000000 | bytes 1000000 | tf_op jit(solution)/shard_map/first/pallas_call | solution.py:445
  51.1 2.9 %collective-permute-start = (f32[192,128]{1,0:T(8,128)S(1)}, f32[192,128]{1,0:T(8,128)S(1)}, u32[]{:S(2)}, u32[]{:S(2)}) collective-permute-start(f32[192,128]{1,0:T(8,128)S(1)} %get-tuple-element.19), channel_id=1, source_target_pairs={{0,2},{2,4},{4,6},{6,8},{8,10},{10,12},{12,14},{14,0},{1,3},{3,5},... | collective-permute-start | bytes 294920 | tf_op jit(solution)/shard_map/ppermute | solution.py:466
  54.0 0.0 collective-permute-start.1
  54.0 0.7 own.1
  54.7 0.9 %collective-permute-done.low = f32[192,128]{1,0:T(8,128)S(1)} collective-permute-done((f32[192,128]{1,0:T(8,128)S(1)}, f32[192,128]{1,0:T(8,128)S(1)}, u32[]{:S(2)}, u32[]{:S(2)}) %collective-permute-start) | collective-permute-done | bytes 98336 | tf_op jit(solution)/shard_map/ppermute | solution.py:466
  55.6 2.4 %collective-permute-done.1.high = f32[192,128]{1,0:T(8,128)S(1)} collective-permute-done((f32[192,128]{1,0:T(8,128)S(1)}, f32[192,128]{1,0:T(8,128)S(1)}, u32[]{:S(2)}, u32[]{:S(2)}) %collective-permute-start.1) | collective-permute-done | bytes 98336 | tf_op jit(solution)/shard_map/ppermute | solution.py:466
  58.0 1.8 %last.1 = f32[512,128]{1,0:T(8,128)S(1)} custom-call(f32[1152,128]{1,0:T(8,128)S(1)} %bitcast.9, f32[1280,128]{1,0:T(8,128)S(1)} %get-tuple-element.13.factors, f32[1280,128]{1,0:T(8,128)S(1)} %get-tuple-element.14.over_factors, f32[512,128]{1,0:T(8,128)S(1)} %get-tuple-element.15.main_in, f32[512,128]{1,0:T(8,128)S(1)} %get-tuple-element.17.main_part, ...), custom_call_target="tpu_custom_call" | custom-call | flops 2000000 | bytes 1000000 | tf_op jit(solution)/shard_map/last/pallas_call | solution.py:445
  59.8 23.9 %all_to_all.11 = f32[32,16,128]{2,1,0:T(8,128)S(1)} all-to-all(f32[32,16,128]{2,1,0:T(8,128)S(1)} %bitcast.11), channel_id=1, replica_groups=mesh['slab'=32,'tile'=8,'tilt'=2] {'slab'}, dimensions={0} | all-to-all | bytes 524288 | tf_op jit(solution)/shard_map/all_to_all | solution.py:493
  83.7 0.9 %unpack.1 = f32[256,256]{1,0:T(8,128)} custom-call(f32[512,128]{1,0:T(8,128)S(1)} %bitcast.12), custom_call_target="tpu_custom_call" | custom-call | flops 2000000 | bytes 1000000 | tf_op jit(solution)/shard_map/unpack/pallas_call | solution.py:445
Async XLA Ops:
  51.1 4.5 %collective-permute-start = (f32[192,128]{1,0:T(8,128)S(1)}, f32[192,128]{1,0:T(8,128)S(1)}, u32[]{:S(2)}, u32[]{:S(2)}) collective-permute-start(f32[192,128]{1,0:T(8,128)S(1)} %get-tuple-element.19), channel_id=1, source_target_pairs={{0,2},{2,4},{4,6},{6,8},{8,10},{10,12},{12,14},{14,0},{1,3},{3,5},... | collective-permute-start | bytes 294920 | tf_op jit(solution)/shard_map/ppermute | solution.py:466
  54.0 4.0 %collective-permute-start.1 = (f32[192,128]{1,0:T(8,128)S(1)}, f32[192,128]{1,0:T(8,128)S(1)}, u32[]{:S(2)}, u32[]{:S(2)}) collective-permute-start(f32[192,128]{1,0:T(8,128)S(1)} %get-tuple-element.20), channel_id=1, source_target_pairs={{2,0},{4,2},{6,4},{8,6},{10,8},{12,10},{14,12},{0,14},{3,1},{5,3},... | collective-permute-start | bytes 294920 | tf_op jit(solution)/shard_map/ppermute | solution.py:466

commit v14 on v13

--- a/solution.py
+++ b/solution.py
@@ -121,9 +121,9 @@
             for i, part in enumerate(block_transpose(turn(parts))):
                 half, x = divmod(i, 8)
                 sides[side, pl.ds(c * LANES + half * 64 + x, 8, stride=8), :] = part
-        lanes = pl.ds(side * LANES, LANES)
-        copies.append(pltpu.make_async_copy(sides.at[side], out.at[:, lanes], sems.at[side]))
-        copies[-1].start()
+            rows, lanes = pl.ds(c * LANES, LANES), pl.ds(side * LANES, LANES)
+            copies.append(pltpu.make_async_copy(sides.at[side, rows], out.at[rows, lanes], sems.at[2 * side + c]))
+            copies[-1].start()
     for copy in copies:
         copy.wait()
 
@@ -493,7 +493,7 @@
     arrived = lax.all_to_all(packed.reshape(SLABS, 16, LANES), "slab", 0, 0).reshape(SLABS * 16, LANES)
     (out,) = call(
         unpack_kernel, "unpack", [(2 * 16 * 8, 256)], arrived, out_spec=HBM,
-        scratch=[pltpu.VMEM((2, 2 * LANES, LANES), F32), pltpu.SemaphoreType.DMA((2,))],
+        scratch=[pltpu.VMEM((2, 2 * LANES, LANES), F32), pltpu.SemaphoreType.DMA((4,))],
     )
     return out.reshape(2, 16, 8, 256)
 

time: 84.9 us -> 84.8 us (level)
  no operation moved by 1% of the time
where the time goes in v14:
time: 84.8 us; the launch traced here: 84.6 us
  blocking collectives  71.7 us (85%)
  Pallas kernels  6.71 us (8%)
  waiting for transfers between devices  3.3 us (4%)
  starting transfers between devices  2.86 us (3%)
    all_to_all x1, blocking collectives, local(): lax.all_to_all(packed.reshape(SLABS, ROWS // 4, 4, LANES), 'slab', 0, 0)  47.8 us
    all_to_all x1, blocking collectives, local(): lax.all_to_all(packed.reshape(SLABS, 16, LANES), 'slab', 0, 0)  23.9 us
    pallas_call x5, Pallas kernels, call(): pl.pallas_call(kernel, out_shape=[jax.ShapeDtypeStruct(s, F32) for s in o...  6.71 us
    ppermute x1, starting transfers between devices, exchange(): lax.ppermute(high, 'tile', RING_UP)  2.86 us
    ppermute x1, waiting for transfers between devices, exchange(): lax.ppermute(low, 'tile', RING_DOWN)  2.4 us
  transfers between devices with their start and end apart: 2, of which 2 were waited for; matrix products, arithmetic and copies ran while one was open for 0% of the time, Pallas kernels for 1%

profile of v14, /device:TPU:1, one launch (start us, length us, event | category | flops | bytes accessed | tf_op | source)
XLA Modules:
  0.0 84.6 jit_solution(12310824810544248343)
XLA Ops:
  0.0 1.7 %pack.1 = f32[1152,128]{1,0:T(8,128)S(1)} custom-call(f32[8]{0:T(128)} %table_hbm.1, f32[256,256]{1,0:T(8,128)} %bitcast.13, s32[128,256]{1,0:T(8,128)} %bitcast.14), custom_call_target="tpu_custom_call" | custom-call | flops 2000000 | bytes 1000000 | tf_op jit(solution)/shard_map/pack/pallas_call | solution.py:445
  1.7 47.8 %all_to_all.10 = f32[32,9,4,128]{3,2,1,0:T(4,128)S(1)} all-to-all(f32[32,9,4,128]{3,2,1,0:T(4,128)S(1)} %bitcast.10), channel_id=1, replica_groups=mesh['slab'=32,'tile'=8,'tilt'=2] {'slab'}, dimensions={0} | all-to-all | bytes 1179648 | tf_op jit(solution)/shard_map/all_to_all | solution.py:482
  49.6 1.6 %first.1 = (f32[1280,128]{1,0:T(8,128)S(1)}, f32[1280,128]{1,0:T(8,128)S(1)}, f32[512,128]{1,0:T(8,128)S(1)}, f32[512,128]{1,0:T(8,128)S(1)}, f32[192,128]{1,0:T(8,128)S(1)}, /*index=5*/f32[192,128]{1,0:T(8,128)S(1)}) custom-call(f32[1152,128]{1,0:T(8,128)S(1)} %bitcast.7), custom_call_target="tpu_custom_call" | custom-call | flops 2000000 | bytes 1000000 | tf_op jit(solution)/shard_map/first/pallas_call | solution.py:445
  51.1 2.9 %collective-permute-start = (f32[192,128]{1,0:T(8,128)S(1)}, f32[192,128]{1,0:T(8,128)S(1)}, u32[]{:S(2)}, u32[]{:S(2)}) collective-permute-start(f32[192,128]{1,0:T(8,128)S(1)} %get-tuple-element.19), channel_id=1, source_target_pairs={{0,2},{2,4},{4,6},{6,8},{8,10},{10,12},{12,14},{14,0},{1,3},{3,5},... | collective-permute-start | bytes 294920 | tf_op jit(solution)/shard_map/ppermute | solution.py:466
  54.0 0.0 collective-permute-start.1
  54.0 0.7 own.1
  54.7 0.9 %collective-permute-done.low = f32[192,128]{1,0:T(8,128)S(1)} collective-permute-done((f32[192,128]{1,0:T(8,128)S(1)}, f32[192,128]{1,0:T(8,128)S(1)}, u32[]{:S(2)}, u32[]{:S(2)}) %collective-permute-start) | collective-permute-done | bytes 98336 | tf_op jit(solution)/shard_map/ppermute | solution.py:466
  55.6 2.4 %collective-permute-done.1.high = f32[192,128]{1,0:T(8,128)S(1)} collective-permute-done((f32[192,128]{1,0:T(8,128)S(1)}, f32[192,128]{1,0:T(8,128)S(1)}, u32[]{:S(2)}, u32[]{:S(2)}) %collective-permute-start.1) | collective-permute-done | bytes 98336 | tf_op jit(solution)/shard_map/ppermute | solution.py:466
  58.0 1.8 %last.1 = f32[512,128]{1,0:T(8,128)S(1)} custom-call(f32[1152,128]{1,0:T(8,128)S(1)} %bitcast.9, f32[1280,128]{1,0:T(8,128)S(1)} %get-tuple-element.13.factors, f32[1280,128]{1,0:T(8,128)S(1)} %get-tuple-element.14.over_factors, f32[512,128]{1,0:T(8,128)S(1)} %get-tuple-element.15.main_in, f32[512,128]{1,0:T(8,128)S(1)} %get-tuple-element.17.main_part, ...), custom_call_target="tpu_custom_call" | custom-call | flops 2000000 | bytes 1000000 | tf_op jit(solution)/shard_map/last/pallas_call | solution.py:445
  59.8 23.9 %all_to_all.11 = f32[32,16,128]{2,1,0:T(8,128)S(1)} all-to-all(f32[32,16,128]{2,1,0:T(8,128)S(1)} %bitcast.11), channel_id=1, replica_groups=mesh['slab'=32,'tile'=8,'tilt'=2] {'slab'}, dimensions={0} | all-to-all | bytes 524288 | tf_op jit(solution)/shard_map/all_to_all | solution.py:493
  83.7 0.9 %unpack.1 = f32[256,256]{1,0:T(8,128)} custom-call(f32[512,128]{1,0:T(8,128)S(1)} %bitcast.12), custom_call_target="tpu_custom_call" | custom-call | flops 2000000 | bytes 1000000 | tf_op jit(solution)/shard_map/unpack/pallas_call | solution.py:445
Async XLA Ops:
  51.1 4.5 %collective-permute-start = (f32[192,128]{1,0:T(8,128)S(1)}, f32[192,128]{1,0:T(8,128)S(1)}, u32[]{:S(2)}, u32[]{:S(2)}) collective-permute-start(f32[192,128]{1,0:T(8,128)S(1)} %get-tuple-element.19), channel_id=1, source_target_pairs={{0,2},{2,4},{4,6},{6,8},{8,10},{10,12},{12,14},{14,0},{1,3},{3,5},... | collective-permute-start | bytes 294920 | tf_op jit(solution)/shard_map/ppermute | solution.py:466
  54.0 4.0 %collective-permute-start.1 = (f32[192,128]{1,0:T(8,128)S(1)}, f32[192,128]{1,0:T(8,128)S(1)}, u32[]{:S(2)}, u32[]{:S(2)}) collective-permute-start(f32[192,128]{1,0:T(8,128)S(1)} %get-tuple-element.20), channel_id=1, source_target_pairs={{2,0},{4,2},{6,4},{8,6},{10,8},{12,10},{14,12},{0,14},{3,1},{5,3},... | collective-permute-start | bytes 294920 | tf_op jit(solution)/shard_map/ppermute | solution.py:466
